TPU v7x, 128 devices: a whole 4x4x4 slice. The times are simulated.
128 devices in a mesh: pop: 4 (over z), row: 4 (over x_hi, core), col: 8 (over x_lo, y).
Axes of the slice: x: 4 (x_hi: 2, x_lo: 2; x = x_hi * 2 + x_lo), y: 4, z: 4, core: 2. Of those that a mesh axis runs over, the one named last changes fastest.
Arguments:
- obs_ids: int32 [512, 16], P('pop'), may hold values from 0 to 155
- member_ids: int32 [512], P('pop'), may hold values from 0 to 511, each once
- fitness: float32 [512], replicated, may hold values from -6 to 6
- embed_table: bfloat16 [156, 4096], replicated, may hold values from -6 to 6
- up_weight: bfloat16 [4096, 11008], P('col', 'row'), may hold values from -0.09375 to 0.09375
- down_weight: bfloat16 [11008, 4096], P(('row', 'col')), may hold values from -0.0546875 to 0.0546875
- up_left: bfloat16 [512, 4096], P('pop', 'col'), may hold values from -6 to 6
- up_right: bfloat16 [512, 11008], P('pop', 'row'), may hold values from -6 to 6
- down_left: bfloat16 [512, 11008], P('pop', ('row', 'col')), may hold values from -6 to 6
- down_right: bfloat16 [512, 4096], P('pop'), may hold values from -6 to 6
- up_moment: float32 [8, 4, 128, 11008], P('col', 'pop', None, 'row'), may hold values from -6 to 6
- up_second: float32 [8, 4, 128, 11008], P('col', 'pop', None, 'row'), may hold values from 0.5 to 4
- down_moment: float32 [32, 4, 86, 4096], P(('row', 'col'), 'pop'), may hold values from -6 to 6
- down_second: float32 [32, 4, 86, 4096], P(('row', 'col'), 'pop'), may hold values from 0.5 to 4
Outputs:
- block_out: bfloat16 [8192, 4096], P(('pop', 'row', 'col'))
- up_moment_new: float32 [8, 4, 128, 11008], P('col', 'pop', None, 'row')
- up_second_new: float32 [8, 4, 128, 11008], P('col', 'pop', None, 'row')
- up_step: float32 [8, 4, 128, 11008], P('col', 'pop', None, 'row')
- down_moment_new: float32 [32, 4, 86, 4096], P(('row', 'col'), 'pop')
- down_second_new: float32 [32, 4, 86, 4096], P(('row', 'col'), 'pop')
- down_step: float32 [32, 4, 86, 4096], P(('row', 'col'), 'pop')
Inputs may be any that keep to these rules, and one draw needn't show every extreme that they name: `member_ids`: each member number appears in exactly one slot.
All inputs are finite; a program needn't handle non-finite values.
Results may differ from a plain program's by a relative error of at most 0.02.
Values may be sent and summed in bfloat16 or wider, within the bound.
No kernel may reach another device: no remote copies, remote signals or barrier semaphores. Data moves between devices by JAX's collectives and lax.ppermute only.
A program may use at most 192 MiB of HBM per device.

v0:
```python
import jax
import jax.numpy as jnp
from jax import lax
from jax.sharding import PartitionSpec as P

noise_scale = 0.01
fitness_eps = 1e-05
beta_first = 0.9
beta_second = 0.999
adam_eps = 1e-08


def adam_update(moment, second, gradient):
    gradient = gradient.reshape(moment.shape)
    first_new = beta_first * moment + (1.0 - beta_first) * gradient
    second_new = beta_second * second + (1.0 - beta_second) * gradient * gradient
    return (first_new, second_new, first_new / (jnp.sqrt(second_new) + adam_eps))


def lookup_rows(code_rows, table):
    one_hot = (code_rows[:, None] == jnp.arange(table.shape[0])[None, :]).astype(jnp.bfloat16)
    return jnp.dot(one_hot, table, preferred_element_type=jnp.float32)


def contract_first(left_part, right_part):
    return lax.dot_general(
        left_part, right_part, (((0,), (0,)), ((), ())), preferred_element_type=jnp.float32
    )


def output_term(hidden_cols, weight_cols, probe_flat, right_factor, per_member, amount):
    product = contract_first(hidden_cols, weight_cols)
    owners_count = amount // per_member
    right_rows = right_factor.astype(jnp.float32)
    low_rank = (
        probe_flat.reshape(owners_count, per_member)[:, :, None] * right_rows[:, None, :]
    ).reshape(amount, right_factor.shape[1])
    return product + low_rank


def pooled(left_factor, right_factor):
    return lax.psum_scatter(
        contract_first(left_factor, right_factor), "pop", scatter_dimension=0, tiled=True
    )


def per_device(
    obs_ids,
    member_ids,
    fitness,
    embed_table,
    up_weight,
    down_weight,
    up_left,
    up_right,
    down_left,
    down_right,
    up_moment,
    up_second,
    down_moment,
    down_second,
):
    member_count, per_member = obs_ids.shape
    row_count = member_count * per_member
    feat_width = up_weight.shape[0]
    ff_quarter = up_weight.shape[1]
    col_index = lax.axis_index("col")
    flat_ids = obs_ids.reshape(row_count)
    table_cols = lax.dynamic_slice_in_dim(embed_table, col_index * feat_width, feat_width, 1)
    feat_cols = lookup_rows(flat_ids, table_cols).astype(jnp.bfloat16)
    probe_one = noise_scale * jnp.einsum(
        "mtd,md->mt",
        feat_cols.reshape(member_count, per_member, feat_width),
        up_left,
        preferred_element_type=jnp.float32,
    )
    product = lax.dot_general(
        up_weight, feat_cols, (((0,), (1,)), ((), ())), preferred_element_type=jnp.float32
    )
    right_cols = up_right.astype(jnp.float32)
    low_rank = (right_cols.T[:, :, None] * probe_one[None, :, :]).reshape(
        lax.axis_size("col") * (ff_quarter // lax.axis_size("col")), row_count
    )
    pre_hidden = lax.psum_scatter(
        (product + low_rank).astype(jnp.bfloat16), "col", scatter_dimension=0, tiled=True
    ).astype(jnp.float32)
    hidden_t = jax.nn.silu(pre_hidden).astype(jnp.bfloat16)
    ff_share = hidden_t.shape[0]
    probe_two = noise_scale * jnp.einsum(
        "fmt,mf->mt",
        hidden_t.reshape(ff_share, member_count, per_member),
        down_left,
        preferred_element_type=jnp.float32,
    ).reshape(row_count)
    summed = lax.psum_scatter(
        output_term(
            hidden_t,
            down_weight,
            probe_two,
            down_right,
            per_member,
            row_count // lax.axis_size(("row", "col")) * lax.axis_size(("row", "col")),
        ),
        ("row", "col"),
        scatter_dimension=0,
        tiled=True,
    )
    share_rows = summed.shape[0]
    mine_ids = lax.dynamic_slice_in_dim(
        flat_ids, lax.axis_index(("row", "col")) * share_rows, share_rows, 0
    )
    residual = lookup_rows(mine_ids, embed_table)
    block_out = (residual + summed).astype(jnp.bfloat16)
    members_all = fitness.shape[0]
    fit_mean = jnp.mean(fitness)
    fit_var = jnp.mean((fitness - fit_mean) * (fitness - fit_mean))
    slot_fit = jnp.sum(
        jnp.where(member_ids[:, None] == jnp.arange(members_all)[None, :], fitness[None, :], 0.0),
        axis=1,
    )
    fit_scale = (
        (slot_fit - fit_mean) / jnp.sqrt(fit_var + fitness_eps) / (members_all * noise_scale)
    )
    up_weighted = (fit_scale[:, None] * up_right.astype(jnp.float32)).astype(jnp.bfloat16)
    down_weighted = (fit_scale[:, None] * down_right.astype(jnp.float32)).astype(jnp.bfloat16)
    up_grad = pooled(up_left, up_weighted)
    down_grad = pooled(down_left, down_weighted)
    up_first, up_sec, up_step = adam_update(up_moment, up_second, up_grad)
    down_first, down_sec, down_step = adam_update(down_moment, down_second, down_grad)
    return (block_out, up_first, up_sec, up_step, down_first, down_sec, down_step)


def solution(mesh):
    in_specs = (
        P("pop", None),
        P("pop"),
        P(),
        P(),
        P("col", "row"),
        P(("row", "col"), None),
        P("pop", "col"),
        P("pop", "row"),
        P("pop", ("row", "col")),
        P("pop", None),
        P("col", "pop", None, "row"),
        P("col", "pop", None, "row"),
        P(("row", "col"), "pop", None, None),
        P(("row", "col"), "pop", None, None),
    )
    out_specs = (
        P(("pop", "row", "col"), None),
        P("col", "pop", None, "row"),
        P("col", "pop", None, "row"),
        P("col", "pop", None, "row"),
        P(("row", "col"), "pop", None, None),
        P(("row", "col"), "pop", None, None),
        P(("row", "col"), "pop", None, None),
    )
    return jax.shard_map(
        per_device, mesh=mesh, in_specs=in_specs, out_specs=out_specs, check_vma=False
    )
```

profile of v0, /device:TPU:1, one launch (start us, length us, event | category | flops | bytes accessed | tf_op | source)
XLA Modules:
  0.0 643.7 jit_solution(15655943854743604016)
XLA Ops:
  7.2 2.4 convert_bitcast_fusion
  9.7 2.9 copy.45
  12.6 10.8 %mul.151 = f32[2752,128,16]{0,2,1:T(8,128)} broadcast(f32[2752,128]{0,1:T(8,128)} %copy.45), dimensions={0,1} | broadcast | bytes 23953408 | tf_op jit(solution)/shard_map/mul | solution.py:81
  23.4 23.2 %copy.46 = f32[2752,2048]{1,0:T(8,128)} copy(f32[2752,2048]{0,1:T(8,128)} %bitcast.51) | data formatting | bytes 45088768 | tf_op jit(solution)/shard_map/mul | solution.py:81
  46.8 2.0 convolution_convert_fusion
  50.3 14.5 %fusion.2 = bf16[2752,2048]{1,0:T(8,128)(2,1)} fusion(f32[2752,2048]{1,0:T(8,128)} %copy.46, bf16[2048,512]{1,0:T(8,128)(2,1)} %copy-done.3, bf16[512,2752]{0,1:T(8,128)(2,1)} %param.18, f32[2048]{0:T(1024)S(1)} %mul.155), kind=kOutput, calls=%fused_computation.3 | convolution fusion | flops 5788270592 | bytes 38739968 | tf_op jit(solution)/shard_map/dot_general | solution.py:77
  68.2 4.3 convolution_bitcast_fusion.1
  72.7 2.7 convert_element_type.36
  75.7 112.4 %reduce-scatter.6.cloned.1.call-done = bf16[344,2048]{1,0:T(8,128)(2,1)} async-done(((bf16[2752,2048]{1,0:T(8,128)(2,1)}), bf16[344,2048]{1,0:T(8,128)(2,1)}) %reduce-scatter.6.cloned.1.call-update) | async-done | bytes 1409040 | tf_op jit(solution)/shard_map/reduce_scatter | solution.py:84
  188.1 3.2 fusion.7
  191.3 2.6 copy.47
  193.9 2.1 fusion.26
  196.1 17.3 %fusion.1 = f32[2048,4096]{1,0:T(8,128)} fusion(f32[128,4096]{1,0:T(8,128)} %convert_element_type.36, f32[2048]{0:T(1024)S(1)} %mul.160, bf16[344,4096]{1,0:T(8,128)(2,1)S(1)} %copy-done, bf16[344,2048]{1,0:T(8,128)(2,1)} %reduce-scatter.6.cloned.1.call-done), kind=kOutput, calls=%fused_computation.1 | convolution fusion | flops 5792366592 | bytes 39886848 | tf_op jit(solution)/shard_map/dot_general | solution.py:26
  214.7 3.4 convolution_bitcast_fusion
  218.1 90.5 %fusion = f32[88,4096]{1,0:T(8,128)S(1)} fusion(f32[344,4096]{1,0:T(8,128)} %convolution_bitcast_fusion), kind=kCustom, calls=%all-reduce-scatter | all-reduce-scatter fusion | flops 1441793 | bytes 7078400
  308.6 1.5 collective-permute-start
  312.2 5.3 concatenate
  317.6 5.0 add_divide_fusion
  322.6 2.5 copy.50
  325.1 2.5 copy.51
  327.7 2.5 copy.52
  330.2 4.8 add_divide_fusion.1
  335.0 299.4 %reduce-scatter.8.cloned.1.call-done = f32[64,4096]{1,0:T(8,128)} async-done(((f32[2048,4096]{1,0:T(8,128)}), f32[64,4096]{1,0:T(8,128)}) %reduce-scatter.8.cloned.1.call-update) | async-done | bytes 1048592 | tf_op jit(solution)/shard_map/reduce_scatter | solution.py:95
  634.4 2.8 fusion.3
  (45 shorter events, 7.0 us)
Async XLA Ops:
  7.2 188.9 %copy-start = (bf16[344,4096]{1,0:T(8,128)(2,1)S(1)}, bf16[344,4096]{1,0:T(8,128)(2,1)}, u32[]{:S(2)}) copy-start(bf16[344,4096]{1,0:T(8,128)(2,1)} %param.19) | copy-start | bytes 8454148
  7.2 180.9 %reduce-scatter.6.cloned.1.call-start = ((), (), s32[]{:S(2)}) async-start(), calls=%async_computation.3 | async-start | bytes 12681216 | tf_op jit(solution)/shard_map/reduce_scatter | solution.py:84
  23.4 23.2 %copy-start.8 = (s32[128,16]{0,1:T(8,128)S(1)}, s32[128,16]{0,1:T(8,128)}, u32[]{:S(2)}) copy-start(s32[128,16]{0,1:T(8,128)} %param.14) | copy-start | bytes 24580
  46.8 2.0 copy-start.6
  48.8 1.4 copy-start.3
  64.7 0.7 copy-start.7
  64.7 3.2 copy-start.10
  64.7 3.4 copy-start.4
  64.8 265.5 %reduce-scatter.10.cloned.1.call-start = ((), (), s32[]{:S(2)}) async-start(), calls=%async_computation.5 | async-start | bytes 7045120 | tf_op jit(solution)/shard_map/reduce_scatter | solution.py:42
  72.5 3.0 copy-start.5
  72.5 561.9 %reduce-scatter.8.cloned.1.call-start = ((), (), s32[]{:S(2)}) async-start(), calls=%async_computation.4 | async-start | bytes 34603008 | tf_op jit(solution)/shard_map/reduce_scatter | solution.py:95
  213.4 1.3 copy-start.2
  218.1 92.2 %copy-start.9 = (u32[128]{0:T(128)S(1)}, u32[128]{0:T(128)}, u32[]{:S(2)}) copy-start(u32[128]{0:T(128)} %constant.60) | copy-start | bytes 1540
  308.6 3.6 collective-permute-start
  330.2 307.0 %copy-start.1 = (bf16[344,4096]{1,0:T(8,128)(2,1)S(1)}, bf16[344,4096]{1,0:T(8,128)(2,1)}, u32[]{:S(2)}) copy-start(bf16[344,4096]{1,0:T(8,128)(2,1)} %param.19) | copy-start | bytes 8454148
Sparse Core Ops, SparseCore 0:
  64.9 123.1 reduce-scatter.5
  190.5 75.7 reduce-scatter.9
  268.7 365.6 reduce-scatter.7
where the time goes:
time: 645 us; the launch traced here: 644 us
  waiting for transfers between devices  413 us (64%)
  blocking collectives  90.5 us (14%)
  local copies, waits for them, and re-layouts  56.2 us (9%)
  matrix products  47 us (7%)
  other arithmetic  19.6 us (3%)
  between operations  15.9 us (2%)
    reduce_scatter x1, waiting for transfers between devices, per_device(): lax.psum_scatter(output_term(hidden_t, down_weight, probe_two, down_right...  299 us
    reduce_scatter x1, waiting for transfers between devices, per_device(): lax.psum_scatter((product + low_rank).astype(jnp.bfloat16), 'col', scatte...  112 us
    unnamed x1, blocking collectives  90.5 us
    mul x3, local copies, waits for them, and re-layouts, per_device(): right_cols.T[:, :, None] * probe_one[None, :, :]  34.1 us
    dot_general x3, matrix products, contract_first(): lax.dot_general(left_part, right_part, (((0,), (0,)), ((), ())), preferre...  25 us
    unnamed x30, local copies, waits for them, and re-layouts  16.4 us
    dot_general x1, matrix products, per_device(): lax.dot_general(up_weight, feat_cols, (((0,), (1,)), ((), ())), preferred...  14.5 us
  transfers between devices with their start and end apart: 4, of which 3 were waited for; matrix products, arithmetic and copies ran while one was open for 23% of the time, Pallas kernels for 0%

commit v1 on v0

v1 whole, which is shorter than its diff:
```python
import functools

import jax
import jax.numpy as jnp
from jax import lax
from jax.experimental import pallas as pl
from jax.experimental.pallas import tpu as pltpu
from jax.sharding import PartitionSpec as P

noise_scale = 0.01
fitness_eps = 1e-05
beta_first = 0.9
beta_second = 0.999
adam_eps = 1e-08

BF = jnp.bfloat16
F32 = jnp.float32
VMEM_LIMIT = 48 * 1024 * 1024
BLOCK = 256
CODES = 160


def shifted(value, axis, step):
    size = lax.axis_size(axis)
    return lax.ppermute(value, axis, [(i, (i + step) % size) for i in range(size)])


def gather_pop(value):
    return [value] + [shifted(value, "pop", step) for step in (1, 3, 2)]


def silu(value):
    half = 0.5 * value
    return half + half * jnp.tanh(half)


def hidden_kernel(codes, probe, table, right, weight, out, rhs, hidden):
    ff = table.shape[1]
    codes_count = table.shape[0]
    slots = right.shape[0]
    rows = codes.shape[0]
    depth = rhs.shape[0]

    @pl.when(pl.program_id(0) == 0)
    def _():
        rhs[...] = jnp.zeros_like(rhs)
        rhs[pl.ds(0, codes_count), :] = table[...]

    rhs[pl.ds(codes_count, slots), :] = right[...]
    rhs[pl.ds(codes_count + slots, slots), :] = right[...]
    lane = lax.broadcasted_iota(jnp.int32, (rows, depth), 1)
    slot = lax.broadcasted_iota(jnp.int32, (rows, depth), 0) // (rows // slots)
    high = probe[...].astype(BF).astype(F32)
    low = probe[...] - high
    lhs = jnp.where(lane == codes[...], 1.0, 0.0)
    lhs = jnp.where(lane - codes_count == slot, high, lhs)
    lhs = jnp.where(lane - codes_count - slots == slot, low, lhs).astype(BF)
    for start in range(0, ff, 256):
        width = min(256, ff - start)
        pre = jnp.dot(lhs, rhs[:, start : start + width], preferred_element_type=F32)
        hidden[:, start : start + width] = silu(pre).astype(BF)
    out[...] = jnp.dot(hidden[...], weight[...], preferred_element_type=F32).astype(out.dtype)


def hidden_product(codes, probe, table, right, weight):
    rows = codes.shape[0]
    ff = table.shape[1]
    slots = right.shape[0] * BLOCK // rows
    width = weight.shape[1]
    return pl.pallas_call(
        hidden_kernel,
        grid=(rows // BLOCK,),
        in_specs=[
            pl.BlockSpec((BLOCK, 1), lambda i: (i, 0)),
            pl.BlockSpec((BLOCK, 1), lambda i: (i, 0)),
            pl.BlockSpec(table.shape, lambda i: (0, 0)),
            pl.BlockSpec((slots, ff), lambda i: (i, 0)),
            pl.BlockSpec(weight.shape, lambda i: (0, 0)),
        ],
        out_specs=pl.BlockSpec((BLOCK, width), lambda i: (i, 0)),
        out_shape=jax.ShapeDtypeStruct((rows, width), BF),
        scratch_shapes=[pltpu.VMEM((256, ff), BF), pltpu.VMEM((BLOCK, ff), BF)],
        compiler_params=pltpu.CompilerParams(vmem_limit_bytes=VMEM_LIMIT),
        cost_estimate=pl.CostEstimate(
            flops=2 * rows * ff * (256 + width), bytes_accessed=8 << 20, transcendentals=rows * ff
        ),
    )(codes, probe, table, right, weight)


def adam_kernel(left, w0, w1, w2, w3, moment, second, first_new, second_new, step):
    grad = None
    for index, part in enumerate((w0, w1, w2, w3)):
        term = lax.dot_general(
            left[index], part[...], (((0,), (0,)), ((), ())), preferred_element_type=F32
        )
        grad = term if grad is None else grad + term
    first = beta_first * moment[...] + (1.0 - beta_first) * grad
    sec = beta_second * second[...] + (1.0 - beta_second) * grad * grad
    first_new[...] = first
    second_new[...] = sec
    step[...] = first / (jnp.sqrt(sec) + adam_eps)


def adam_update(left, weighted, moment, second, tile):
    rows, width = moment.shape
    slots = left.shape[1]
    wide = pl.BlockSpec((slots, tile), lambda j: (0, j))
    state = pl.BlockSpec((rows, tile), lambda j: (0, j))
    return pl.pallas_call(
        adam_kernel,
        grid=(pl.cdiv(width, tile),),
        in_specs=[pl.BlockSpec(left.shape, lambda j: (0, 0, 0))] + [wide] * 4 + [state] * 2,
        out_specs=[state] * 3,
        out_shape=[jax.ShapeDtypeStruct(moment.shape, F32)] * 3,
        compiler_params=pltpu.CompilerParams(vmem_limit_bytes=VMEM_LIMIT),
        cost_estimate=pl.CostEstimate(
            flops=8 * slots * rows * width, bytes_accessed=20 * rows * width, transcendentals=0
        ),
    )(left, *weighted, moment, second)


def per_device(
    obs_ids,
    member_ids,
    fitness,
    embed_table,
    up_weight,
    down_weight,
    up_left,
    up_right,
    down_left,
    down_right,
    up_moment,
    up_second,
    down_moment,
    down_second,
):
    member_count, per_member = obs_ids.shape
    row_count = member_count * per_member
    vocab, model = embed_table.shape
    feat_width, ff_quarter = up_weight.shape
    ff_share = down_weight.shape[0]
    cols = lax.axis_size("col")
    rows_axis = lax.axis_size("row")
    pops = lax.axis_size("pop")
    col_index = lax.axis_index("col")
    flat_ids = obs_ids.reshape(row_count)

    members_all = fitness.shape[0]
    fit_mean = jnp.mean(fitness)
    fit_var = jnp.mean((fitness - fit_mean) * (fitness - fit_mean))
    slot_fit = jnp.sum(
        jnp.where(member_ids[:, None] == jnp.arange(members_all)[None, :], fitness[None, :], 0.0),
        axis=1,
    )
    fit_scale = (
        (slot_fit - fit_mean) / jnp.sqrt(fit_var + fitness_eps) / (members_all * noise_scale)
    )
    up_weighted = (fit_scale[:, None] * up_right.astype(F32)).astype(BF)
    down_weighted = (fit_scale[:, None] * down_right.astype(F32)).astype(BF)

    table = jnp.pad(embed_table, ((0, CODES - vocab), (0, 0)))
    table_cols = lax.dynamic_slice_in_dim(table, col_index * feat_width, feat_width, 1)
    part = jnp.dot(table_cols, up_weight, preferred_element_type=F32).astype(BF)
    probe_table = lax.dot_general(
        up_left, table_cols, (((1,), (1,)), ((), ())), preferred_element_type=F32
    )
    one_hot = obs_ids[:, :, None] == jnp.arange(CODES)[None, None, :]
    probe_part = jnp.sum(jnp.where(one_hot, probe_table[:, None, :], 0.0), axis=2).astype(BF)
    probe_part = jnp.pad(probe_part, ((0, CODES - member_count), (0, 0)))
    sent = jnp.concatenate(
        [
            part.reshape(CODES, cols, ff_share).transpose(1, 0, 2),
            jnp.broadcast_to(probe_part[None], (cols, CODES, per_member)),
        ],
        axis=2,
    )
    got = lax.all_to_all(sent, "col", 0, 0, tiled=True)
    total = jnp.sum(got.astype(F32), axis=0)
    table_share = total[:, :ff_share].astype(BF)
    probe = noise_scale * total[:member_count, ff_share:]
    probe_col = probe.reshape(row_count, 1)

    weight = lax.all_to_all(down_weight, "col", 1, 0, tiled=True)

    shares = lax.all_to_all(
        jnp.broadcast_to(table_share[None], (cols, CODES, ff_share)), "col", 0, 0, tiled=True
    )
    table_wide = shares.transpose(1, 0, 2).reshape(CODES, ff_quarter)

    codes_col = flat_ids.reshape(row_count, 1)
    partial = hidden_product(codes_col, probe_col, table_wide, up_right, weight)

    right_share = lax.dynamic_slice_in_dim(up_right, col_index * ff_share, ff_share, 1)
    hot = (flat_ids[:, None] == jnp.arange(CODES)[None, :]).astype(BF)
    pre_share = jnp.dot(hot, table_share, preferred_element_type=F32)
    pre_share = pre_share.reshape(member_count, per_member, ff_share) + (
        probe[:, :, None] * right_share.astype(F32)[:, None, :]
    )
    hidden_share = silu(pre_share).astype(BF)
    probe_two = jnp.sum(hidden_share.astype(F32) * down_left.astype(F32)[:, None, :], axis=2)
    probe_two = noise_scale * jnp.sum(
        lax.all_to_all(
            probe_two.reshape(rows_axis * cols, 1, row_count // (rows_axis * cols)),
            ("row", "col"),
            0,
            0,
            tiled=True,
        ),
        axis=(0, 1),
    )

    share_rows = row_count // (rows_axis * cols)
    by_row = lax.all_to_all(
        partial.reshape(rows_axis, row_count // rows_axis, model // cols), "row", 0, 0, tiled=True
    )
    reduced = jnp.sum(by_row.astype(F32), axis=0).astype(BF)
    final = lax.all_to_all(
        reduced.reshape(cols, share_rows, model // cols), "col", 0, 0, tiled=True
    )
    product = final.transpose(1, 0, 2).reshape(share_rows, model).astype(F32)
    place = lax.axis_index(("row", "col"))
    mine_ids = lax.dynamic_slice_in_dim(flat_ids, place * share_rows, share_rows, 0)
    mine_hot = (mine_ids[:, None] == jnp.arange(vocab)[None, :]).astype(BF)
    residual = jnp.dot(mine_hot, embed_table, preferred_element_type=F32)
    share_slots = share_rows // per_member
    mine_right = lax.dynamic_slice_in_dim(down_right, place * share_slots, share_slots, 0)
    low_rank = (
        probe_two.reshape(share_slots, per_member)[:, :, None]
        * mine_right.astype(F32)[:, None, :]
    ).reshape(share_rows, model)
    block_out = (residual + product + low_rank).astype(BF)

    pop_index = lax.axis_index("pop")
    up_parts = gather_pop(up_weighted)
    down_parts = gather_pop(down_weighted)
    up_rows = feat_width // pops
    down_rows = ff_share // pops
    lefts = jnp.concatenate(
        [
            up_left.reshape(member_count, pops, up_rows).transpose(1, 0, 2),
            down_left.reshape(member_count, pops, down_rows).transpose(1, 0, 2),
        ],
        axis=2,
    )
    lefts = lax.all_to_all(lefts, "pop", 0, 0, tiled=True)
    order = (pop_index + jnp.array([0, 3, 1, 2], jnp.int32)) % pops
    lefts = jnp.take(lefts, order, axis=0)
    up_out = adam_update(
        lefts[:, :, :up_rows],
        up_parts,
        up_moment.reshape(up_rows, ff_quarter),
        up_second.reshape(up_rows, ff_quarter),
        1408,
    )
    down_out = adam_update(
        lefts[:, :, up_rows:],
        down_parts,
        down_moment.reshape(down_rows, model),
        down_second.reshape(down_rows, model),
        2048,
    )
    up_out = [value.reshape(up_moment.shape) for value in up_out]
    down_out = [value.reshape(down_moment.shape) for value in down_out]
    return (block_out, *up_out, *down_out)


def solution(mesh):
    in_specs = (
        P("pop", None),
        P("pop"),
        P(),
        P(),
        P("col", "row"),
        P(("row", "col"), None),
        P("pop", "col"),
        P("pop", "row"),
        P("pop", ("row", "col")),
        P("pop", None),
        P("col", "pop", None, "row"),
        P("col", "pop", None, "row"),
        P(("row", "col"), "pop", None, None),
        P(("row", "col"), "pop", None, None),
    )
    out_specs = (
        P(("pop", "row", "col"), None),
        P("col", "pop", None, "row"),
        P("col", "pop", None, "row"),
        P("col", "pop", None, "row"),
        P(("row", "col"), "pop", None, None),
        P(("row", "col"), "pop", None, None),
        P(("row", "col"), "pop", None, None),
    )
    return jax.shard_map(
        per_device, mesh=mesh, in_specs=in_specs, out_specs=out_specs, check_vma=False
    )
```

time: 645 us -> 219 us (0.34)
  waiting for transfers between devices: 413 us -> 31 us
  blocking collectives: 90.5 us -> 19.4 us
  starting transfers between devices: 1.82 us -> 41.8 us
  matrix products: 47 us -> 7.72 us
  local copies, waits for them, and re-layouts: 56.2 us -> 80 us
  Pallas kernels: 0 us -> 23.1 us
  between operations: 15.9 us -> 2.38 us
  other arithmetic: 19.6 us -> 12.2 us
    reduce_scatter x3 -> x0, waiting for transfers between devices: 412 us -> none  [the longest x1 299 us: per_device(): lax.psum_scatter(output_term(hidden_t, down_weight, probe_two, down_right...]
    unnamed x1 -> x0, blocking collectives: 90.5 us -> none
    dot_general x8 -> x4, matrix products: 47 us -> 7.72 us  [the longest x1 3.42 us: per_device(): pre_share = jnp.dot(hot, table_share, preferred_element_type=F32)]
    all_to_all x0 -> x6, starting transfers between devices: none -> 34.2 us  [the longest x1 7.05 us: per_device(): weight = lax.all_to_all(down_weight, 'col', 1, 0, tiled=True)]
    all_to_all x0 -> x6, waiting for transfers between devices: none -> 31 us  [the longest x1 13.1 us: per_device(): lefts = lax.all_to_all(lefts, 'pop', 0, 0, tiled=True)]
    unnamed x30 -> x73, local copies, waits for them, and re-layouts: 16.4 us -> 42.5 us
    mul x4 -> x5, local copies, waits for them, and re-layouts: 34.2 us -> 10.9 us  [the longest x2 5.47 us: per_device(): hidden_share.astype(F32) * down_left.astype(F32)[:, None, :]]
    pallas_call x0 -> x3, Pallas kernels: none -> 23.1 us  [the longest x1 13.8 us: hidden_product(): pl.pallas_call(hidden_kernel, grid=(rows // BLOCK,), in_specs=[pl.BlockSp...]
  transfers between devices with their start and end apart: 4 -> 12, of which waited for: 3 -> 4; matrix products, arithmetic and copies ran while one was open for 23% -> 35% of each run, Pallas kernels for 0% -> 11%
where the time goes in v1:
time: 219 us; the launch traced here: 218 us
  local copies, waits for them, and re-layouts  80 us (37%)
  starting transfers between devices  41.8 us (19%)
  waiting for transfers between devices  31 us (14%)
  Pallas kernels  23.1 us (11%)
  blocking collectives  19.4 us (9%)
  other arithmetic  12.2 us (6%)
  matrix products  7.72 us (4%)
  between operations  2.38 us (1%)
    unnamed x73, local copies, waits for them, and re-layouts  42.5 us
    all_to_all x1, blocking collectives, per_device(): got = lax.all_to_all(sent, 'col', 0, 0, tiled=True)  19.4 us
    pallas_call x1, Pallas kernels, hidden_product(): pl.pallas_call(hidden_kernel, grid=(rows // BLOCK,), in_specs=[pl.BlockSp...  13.8 us
    all_to_all x1, waiting for transfers between devices, per_device(): lefts = lax.all_to_all(lefts, 'pop', 0, 0, tiled=True)  13.1 us
    pallas_call x2, Pallas kernels, adam_update(): pl.pallas_call(adam_kernel, grid=(pl.cdiv(width, tile),), in_specs=[pl.Bl...  9.22 us
    all_to_all x1, waiting for transfers between devices, per_device(): weight = lax.all_to_all(down_weight, 'col', 1, 0, tiled=True)  8.14 us
    ppermute x6, starting transfers between devices, shifted(): lax.ppermute(value, axis, [(i, (i + step) % size) for i in range(size)])  7.61 us
    all_to_all x1, starting transfers between devices, per_device(): weight = lax.all_to_all(down_weight, 'col', 1, 0, tiled=True)  7.05 us
  transfers between devices with their start and end apart: 12, of which 4 were waited for; matrix products, arithmetic and copies ran while one was open for 35% of the time, Pallas kernels for 11%

profile of v1, /device:TPU:1, one launch (start us, length us, event | category | flops | bytes accessed | tf_op | source)
XLA Modules:
  0.0 217.5 jit_solution(5276682659468558195)
XLA Ops:
  2.4 2.9 %convolution_convert_fusion = bf16[160,2752]{1,0:T(8,128)(2,1)} fusion(bf16[512,2752]{0,1:T(8,128)(2,1)S(1)} %copy-done, s32[]{:T(128)S(6)} %select_n.37, bf16[156,4096]{1,0:T(8,128)(2,1)} %param.18), kind=kOutput, calls=%fused_computation.5 | convolution fusion | flops 451328000 | bytes 4976644 | tf_op jit(solution)/shard_map/dot_general | solution.py:164
  10.9 19.4 %all_to_all.49 = bf16[8,160,360]{2,1,0:T(8,128)(2,1)S(1)} all-to-all(bf16[8,160,360]{2,1,0:T(8,128)(2,1)S(1)} %pad_maximum_fusion), channel_id=1, replica_groups=mesh['pop'=4,'row'=4,'col'=8] {'col'}, dimensions={0} | all-to-all | bytes 1843200 | tf_op jit(solution)/shard_map/all_to_all | solution.py:178
  31.5 3.6 %all-to-all-start.1 = ((bf16[8,160,344]{2,1,0:T(8,128)(2,1)}), bf16[8,160,344]{2,1,0:T(8,128)(2,1)S(1)}, u32[]{:S(2)}, u32[]{:S(2)}) async-start(bf16[8,160,344]{2,1,0:T(8,128)(2,1)} %broadcast_in_dim.40), calls=%async_computation.1 | async-start | bytes 1966080 | tf_op jit(solution)/shard_map/all_to_all | solution.py:186
  35.1 3.6 %copy.198 = bf16[43,8,8,512]{3,2,0,1:T(8,128)(2,1)} copy(bf16[43,8,8,512]{3,2,1,0:T(8,128)(2,1)} %bitcast.56) | data formatting | bytes 5636096 | tf_op jit(solution)/shard_map/all_to_all | solution.py:184
  38.7 7.0 %all-to-all-done.1 = bf16[8,160,344]{2,1,0:T(8,128)(2,1)S(1)} async-done(((bf16[8,160,344]{2,1,0:T(8,128)(2,1)}), bf16[8,160,344]{2,1,0:T(8,128)(2,1)S(1)}, u32[]{:S(2)}, u32[]{:S(2)}) %all-to-all-start.1) | async-done | bytes 880672 | tf_op jit(solution)/shard_map/all_to_all | solution.py:186
  46.6 7.1 %all-to-all-start.2 = ((bf16[344,8,512]{2,0,1:T(8,128)(2,1)}), bf16[344,8,512]{2,0,1:T(8,128)(2,1)}, u32[]{:S(2)}, u32[]{:S(2)}) async-start(bf16[344,8,512]{2,0,1:T(8,128)(2,1)} %bitcast.43), calls=%async_computation.2 | async-start | bytes 5636096 | tf_op jit(solution)/shard_map/all_to_all | solution.py:184
  79.5 8.1 %all-to-all-done.2 = bf16[344,8,512]{2,0,1:T(8,128)(2,1)} async-done(((bf16[344,8,512]{2,0,1:T(8,128)(2,1)}), bf16[344,8,512]{2,0,1:T(8,128)(2,1)}, u32[]{:S(2)}, u32[]{:S(2)}) %all-to-all-start.2) | async-done | bytes 2818080 | tf_op jit(solution)/shard_map/all_to_all | solution.py:184
  87.7 5.0 %all-to-all-start.6 = ((bf16[4,128,214]{1,2,0:T(8,128)(2,1)}), bf16[4,128,214]{1,2,0:T(8,128)(2,1)S(1)}, u32[]{:S(2)}, u32[]{:S(2)}) async-start(bf16[4,128,214]{1,2,0:T(8,128)(2,1)} %pad_maximum_fusion.1), calls=%async_computation.6 | async-start | bytes 442368 | tf_op jit(solution)/shard_map/all_to_all | solution.py:246
  96.3 13.8 %shard_map.198 = bf16[2048,512]{1,0:T(8,128)(2,1)S(1)} custom-call(s32[2048,1]{1,0:T(8,128)S(1)} %copy-done.7, f32[2048,1]{1,0:T(8,128)S(1)} %copy-done.8, bf16[160,2752]{1,0:T(8,128)(2,1)S(1)} %copy-done.9, bf16[128,2752]{1,0:T(8,128)(2,1)S(1)} %copy.164.right, bf16[2752,512]{1,0:T(8,128)(2,1)} %bitcast.4.weight), custom_call_target="tpu_custom_call" | custom-call | flops 8657043456 | bytes 8388608 | tf_op jit(solution)/shard_map/pallas_call | solution.py:70
  111.6 13.1 %all-to-all-done.6 = bf16[4,128,214]{1,2,0:T(8,128)(2,1)S(1)} async-done(((bf16[4,128,214]{1,2,0:T(8,128)(2,1)}), bf16[4,128,214]{1,2,0:T(8,128)(2,1)S(1)}, u32[]{:S(2)}, u32[]{:S(2)}) %all-to-all-start.6) | async-done | bytes 219168 | tf_op jit(solution)/shard_map/all_to_all | solution.py:246
  124.7 7.0 %all-to-all-start.3 = ((bf16[4,512,512]{2,1,0:T(8,128)(2,1)}), bf16[4,512,512]{2,1,0:T(8,128)(2,1)}, u32[]{:S(2)}, u32[]{:S(2)}) async-start(bf16[4,512,512]{2,1,0:T(8,128)(2,1)} %bitcast.45), calls=%async_computation.3 | async-start | bytes 4194304 | tf_op jit(solution)/shard_map/all_to_all | solution.py:214
  131.7 5.8 %copy_bitcast_fusion.1 = (f32[86,4096]{1,0:T(8,128)}, f32[86,4096]{1,0:T(8,128)}) fusion(f32[1,1,86,4096]{3,1,2,0:T(1,128)} %param.28, f32[1,1,86,4096]{3,1,2,0:T(1,128)} %param.27), kind=kLoop, calls=%fused_computation.14 | loop fusion | bytes 5636096
  141.2 3.5 %copy.167 = f32[2048,344]{0,1:T(8,128)} copy(f32[2048,344]{1,0:T(8,128)} %bitcast.49) | data formatting | bytes 5636096 | tf_op jit(solution)/shard_map/mul | solution.py:198
  146.6 3.6 %copy.169 = f32[2048,344]{0,1:T(8,128)} copy(f32[2048,344]{1,0:T(8,128)} %bitcast.50) | data formatting | bytes 5636096 | tf_op jit(solution)/shard_map/mul | solution.py:201
  151.3 3.4 %multiply_reduce_fusion = f32[2048]{0:T(1024)S(1)} fusion(f32[2048,344]{0,1:T(8,128)} %copy.169, f32[2048,344]{0,1:T(8,128)} %copy.167, f32[2048]{0:T(1024)S(1)} %mul.111, s32[2048]{0:T(1024)S(1)} %reshape.114, f32[160,360]{1,0:T(8,128)S(1)} %copy-done.19), kind=kOutput, calls=%fused_computation.9 | convolution fusion | flops 232110080 | bytes 5783552 | tf_op jit(solution)/shard_map/dot_general | solution.py:196
  158.1 6.5 %all-to-all-start.5 = ((f32[32,1,64]{2,1,0:T(1,128)}), f32[32,1,64]{2,1,0:T(1,128)S(1)}, u32[]{:S(2)}, u32[]{:S(2)}) async-start(f32[32,1,64]{2,1,0:T(1,128)} %reshape.120), calls=%async_computation.5 | async-start | bytes 32768 | tf_op jit(solution)/shard_map/all_to_all | solution.py:203
  165.2 2.9 %copy.178 = f32[1,1,128,2752]{3,2,1,0:T(8,128)} copy(f32[1,1,128,2752]{2,3,1,0:T(8,128)} %param.25) | data formatting | bytes 2818048 | tf_op args[10]
  168.1 2.9 %copy.179 = f32[1,1,128,2752]{3,2,1,0:T(8,128)} copy(f32[1,1,128,2752]{2,3,1,0:T(8,128)} %param.26) | data formatting | bytes 2818048 | tf_op args[11]
  171.8 2.9 %reduce_sum.77 = bf16[512,512]{1,0:T(8,128)(2,1)} reduce(bf16[4,512,512]{2,1,0:T(8,128)(2,1)} %all-to-all-done.3, bf16[]{:T(256)} %constant.62.clone.1), dimensions={0}, to_apply=%region_2.3 | reduce | flops 786432 | bytes 2621442 | tf_op jit(solution)/shard_map/reduce_sum | solution.py:217
  174.6 5.1 %all-to-all-start.4 = ((bf16[8,64,512]{2,1,0:T(8,128)(2,1)}), bf16[8,64,512]{2,1,0:T(8,128)(2,1)}, u32[]{:S(2)}, u32[]{:S(2)}) async-start(bf16[8,64,512]{2,1,0:T(8,128)(2,1)} %bitcast.6), calls=%async_computation.4 | async-start | bytes 1048576 | tf_op jit(solution)/shard_map/all_to_all | solution.py:218
  186.0 4.3 %shard_map.199 = (f32[128,2752]{1,0:T(8,128)S(1)}, f32[128,2752]{1,0:T(8,128)S(1)}, f32[128,2752]{1,0:T(8,128)}) custom-call(bf16[4,128,128]{2,1,0:T(8,128)(2,1)S(1)} %slice.21.left, bf16[128,2752]{1,0:T(8,128)(2,1)S(1)} %multiply_convert_fusion.1.w0, bf16[128,2752]{1,0:T(8,128)(2,1)S(1)} %copy.180.w1, bf16[128,2752]{1,0:T(8,128)(2,1)S(1)} %copy.181.w2, ...), custom_call_target="tpu_custom_call" | custom-call | flops 360710144 | bytes 7045120 | tf_op jit(solution)/shard_map/pallas_call | solution.py:109
  192.5 3.0 %copy.183 = f32[1,1,128,2752]{2,3,1,0:T(8,128)} copy(f32[1,1,128,2752]{3,2,1,0:T(8,128)} %bitcast.47) | data formatting | bytes 2818048
  197.1 2.9 %copy.185 = f32[1,1,128,2752]{2,3,1,0:T(8,128)} copy(f32[1,1,128,2752]{3,2,1,0:T(8,128)} %bitcast.57) | data formatting | bytes 2818048
  201.2 4.9 %shard_map.200 = (f32[86,4096]{1,0:T(8,128)S(1)}, f32[86,4096]{1,0:T(8,128)}, f32[86,4096]{1,0:T(8,128)}) custom-call(bf16[4,128,86]{2,1,0:T(8,128)(2,1)S(1)} %slice.22.left, bf16[128,4096]{1,0:T(8,128)(2,1)S(1)} %multiply_convert_fusion.w0, bf16[128,4096]{1,0:T(8,128)(2,1)} %collective-permute-done.3.w1, bf16[128,4096]{1,0:T(8,128)(2,1)} %collective-permute-done.4.w2, ...), custom_call_target="tpu_custom_call" | custom-call | flops 360710144 | bytes 7045120 | tf_op jit(solution)/shard_map/pallas_call | solution.py:109
  (133 shorter events, 72.8 us)
Async XLA Ops:
  30.5 42.3 %copy-start.18 = (f32[160,360]{1,0:T(8,128)}, f32[160,360]{1,0:T(8,128)S(1)}, u32[]{:S(2)}) copy-start(f32[160,360]{1,0:T(8,128)S(1)} %convert_reduce_fusion) | copy-start | bytes 691204
  31.5 14.2 %all-to-all-start.1 = ((bf16[8,160,344]{2,1,0:T(8,128)(2,1)}), bf16[8,160,344]{2,1,0:T(8,128)(2,1)S(1)}, u32[]{:S(2)}, u32[]{:S(2)}) async-start(bf16[8,160,344]{2,1,0:T(8,128)(2,1)} %broadcast_in_dim.40), calls=%async_computation.1 | async-start | bytes 1966080 | tf_op jit(solution)/shard_map/all_to_all | solution.py:186
  45.7 8.0 %copy-start.17 = (bf16[128,2752]{0,1:T(8,128)(2,1)S(1)}, bf16[128,2752]{0,1:T(8,128)(2,1)}, u32[]{:S(2)}) copy-start(bf16[128,2752]{0,1:T(8,128)(2,1)} %param.22) | copy-start | bytes 2113540
  45.7 8.3 %copy-start.26 = (f32[512]{0:T(512)S(1)}, f32[512]{0:T(512)}, u32[]{:S(2)}) copy-start(f32[512]{0:T(512)} %param.17) | copy-start | bytes 6148
  45.7 10.8 %copy-start.28 = (s32[128]{0:T(128)S(1)}, s32[128]{0:T(128)}, u32[]{:S(2)}) copy-start(s32[128]{0:T(128)} %param.16) | copy-start | bytes 1540
  46.6 41.0 %all-to-all-start.2 = ((bf16[344,8,512]{2,0,1:T(8,128)(2,1)}), bf16[344,8,512]{2,0,1:T(8,128)(2,1)}, u32[]{:S(2)}, u32[]{:S(2)}) async-start(bf16[344,8,512]{2,0,1:T(8,128)(2,1)} %bitcast.43), calls=%async_computation.2 | async-start | bytes 5636096 | tf_op jit(solution)/shard_map/all_to_all | solution.py:184
  58.1 92.2 %collective-permute-start = (bf16[128,2752]{0,1:T(8,128)(2,1)}, bf16[128,2752]{0,1:T(8,128)(2,1)}, u32[]{:S(2)}, u32[]{:S(2)}) collective-permute-start(bf16[128,2752]{0,1:T(8,128)(2,1)} %copy.175), channel_id=1, source_target_pairs={{0,32},{32,64},{64,96},{96,0},{1,33},{33,65},{65,97},{97,1},{2,34}... | collective-permute-start | bytes 2113544 | tf_op jit(solution)/shard_map/ppermute | solution.py:25
  59.7 121.5 %collective-permute-start.1 = (bf16[128,2752]{0,1:T(8,128)(2,1)}, bf16[128,2752]{0,1:T(8,128)(2,1)}, u32[]{:S(2)}, u32[]{:S(2)}) collective-permute-start(bf16[128,2752]{0,1:T(8,128)(2,1)} %copy.175), channel_id=1, source_target_pairs={{0,96},{32,0},{64,32},{96,64},{1,97},{33,1},{65,33},{97,65},{2,98}... | collective-permute-start | bytes 2113544 | tf_op jit(solution)/shard_map/ppermute | solution.py:25
  63.3 137.8 %collective-permute-start.3 = (bf16[128,4096]{1,0:T(8,128)(2,1)S(1)}, bf16[128,4096]{1,0:T(8,128)(2,1)}, u32[]{:S(2)}, u32[]{:S(2)}) collective-permute-start(bf16[128,4096]{1,0:T(8,128)(2,1)S(1)} %multiply_convert_fusion.w0), channel_id=1, source_target_pairs={{0,32},{32,64},{64,96},{96,0},{1,33},{33,65},{65,97},{97,1},{2,34}... | collective-permute-start | bytes 3145736 | tf_op jit(solution)/shard_map/ppermute | solution.py:25
  63.4 137.7 %collective-permute-start.4 = (bf16[128,4096]{1,0:T(8,128)(2,1)S(1)}, bf16[128,4096]{1,0:T(8,128)(2,1)}, u32[]{:S(2)}, u32[]{:S(2)}) collective-permute-start(bf16[128,4096]{1,0:T(8,128)(2,1)S(1)} %multiply_convert_fusion.w0), channel_id=1, source_target_pairs={{0,96},{32,0},{64,32},{96,64},{1,97},{33,1},{65,33},{97,65},{2,98}... | collective-permute-start | bytes 3145736 | tf_op jit(solution)/shard_map/ppermute | solution.py:25
  66.1 135.1 %collective-permute-start.5 = (bf16[128,4096]{1,0:T(8,128)(2,1)S(1)}, bf16[128,4096]{1,0:T(8,128)(2,1)}, u32[]{:S(2)}, u32[]{:S(2)}) collective-permute-start(bf16[128,4096]{1,0:T(8,128)(2,1)S(1)} %multiply_convert_fusion.w0), channel_id=1, source_target_pairs={{0,64},{32,96},{64,0},{96,32},{1,65},{33,97},{65,1},{97,33},{2,66}... | collective-permute-start | bytes 3145736 | tf_op jit(solution)/shard_map/ppermute | solution.py:25
  66.3 4.8 %copy-start.20 = (s32[128,16]{1,0:T(8,128)}, s32[128,16]{1,0:T(8,128)S(1)}, u32[]{:S(2)}) copy-start(s32[128,16]{1,0:T(8,128)S(1)} %copy.156) | copy-start | bytes 24580
  87.7 37.0 %all-to-all-start.6 = ((bf16[4,128,214]{1,2,0:T(8,128)(2,1)}), bf16[4,128,214]{1,2,0:T(8,128)(2,1)S(1)}, u32[]{:S(2)}, u32[]{:S(2)}) async-start(bf16[4,128,214]{1,2,0:T(8,128)(2,1)} %pad_maximum_fusion.1), calls=%async_computation.6 | async-start | bytes 442368 | tf_op jit(solution)/shard_map/all_to_all | solution.py:246
  124.7 33.5 %all-to-all-start.3 = ((bf16[4,512,512]{2,1,0:T(8,128)(2,1)}), bf16[4,512,512]{2,1,0:T(8,128)(2,1)}, u32[]{:S(2)}, u32[]{:S(2)}) async-start(bf16[4,512,512]{2,1,0:T(8,128)(2,1)} %bitcast.45), calls=%async_computation.3 | async-start | bytes 4194304 | tf_op jit(solution)/shard_map/all_to_all | solution.py:214
  131.7 5.8 %copy-start.29 = (s32[4]{0:T(128)S(1)}, s32[4]{0:T(128)}, u32[]{:S(2)}) copy-start(s32[4]{0:T(128)} %constant.78.clone) | copy-start | bytes 52
  131.7 7.3 %copy-start.21 = (s32[128,16]{1,0:T(8,128)S(1)}, s32[128,16]{1,0:T(8,128)}, u32[]{:S(2)}) copy-start(s32[128,16]{1,0:T(8,128)} %copy-done.20) | copy-start | bytes 24580
  131.7 7.4 %copy-start.23 = (bf16[128,344]{0,1:T(8,128)(2,1)S(1)}, bf16[128,344]{0,1:T(8,128)(2,1)}, u32[]{:S(2)}) copy-start(bf16[128,344]{0,1:T(8,128)(2,1)} %param.23) | copy-start | bytes 264196
  146.6 4.7 %copy-start.19 = (f32[160,360]{1,0:T(8,128)S(1)}, f32[160,360]{1,0:T(8,128)}, u32[]{:S(2)}) copy-start(f32[160,360]{1,0:T(8,128)} %copy-done.18) | copy-start | bytes 691204
  150.3 32.4 %collective-permute-start.2 = (bf16[128,2752]{0,1:T(8,128)(2,1)}, bf16[128,2752]{0,1:T(8,128)(2,1)}, u32[]{:S(2)}, u32[]{:S(2)}) collective-permute-start(bf16[128,2752]{0,1:T(8,128)(2,1)} %copy.175), channel_id=1, source_target_pairs={{0,64},{32,96},{64,0},{96,32},{1,65},{33,97},{65,1},{97,33},{2,66}... | collective-permute-start | bytes 2113544 | tf_op jit(solution)/shard_map/ppermute | solution.py:25
  158.1 16.5 %all-to-all-start.5 = ((f32[32,1,64]{2,1,0:T(1,128)}), f32[32,1,64]{2,1,0:T(1,128)S(1)}, u32[]{:S(2)}, u32[]{:S(2)}) async-start(f32[32,1,64]{2,1,0:T(1,128)} %reshape.120), calls=%async_computation.5 | async-start | bytes 32768 | tf_op jit(solution)/shard_map/all_to_all | solution.py:203
  174.6 39.1 %all-to-all-start.4 = ((bf16[8,64,512]{2,1,0:T(8,128)(2,1)}), bf16[8,64,512]{2,1,0:T(8,128)(2,1)}, u32[]{:S(2)}, u32[]{:S(2)}) async-start(bf16[8,64,512]{2,1,0:T(8,128)(2,1)} %bitcast.6), calls=%async_computation.4 | async-start | bytes 1048576 | tf_op jit(solution)/shard_map/all_to_all | solution.py:218
  192.5 3.0 %copy-start.5 = (f32[128,2752]{1,0:T(8,128)S(1)}, f32[128,2752]{1,0:T(8,128)}, u32[]{:S(2)}) copy-start(f32[128,2752]{1,0:T(8,128)} %copy-done.4) | copy-start | bytes 4227076
  197.0 3.0 %copy-start.24 = (f32[4,4096]{1,0:T(4,128)S(1)}, f32[4,4096]{1,0:T(4,128)}, u32[]{:S(2)}) copy-start(f32[4,4096]{1,0:T(4,128)} %dynamic-slice_convert_fusion.1) | copy-start | bytes 196612
  208.6 2.5 %copy-start.15 = (f32[86,4096]{1,0:T(8,128)S(1)}, f32[86,4096]{1,0:T(8,128)}, u32[]{:S(2)}) copy-start(f32[86,4096]{1,0:T(8,128)} %get-tuple-element.18) | copy-start | bytes 4227076
  (18 other events, 26.6 us)

commit v2 on v0

v2 whole, which is shorter than its diff:
```python
import jax
import jax.numpy as jnp
from jax import lax
from jax.experimental import pallas as pl
from jax.experimental.pallas import tpu as pltpu
from jax.sharding import Mesh
from jax.sharding import PartitionSpec as P

noise_scale = 0.01
fitness_eps = 1e-05
beta_first = 0.9
beta_second = 0.999
adam_eps = 1e-08

BF = jnp.bfloat16
F32 = jnp.float32
VMEM_LIMIT = 60 * 1024 * 1024
CODES = 160
CHUNK = 512
TAIL = 16
NT = (((1,), (1,)), ((), ()))
TN = (((0,), (0,)), ((), ()))
ROW = ("xh", "core")


def params():
    return pltpu.CompilerParams(vmem_limit_bytes=VMEM_LIMIT)


def cost(flops, moved):
    return pl.CostEstimate(flops=flops, bytes_accessed=moved, transcendentals=0)


def whole(value):
    rank = len(value.shape)
    return pl.BlockSpec(value.shape, lambda *_: (0,) * rank)


def shifted(value, axis, step):
    size = lax.axis_size(axis)
    return lax.ppermute(value, axis, [(i, (i + step) % size) for i in range(size)])


def exchange(value, axis, split=0):
    return lax.all_to_all(value, axis, split, 0, tiled=True)


def ring_first(value):
    return shifted(value, "pop", 1), shifted(value, "pop", 3)


def ring_second(below, above):
    return shifted(below, "pop", 1), shifted(above, "pop", 3)


def together(*values):
    return lax.optimization_barrier(values)


def silu(value):
    half = 0.5 * value
    return half + half * jnp.tanh(half)


def cut_kernel(pop, down, out, sems):
    parts, _, lanes = out.shape
    pops = down.shape[1] // parts // lanes
    copies = [
        pltpu.make_async_copy(
            down.at[:, pl.ds(pl.multiple_of((i * pops + pop[0]) * lanes, lanes), lanes)],
            out.at[i],
            sems.at[i],
        )
        for i in range(parts)
    ]
    for copy in copies:
        copy.start()
    for copy in copies:
        copy.wait()


def cut_weight(pop, down, parts, pops):
    shape = (parts, down.shape[0], down.shape[1] // parts // pops)
    return pl.pallas_call(
        cut_kernel,
        grid_spec=pltpu.PrefetchScalarGridSpec(
            num_scalar_prefetch=1,
            grid=(1,),
            in_specs=[pl.BlockSpec(memory_space=pl.ANY)],
            out_specs=pl.BlockSpec(shape, lambda i, p: (0, 0, 0)),
            scratch_shapes=[pltpu.SemaphoreType.DMA((parts,))],
        ),
        out_shape=jax.ShapeDtypeStruct(shape, BF),
        compiler_params=params(),
        cost_estimate=cost(1 << 20, 1 << 20),
    )(pop, down)


def table_kernel(col, table, up_t, left, sent, columns):
    @pl.when(pl.program_id(0) == 0)
    def _():
        columns[...] = jnp.zeros_like(columns)
        columns[:, 0 : table.shape[0]] = table[...].astype(F32).T.astype(BF)

    codes = columns[...]
    product = jnp.dot(up_t[0], codes, preferred_element_type=F32)
    probe = jnp.dot(left[...], codes, preferred_element_type=F32)
    spare = sent.shape[2] - product.shape[0] - probe.shape[0]
    both = jnp.concatenate([product, probe, jnp.zeros((spare, codes.shape[1]), F32)], axis=0)
    sent[0] = both.T[0:CODES].astype(BF)


def table_products(col, table, up_t, left):
    vocab = table.shape[0]
    parts, share, width = up_t.shape
    slots = left.shape[0] // parts
    lanes = pl.cdiv(share + slots, 128) * 128
    return pl.pallas_call(
        table_kernel,
        grid_spec=pltpu.PrefetchScalarGridSpec(
            num_scalar_prefetch=1,
            grid=(parts,),
            in_specs=[
                pl.BlockSpec((vocab, width), lambda i, c: (0, c[0])),
                pl.BlockSpec((1, share, width), lambda i, c: (i, 0, 0)),
                pl.BlockSpec((slots, width), lambda i, c: (i, 0)),
            ],
            out_specs=pl.BlockSpec((1, CODES, lanes), lambda i, c: (i, 0, 0)),
            scratch_shapes=[pltpu.VMEM((width, 256), BF)],
        ),
        out_shape=jax.ShapeDtypeStruct((parts, CODES, lanes), BF),
        compiler_params=params(),
        cost_estimate=cost(1 << 20, 1 << 20),
    )(col, table, up_t, left)


def hidden_kernel(
    pop, codes, shares, right, own_share, own_right, own_left, w0, w1, w2, w3, w4,
    out, rhs, own, hid, weight, sems,
):
    parts, _, lanes = shares.shape
    ff = right.shape[1]
    share = own_right.shape[1]
    slots = right.shape[0]
    rows = codes.shape[2]
    depth = rhs.shape[0]
    per_slot = rows // slots
    width = w0.shape[1]
    step = pl.program_id(0)
    half = w3.shape[0]
    copies = [
        pltpu.make_async_copy(part, weight.at[:, pl.ds(i * width, width)], sems.at[i])
        for i, part in enumerate((w0, w1, w2))
    ] + [
        pltpu.make_async_copy(
            part, weight.at[pl.ds(i * half, half), pl.ds(3 * width, width)], sems.at[3 + i]
        )
        for i, part in enumerate((w3, w4))
    ]

    @pl.when(step == 0)
    def _():
        for copy in copies:
            copy.start()
        rhs[...] = jnp.zeros_like(rhs)
        for part in range(parts):
            rhs[pl.ds(0, CODES), part * share : (part + 1) * share] = shares[part, :, 0:share]
        own[...] = jnp.zeros_like(own)
        own[pl.ds(0, CODES), :] = own_share[:, 0:share]

    first = CODES
    second = CODES + slots
    for start in (first, second):
        rhs[pl.ds(start, slots), :] = right[...]
        own[pl.ds(start, slots), :] = own_right[...]

    pairs = 2
    per_part = slots // pairs
    tile = lanes - 128
    source = lax.broadcasted_iota(jnp.int32, (128, depth), 0) - (share - tile)
    target = lax.broadcasted_iota(jnp.int32, (128, depth), 1)
    place = None
    for pair in range(pairs):
        at = (target == source + first + pair * per_part) | (
            target == source + second + pair * per_part
        )
        at = at & (source >= 0) & (source < per_part)
        term = jnp.dot(
            shares[step * pairs + pair, :, tile:lanes],
            jnp.where(at, 1.0, 0.0).astype(BF),
            preferred_element_type=F32,
        )
        place = term if place is None else place + term
    line = lax.broadcasted_iota(jnp.int32, (depth, rows), 0)
    slot = lax.broadcasted_iota(jnp.int32, (depth, rows), 1) // per_slot
    hot = jnp.where(line == codes[0], 1.0, 0.0)
    hot_b = hot.astype(BF)
    probe = noise_scale * lax.dot_general(
        place.astype(BF), hot_b[0:CODES, :], TN, preferred_element_type=F32
    )
    high = probe.astype(BF).astype(F32)
    lhs = jnp.where(line - first == slot, high, hot)
    lhs = jnp.where(line - second == slot, probe - high, lhs)
    lhs = lhs.T.astype(BF)

    pre = jnp.dot(lhs, own[...], preferred_element_type=F32)
    mine = silu(pre).astype(BF)
    probes = lax.dot_general(own_left[...], mine, NT, preferred_element_type=F32)
    row_slot = lax.broadcasted_iota(jnp.int32, (slots, rows), 1) // per_slot
    which = lax.broadcasted_iota(jnp.int32, (slots, rows), 0)
    probe_row = jnp.sum(jnp.where(which == row_slot, probes, 0.0), axis=0, keepdims=True)
    probe_high = probe_row.astype(BF).astype(F32)
    index = lax.broadcasted_iota(jnp.int32, (TAIL, rows), 0)
    tail = jnp.where(index == 0, probe_high, jnp.where(index == 1, probe_row - probe_high, 0.0))
    out[0, pl.ds(rows, TAIL), :] = tail.astype(BF)

    for start in range(0, ff, 256):
        size = min(256, ff - start)
        pre = jnp.dot(lhs, rhs[:, start : start + size], preferred_element_type=F32)
        hid[:, start : start + size] = silu(pre).astype(BF)

    @pl.when(step == 0)
    def _():
        for copy in copies:
            copy.wait()

    product = jnp.dot(hid[...], weight[...], preferred_element_type=F32).astype(BF)
    for i, source in enumerate(slot_order(pop[0])):
        at = pl.multiple_of(source * width, width)
        out[0, pl.ds(0, rows), pl.ds(at, width)] = product[:, i * width : (i + 1) * width]


def hidden_product(pop, codes, shares, right, own_share, own_right, own_left, weights):
    steps, _, rows = codes.shape
    ff = right.shape[1]
    share = own_right.shape[1]
    slots = right.shape[0] // steps
    width = 4 * weights[0].shape[1]
    assert width == rows
    return pl.pallas_call(
        hidden_kernel,
        grid_spec=pltpu.PrefetchScalarGridSpec(
            num_scalar_prefetch=1,
            grid=(steps,),
            in_specs=[
                pl.BlockSpec((1, 1, rows), lambda i, p: (i, 0, 0)),
                whole(shares),
                pl.BlockSpec((slots, ff), lambda i, p: (i, 0)),
                whole(own_share),
                pl.BlockSpec((slots, share), lambda i, p: (i, 0)),
                pl.BlockSpec((slots, share), lambda i, p: (i, 0)),
            ]
            + [pl.BlockSpec(memory_space=pl.ANY)] * 5,
            out_specs=pl.BlockSpec((1, rows + TAIL, width), lambda i, p: (i, 0, 0)),
            scratch_shapes=[
                pltpu.VMEM((256, ff), BF),
                pltpu.VMEM((256, share), BF),
                pltpu.VMEM((rows, ff), BF),
                pltpu.VMEM((ff, width), BF),
                pltpu.SemaphoreType.DMA((5,)),
            ],
        ),
        out_shape=jax.ShapeDtypeStruct((steps, rows + TAIL, width), BF),
        compiler_params=params(),
        cost_estimate=cost(2 * steps * rows * ff * (256 + width), 8 << 20),
    )(pop, codes, shares, right, own_share, own_right, own_left, *weights)


def pieces_kernel(mine, theirs, out):
    parts, piece, _ = out.shape
    rows = piece - TAIL
    total = mine[0].astype(F32) + theirs[0].astype(F32)
    top = total.shape[0] - TAIL
    probe = total[top : top + 1, :] + total[top + 1 : top + 2, :]
    high = probe.astype(BF).astype(F32)
    index = lax.broadcasted_iota(jnp.int32, (TAIL, total.shape[1]), 0)
    tail = jnp.where(index == 0, high, jnp.where(index == 1, probe - high, 0.0)).astype(BF)
    for part in range(parts):
        out[part, pl.ds(0, rows), :] = total[part * rows : (part + 1) * rows, :].astype(BF)
        out[part, pl.ds(rows, TAIL), :] = tail


def pieces(mine, theirs, parts):
    count, height, width = mine.shape
    rows = (height - TAIL) // parts
    spec = pl.BlockSpec((1, height, width), lambda i: (i, 0, 0))
    return pl.pallas_call(
        pieces_kernel,
        grid=(count,),
        in_specs=[spec, spec],
        out_specs=pl.BlockSpec((parts, rows + TAIL, width), lambda i: (i, 0, 0)),
        out_shape=jax.ShapeDtypeStruct((count * parts, rows + TAIL, width), BF),
        compiler_params=params(),
        cost_estimate=cost(1 << 20, 4 << 20),
    )(mine, theirs)


def final_kernel(col, got, tails, codes, table, right, out):
    rows = out.shape[0]
    parts = got.shape[0]
    product = got[0, 0, 0:rows, :].astype(F32)
    for part in range(1, parts):
        product = product + got[part, 0, 0:rows, :].astype(F32)
    probe = jnp.sum(tails[...].astype(F32), axis=(0, 1))
    probe = jnp.sum(probe, axis=0, keepdims=True)
    lane = lax.broadcasted_iota(jnp.int32, (rows, probe.shape[1]), 1)
    line = lax.broadcasted_iota(jnp.int32, (rows, probe.shape[1]), 0)
    own = jnp.sum(
        jnp.where(lane == line + col[0] * rows, probe, 0.0), axis=1, keepdims=True
    )
    slots = right.shape[0]
    per_slot = rows // slots
    spread = jnp.concatenate(
        [
            jnp.broadcast_to(right[i : i + 1, :].astype(F32), (per_slot, right.shape[1]))
            for i in range(slots)
        ],
        axis=0,
    )
    hot = lax.broadcasted_iota(jnp.int32, (rows, table.shape[0]), 1) == codes[...]
    residual = jnp.dot(
        jnp.where(hot, 1.0, 0.0).astype(BF), table[...], preferred_element_type=F32
    )
    out[...] = (residual + product + (noise_scale * own) * spread).astype(BF)


def final_sum(col, got, codes, table, right):
    halves, parts, height, width = got.shape
    rows = height - TAIL
    return pl.pallas_call(
        final_kernel,
        grid_spec=pltpu.PrefetchScalarGridSpec(
            num_scalar_prefetch=1,
            grid=(parts,),
            in_specs=[
                pl.BlockSpec((halves, 1, height, width), lambda i, c: (0, i, 0, 0)),
                pl.BlockSpec(
                    (halves, parts, TAIL, width), lambda i, c: (0, 0, rows // TAIL, 0)
                ),
                whole(codes),
                pl.BlockSpec((table.shape[0], width), lambda i, c: (0, i)),
                pl.BlockSpec((right.shape[0], width), lambda i, c: (0, i)),
            ],
            out_specs=pl.BlockSpec((rows, width), lambda i, c: (0, i)),
        ),
        out_shape=jax.ShapeDtypeStruct((rows, parts * width), BF),
        compiler_params=params(),
        cost_estimate=cost(1 << 20, 4 << 20),
    )(col, got, got, codes, table, right)


def slot_order(pop):
    return [lax.rem(pop + step, 4) for step in (0, 3, 1, 2)]


def moments(grad, moment, second):
    first = beta_first * moment + (1.0 - beta_first) * grad
    sec = beta_second * second + (1.0 - beta_second) * grad * grad
    return first, sec, first / (jnp.sqrt(sec) + adam_eps)


def up_kernel(left, w0, w1, w2, wa, wb, moment, second, first_new, second_new, step):
    tail = jnp.where(pl.program_id(0) < pl.num_programs(0) // 2, wa[...], wb[...])
    weighted = jnp.concatenate([w0[...], w1[...], w2[...], tail], axis=1)
    grad = jnp.dot(weighted, left[...], preferred_element_type=F32)
    first, sec, direction = moments(grad, moment[...], second[...])
    first_new[...] = first
    second_new[...] = sec
    step[...] = direction


def up_adam(left, weighted, moment, second, tile):
    rows, columns = moment.shape
    slots = left.shape[0] // 4
    half = rows // tile // 2
    assert rows == 2 * half * tile
    state = pl.BlockSpec((tile, columns), lambda j: (j, 0))
    return pl.pallas_call(
        up_kernel,
        grid=(rows // tile,),
        in_specs=[whole(left)]
        + [pl.BlockSpec((tile, slots), lambda j: (j, 0))] * 3
        + [
            pl.BlockSpec((tile, slots), lambda j: (jnp.minimum(j, half - 1), 0)),
            pl.BlockSpec((tile, slots), lambda j: (jnp.maximum(j - half, 0), 0)),
        ]
        + [state] * 2,
        out_specs=[state] * 3,
        out_shape=[jax.ShapeDtypeStruct(moment.shape, F32)] * 3,
        compiler_params=params(),
        cost_estimate=cost(1 << 20, 8 << 20),
    )(left, *weighted, moment, second)


def down_kernel(
    core, left, own, a, b, c, d, e, f, g, h,
    moment, second, first_new, second_new, step, grad, factor, sems,
):
    lines = grad.shape[1] // 128
    rows = moment.shape[0] // lines
    count = left.shape[1]
    slots = own.shape[0]
    half = slots // 2
    quarter = half // 2

    @pl.when(pl.program_id(0) == 0)
    def _():
        copies = [pltpu.make_async_copy(own, factor.at[pl.ds(0, slots)], sems.at[0])]
        for place, parts in ((core[0], (a, b, c, d)), (1 - core[0], (e, f, g, h))):
            at = pl.multiple_of(place * half, half)
            starts = (slots, 2 * slots, 3 * slots, 3 * slots + quarter)
            for start, part in zip(starts, parts):
                copies.append(
                    pltpu.make_async_copy(
                        part, factor.at[pl.ds(at + start, part.shape[0])], sems.at[len(copies)]
                    )
                )
        for copy in copies:
            copy.start()
        for copy in copies:
            copy.wait()
        grad[0:count, :] = lax.dot_general(
            left[...], factor[...], TN, preferred_element_type=F32
        )

    start = pl.program_id(0) * rows
    for block in range(rows // 8):
        for line in range(lines):
            where = pl.ds(block * 8 * lines + line, 8, stride=lines)
            first, sec, direction = moments(
                grad[pl.ds(pl.multiple_of(start + block * 8, 8), 8), line * 128 : (line + 1) * 128],
                moment[where, :],
                second[where, :],
            )
            first_new[where, :] = first
            second_new[where, :] = sec
            step[where, :] = direction


def down_adam(core, left, own, parts, moment, second, rows):
    slots, width = own.shape
    lines = width // 128
    steps = pl.cdiv(moment.shape[0] // lines, rows)
    state = pl.BlockSpec((rows * lines, 128), lambda j, p: (j, 0))
    return pl.pallas_call(
        down_kernel,
        grid_spec=pltpu.PrefetchScalarGridSpec(
            num_scalar_prefetch=1,
            grid=(steps,),
            in_specs=[whole(left)] + [pl.BlockSpec(memory_space=pl.ANY)] * 9 + [state] * 2,
            out_specs=[state] * 3,
            scratch_shapes=[
                pltpu.VMEM((rows * steps, width), F32),
                pltpu.VMEM((4 * slots, width), BF),
                pltpu.SemaphoreType.DMA((9,)),
            ],
        ),
        out_shape=[jax.ShapeDtypeStruct(moment.shape, F32)] * 3,
        compiler_params=params(),
        cost_estimate=cost(1 << 20, 8 << 20),
    )(core, left, own, *parts, moment, second)


def per_device(
    obs_ids,
    member_ids,
    fitness,
    embed_table,
    up_weight,
    down_weight,
    up_left,
    up_right,
    down_left,
    down_right,
    up_moment,
    up_second,
    down_moment,
    down_second,
):
    member_count, per_member = obs_ids.shape
    row_count = member_count * per_member
    model = embed_table.shape[1]
    feat_width, ff_quarter = up_weight.shape
    ff_share = down_weight.shape[0]
    cols = lax.axis_size("col")
    pops = lax.axis_size("pop")
    col_index = lax.axis_index("col")
    col_ref = col_index.reshape(1)
    pop_ref = lax.axis_index("pop").reshape(1)
    codes = obs_ids.reshape(row_count, 1)

    members_all = fitness.shape[0]
    fit_mean = jnp.mean(fitness)
    fit_var = jnp.mean((fitness - fit_mean) * (fitness - fit_mean))
    slot_fit = jnp.sum(
        jnp.where(member_ids[:, None] == jnp.arange(members_all)[None, :], fitness[None, :], 0.0),
        axis=1,
    )
    fit_scale = (
        (slot_fit - fit_mean) / jnp.sqrt(fit_var + fitness_eps) / (members_all * noise_scale)
    )
    up_weighted = (fit_scale[None, :] * up_right.T.astype(F32)).astype(BF)
    down_weighted = (fit_scale[:, None] * down_right.astype(F32)).astype(BF)
    up_rows = feat_width // pops
    down_rows = ff_share // pops
    lefts = jnp.concatenate(
        [
            up_left.reshape(member_count, pops, up_rows).transpose(1, 0, 2),
            jnp.pad(
                down_left.reshape(member_count, pops, down_rows).transpose(1, 0, 2),
                ((0, 0), (0, 0), (0, up_rows - down_rows)),
            ),
        ],
        axis=1,
    )
    core = lax.axis_index("core")
    pop_index = lax.axis_index("pop")

    cut = exchange(cut_weight(pop_ref, down_weight, cols, pops), "col")
    sent = table_products(
        col_ref, embed_table, up_weight.T.reshape(cols, ff_share, feat_width), up_left
    )
    half = member_count // 2
    down_own = lax.dynamic_slice_in_dim(down_weighted, core * half, half, 0)
    down_first = ring_first(down_own)
    cut, sent, *down_first = together(cut, sent, *down_first)

    got = exchange(sent, "col")
    weight = cut.reshape(ff_quarter, -1)
    weight_first = ring_first(weight)
    got, *weight_first = together(got, *weight_first)
    share = jnp.sum(got.astype(F32), axis=0).astype(BF)

    shares = exchange(jnp.broadcast_to(share[None], (cols,) + share.shape), "col")
    weight_second = ring_second(
        weight_first[0][: ff_quarter // 2], weight_first[1][ff_quarter // 2 :]
    )
    down_second_parts = ring_second(down_first[0][: half // 2], down_first[1][half // 2 :])

    def factor(step):
        return lax.dynamic_index_in_dim(lefts, (pop_index + step) % pops, 0, keepdims=False)

    shares, *rest = together(
        shares, *weight_second, *down_second_parts, up_weighted, factor(1), factor(2), factor(3)
    )
    weight_second, rest = rest[:2], rest[2:]
    down_parts = list(down_first) + rest[:2]
    up_weighted, next_factor, far_factor, last_factor = rest[2:]

    up_below = shifted(
        jnp.concatenate([up_weighted, next_factor, far_factor[:member_count]], axis=0), "pop", 1
    )
    up_above = shifted(
        jnp.concatenate([up_weighted, last_factor, far_factor[member_count:]], axis=0), "pop", 3
    )
    own_right = lax.dynamic_slice_in_dim(up_right, col_index * ff_share, ff_share, 1)
    partial = hidden_product(
        pop_ref,
        obs_ids.reshape(row_count // CHUNK, 1, CHUNK),
        shares,
        up_right,
        share,
        own_right,
        down_left,
        (weight, *weight_first, *weight_second),
    )
    partial, up_below, up_above = together(partial, up_below, up_above)
    up_half = ff_quarter // 2
    relay = ff_quarter + 2 * member_count
    far_below, far_above = ring_second(
        jnp.concatenate([up_below[:up_half], up_below[relay:]], axis=0),
        jnp.concatenate([up_above[up_half:ff_quarter], up_above[relay:]], axis=0),
    )
    own_factor = factor(0)

    by_core = partial.reshape((2, 2) + partial.shape[1:])
    mine = lax.dynamic_index_in_dim(by_core, core, 1, keepdims=False)
    other = lax.dynamic_index_in_dim(by_core, 1 - core, 1, keepdims=False)
    theirs = shifted(other, "core", 1)
    cut = exchange(pieces(mine, theirs, cols), ("xh", "col"))
    cut = cut.reshape((2, cols) + cut.shape[1:])
    share_rows = row_count // (4 * cols)
    share_slots = share_rows // per_member
    place_index = lax.axis_index(ROW + ("col",))
    mine_codes = lax.dynamic_slice_in_dim(codes, place_index * share_rows, share_rows, 0)
    mine_right = lax.dynamic_slice_in_dim(down_right, place_index * share_slots, share_slots, 0)
    block_out = final_sum(col_ref, cut, mine_codes, embed_table, mine_right)

    down_theirs = [shifted(part, "core", 1) for part in down_parts]
    near = slice(ff_quarter, ff_quarter + member_count)
    more = slice(ff_quarter + member_count, relay)
    up_out = up_adam(
        jnp.concatenate(
            [own_factor[:member_count], up_below[near], up_above[near], far_below[up_half:]], axis=0
        ),
        (up_weighted, up_below, up_above, far_below, far_above),
        up_moment.reshape(up_rows, ff_quarter).T,
        up_second.reshape(up_rows, ff_quarter).T,
        688,
    )
    down_left_all = jnp.concatenate(
        [own_factor[member_count:], up_below[more], up_above[more], far_above[up_half:]], axis=0
    )
    down_out = down_adam(
        core.reshape(1),
        down_left_all[:, :down_rows],
        down_weighted,
        (*down_parts, *down_theirs),
        down_moment.reshape(-1, 128),
        down_second.reshape(-1, 128),
        24,
    )
    up_out = [value.T.reshape(up_moment.shape) for value in up_out]
    down_out = [value.reshape(down_moment.shape) for value in down_out]
    return (block_out, *up_out, *down_out)


def solution(mesh):
    devices = mesh.devices
    pops, rows, cols = devices.shape
    fine = Mesh(devices.reshape(pops, rows // 2, 2, cols), ("pop", "xh", "core", "col"))
    split = ROW + ("col",)
    in_specs = (
        P("pop", None),
        P("pop"),
        P(),
        P(),
        P("col", ROW),
        P(split, None),
        P("pop", "col"),
        P("pop", ROW),
        P("pop", split),
        P("pop", None),
        P("col", "pop", None, ROW),
        P("col", "pop", None, ROW),
        P(split, "pop", None, None),
        P(split, "pop", None, None),
    )
    out_specs = (
        P(("pop",) + split, None),
        P("col", "pop", None, ROW),
        P("col", "pop", None, ROW),
        P("col", "pop", None, ROW),
        P(split, "pop", None, None),
        P(split, "pop", None, None),
        P(split, "pop", None, None),
    )
    return jax.shard_map(
        per_device, mesh=fine, in_specs=in_specs, out_specs=out_specs, check_vma=False
    )
```

time: 645 us -> 156 us (0.24)
  waiting for transfers between devices: 413 us -> 25.6 us
  blocking collectives: 90.5 us -> 0 us
  Pallas kernels: 0 us -> 52.4 us
  matrix products: 47 us -> 0 us
  starting transfers between devices: 1.82 us -> 47.2 us
  local copies, waits for them, and re-layouts: 56.2 us -> 20.9 us
  between operations: 15.9 us -> 2.49 us
  other arithmetic: 19.6 us -> 6.2 us
    reduce_scatter x3 -> x0, waiting for transfers between devices: 412 us -> none  [the longest x1 299 us: per_device(): lax.psum_scatter(output_term(hidden_t, down_weight, probe_two, down_right...]
    unnamed x1 -> x0, blocking collectives: 90.5 us -> none
    pallas_call x0 -> x7, Pallas kernels: none -> 52.4 us  [the longest x1 18 us: hidden_product(): pl.pallas_call(hidden_kernel, grid_spec=pltpu.PrefetchScalarGridSpec(num_...]
    dot_general x8 -> x0, matrix products: 47 us -> none  [the longest x3 25 us: contract_first(): lax.dot_general(left_part, right_part, (((0,), (0,)), ((), ())), preferre...]
    mul x4 -> x0, local copies, waits for them, and re-layouts: 34.2 us -> none  [the longest x3 34.1 us: per_device(): right_cols.T[:, :, None] * probe_one[None, :, :]]
    ppermute x0 -> x17, waiting for transfers between devices: none -> 25.6 us  [shifted(): lax.ppermute(value, axis, [(i, (i + step) % size) for i in range(size)])]
    ppermute x0 -> x17, starting transfers between devices: none -> 24.7 us  [shifted(): lax.ppermute(value, axis, [(i, (i + step) % size) for i in range(size)])]
    all_to_all x0 -> x4, starting transfers between devices: none -> 22.4 us  [exchange(): return lax.all_to_all(value, axis, split, 0, tiled=True)]
  transfers between devices with their start and end apart: 4 -> 21, of which waited for: 3 -> 6; matrix products, arithmetic and copies ran while one was open for 23% -> 12% of each run, Pallas kernels for 0% -> 28%
where the time goes in v2:
time: 156 us; the launch traced here: 155 us
  Pallas kernels  52.4 us (34%)
  starting transfers between devices  47.2 us (30%)
  waiting for transfers between devices  25.6 us (16%)
  local copies, waits for them, and re-layouts  20.9 us (13%)
  other arithmetic  6.2 us (4%)
  between operations  2.49 us (2%)
    ppermute x17, waiting for transfers between devices, shifted(): lax.ppermute(value, axis, [(i, (i + step) % size) for i in range(size)])  25.6 us
    ppermute x17, starting transfers between devices, shifted(): lax.ppermute(value, axis, [(i, (i + step) % size) for i in range(size)])  24.7 us
    all_to_all x4, starting transfers between devices, exchange(): return lax.all_to_all(value, axis, split, 0, tiled=True)  22.4 us
    pallas_call x1, Pallas kernels, hidden_product(): pl.pallas_call(hidden_kernel, grid_spec=pltpu.PrefetchScalarGridSpec(num_...  18 us
    pallas_call x1, Pallas kernels, down_adam(): pl.pallas_call(down_kernel, grid_spec=pltpu.PrefetchScalarGridSpec(num_sc...  10.3 us
    pallas_call x1, Pallas kernels, table_products(): pl.pallas_call(table_kernel, grid_spec=pltpu.PrefetchScalarGridSpec(num_s...  7.23 us
    pallas_call x1, Pallas kernels, final_sum(): pl.pallas_call(final_kernel, grid_spec=pltpu.PrefetchScalarGridSpec(num_s...  6.43 us
    pallas_call x1, Pallas kernels, up_adam(): pl.pallas_call(up_kernel, grid=(rows // tile,), in_specs=[whole(left)] +...  5.77 us
  transfers between devices with their start and end apart: 21, of which 6 were waited for; matrix products, arithmetic and copies ran while one was open for 12% of the time, Pallas kernels for 28%

profile of v2, /device:TPU:1, one launch (start us, length us, event | category | flops | bytes accessed | tf_op | source)
XLA Modules:
  0.0 154.8 jit_solution(17827520733455421791)
XLA Ops:
  0.6 2.1 %shard_map.189 = bf16[8,344,128]{2,1,0:T(8,128)(2,1)} custom-call(s32[1]{0:T(128)} %bitcast.1.pop, bf16[344,4096]{1,0:T(8,128)(2,1)} %down.1), custom_call_target="tpu_custom_call" | custom-call | flops 1048576 | bytes 1048576 | tf_op jit(solution)/shard_map/pallas_call | solution.py:84
  2.8 6.1 %all-to-all-start = ((bf16[8,344,128]{2,1,0:T(8,128)(2,1)}), bf16[8,344,128]{2,1,0:T(8,128)(2,1)}, u32[]{:S(2)}, u32[]{:S(2)}) async-start(bf16[8,344,128]{2,1,0:T(8,128)(2,1)} %shard_map.189), calls=%async_computation | async-start | bytes 1409024 | tf_op jit(solution)/shard_map/all_to_all | solution.py:45
  13.7 2.2 %collective-permute-start.1 = (bf16[64,4096]{1,0:T(8,128)(2,1)S(1)}, bf16[64,4096]{1,0:T(8,128)(2,1)}, u32[]{:S(2)}, u32[]{:S(2)}) collective-permute-start(bf16[64,4096]{1,0:T(8,128)(2,1)S(1)} %constant_dynamic-slice_fusion.3), channel_id=1, source_target_pairs={{0,96},{32,0},{64,32},{96,64},{1,97},{33,1},{65,33},{97,65},{2,98}... | collective-permute-start | bytes 1572872 | tf_op jit(solution)/shard_map/ppermute | solution.py:41
  15.9 7.2 %shard_map.190 = bf16[8,160,384]{2,1,0:T(8,128)(2,1)} custom-call(s32[1]{0:T(128)} %bitcast.col, bf16[156,4096]{1,0:T(8,128)(2,1)} %table.3, bf16[8,344,512]{2,1,0:T(8,128)(2,1)} %bitcast.56, bf16[128,512]{1,0:T(8,128)(2,1)} %left.1), custom_call_target="tpu_custom_call" | custom-call | flops 1048576 | bytes 1048576 | tf_op jit(solution)/shard_map/pallas_call | solution.py:118
  23.1 4.0 %collective-permute-done.a = bf16[64,4096]{1,0:T(8,128)(2,1)S(1)} collective-permute-done((bf16[64,4096]{1,0:T(8,128)(2,1)S(1)}, bf16[64,4096]{1,0:T(8,128)(2,1)S(1)}, u32[]{:S(2)}, u32[]{:S(2)}) %collective-permute-start) | collective-permute-done | bytes 524320 | tf_op jit(solution)/shard_map/ppermute | solution.py:41
  27.2 4.8 %all-to-all-start.1 = ((bf16[8,160,384]{2,1,0:T(8,128)(2,1)}), bf16[8,160,384]{2,1,0:T(8,128)(2,1)S(1)}, u32[]{:S(2)}, u32[]{:S(2)}) async-start(bf16[8,160,384]{2,1,0:T(8,128)(2,1)} %shard_map.190), calls=%async_computation.1 | async-start | bytes 1966080 | tf_op jit(solution)/shard_map/all_to_all | solution.py:45
  32.5 2.2 %collective-permute-start.3 = (bf16[2752,128]{1,0:T(8,128)(2,1)}, bf16[2752,128]{1,0:T(8,128)(2,1)}, u32[]{:S(2)}, u32[]{:S(2)}) collective-permute-start(bf16[2752,128]{1,0:T(8,128)(2,1)} %bitcast.4.w0), channel_id=1, source_target_pairs={{0,96},{32,0},{64,32},{96,64},{1,97},{33,1},{65,33},{97,65},{2,98}... | collective-permute-start | bytes 2113544 | tf_op jit(solution)/shard_map/ppermute | solution.py:41
  35.8 12.7 %collective-permute-done.2.w1 = bf16[2752,128]{1,0:T(8,128)(2,1)S(1)} collective-permute-done((bf16[2752,128]{1,0:T(8,128)(2,1)}, bf16[2752,128]{1,0:T(8,128)(2,1)S(1)}, u32[]{:S(2)}, u32[]{:S(2)}) %collective-permute-start.2) | collective-permute-done | bytes 704544 | tf_op jit(solution)/shard_map/ppermute | solution.py:41
  49.8 4.9 %all-to-all-start.2 = ((bf16[8,160,384]{2,1,0:T(8,128)(2,1)}), bf16[8,160,384]{2,1,0:T(8,128)(2,1)S(1)}, u32[]{:S(2)}, u32[]{:S(2)}) async-start(bf16[8,160,384]{2,1,0:T(8,128)(2,1)} %broadcast_in_dim.16), calls=%async_computation.2 | async-start | bytes 1966080 | tf_op jit(solution)/shard_map/all_to_all | solution.py:45
  57.4 2.6 %collective-permute-start.7 = (bf16[32,4096]{1,0:T(8,128)(2,1)}, bf16[32,4096]{1,0:T(8,128)(2,1)}, u32[]{:S(2)}, u32[]{:S(2)}) collective-permute-start(bf16[32,4096]{1,0:T(8,128)(2,1)} %slice.66), channel_id=1, source_target_pairs={{0,96},{32,0},{64,32},{96,64},{1,97},{33,1},{65,33},{97,65},{2,98}... | collective-permute-start | bytes 786440 | tf_op jit(solution)/shard_map/ppermute | solution.py:41
  60.0 1.7 %slice.64 = bf16[1376,128]{1,0:T(8,128)(2,1)} slice(bf16[2752,128]{1,0:T(8,128)(2,1)} %collective-permute-done.3.w2), slice={[1376:2752], [0:128]} | slice | bytes 704512 | tf_op jit(solution)/shard_map/slice | solution.py:536
  61.8 2.7 %collective-permute-start.5 = (bf16[1376,128]{1,0:T(8,128)(2,1)}, bf16[1376,128]{1,0:T(8,128)(2,1)}, u32[]{:S(2)}, u32[]{:S(2)}) collective-permute-start(bf16[1376,128]{1,0:T(8,128)(2,1)} %slice.64), channel_id=1, source_target_pairs={{0,96},{32,0},{64,32},{96,64},{1,97},{33,1},{65,33},{97,65},{2,98}... | collective-permute-start | bytes 1056776 | tf_op jit(solution)/shard_map/ppermute | solution.py:41
  68.2 3.3 %collective-permute-done.4.w3 = bf16[1376,128]{1,0:T(8,128)(2,1)} collective-permute-done((bf16[1376,128]{1,0:T(8,128)(2,1)S(1)}, bf16[1376,128]{1,0:T(8,128)(2,1)}, u32[]{:S(2)}, u32[]{:S(2)}) %collective-permute-start.4) | collective-permute-done | bytes 352288 | tf_op jit(solution)/shard_map/ppermute | solution.py:41
  74.3 3.4 %collective-permute-start.9 = (bf16[3136,128]{1,0:T(8,128)(2,1)}, bf16[3136,128]{1,0:T(8,128)(2,1)S(1)}, u32[]{:S(2)}, u32[]{:S(2)}) collective-permute-start(bf16[3136,128]{1,0:T(8,128)(2,1)} %get-tuple-element.86), channel_id=1, source_target_pairs={{0,96},{32,0},{64,32},{96,64},{1,97},{33,1},{65,33},{97,65},{2,98}... | collective-permute-start | bytes 2408456 | tf_op jit(solution)/shard_map/ppermute | solution.py:41
  77.7 18.0 %shard_map.191 = bf16[4,528,512]{2,1,0:T(8,128)(2,1)} custom-call(s32[1]{0:T(128)} %bitcast.1.pop, s32[4,1,512]{2,1,0:T(1,128)} %reshape.113.codes, bf16[8,160,384]{2,1,0:T(8,128)(2,1)} %copy-done.9, bf16[128,2752]{1,0:T(8,128)(2,1)} %copy.52.right, bf16[160,384]{1,0:T(8,128)(2,1)} %copy-done.11, bf16[128,344]{1,0:T(8,128)(2,1)} %constant_dynamic-slice_fusion.2.own_right, ...), custom_call_target="tpu_custom_call" | custom-call | flops 8657043456 | bytes 8388608 | tf_op jit(solution)/shard_map/pallas_call | solution.py:240
  95.7 3.3 %dynamic-slice_bitcast_fusion = (bf16[2,528,512]{2,1,0:T(8,128)(2,1)S(1)}, bf16[2,528,512]{2,1,0:T(8,128)(2,1)}) fusion(bf16[2,2,528,512]{3,2,1,0:T(8,128)(2,1)} %bitcast.57, s32[]{:T(128)S(6)} %select_n.65, s32[]{:T(128)S(6)} %select_n.64), kind=kLoop, calls=%fused_computation.2 | loop fusion | bytes 4325384 | tf_op jit(solution)/shard_map/jit(dynamic_index_in_dim)/squeeze | solution.py:578
  99.0 3.4 %collective-permute-start.10 = (bf16[2,528,512]{2,1,0:T(8,128)(2,1)S(1)}, bf16[2,528,512]{2,1,0:T(8,128)(2,1)}, u32[]{:S(2)}, u32[]{:S(2)}) collective-permute-start(bf16[2,528,512]{2,1,0:T(8,128)(2,1)S(1)} %get-tuple-element.78), channel_id=1, source_target_pairs={{0,8},{8,0},{1,9},{9,1},{2,10},{10,2},{3,11},{11,3},{4,12},{12,4},... | collective-permute-start | bytes 3244040 | tf_op jit(solution)/shard_map/ppermute | solution.py:41
  104.9 2.5 %shard_map.192 = bf16[16,80,512]{2,1,0:T(8,128)(2,1)} custom-call(bf16[2,528,512]{2,1,0:T(8,128)(2,1)} %get-tuple-element.79.mine, bf16[2,528,512]{2,1,0:T(8,128)(2,1)} %collective-permute-done.10.theirs), custom_call_target="tpu_custom_call" | custom-call | flops 1048576 | bytes 4194304 | tf_op jit(solution)/shard_map/pallas_call | solution.py:287
  107.4 6.6 %all-to-all-start.3 = ((bf16[16,80,512]{2,1,0:T(8,128)(2,1)}), bf16[16,80,512]{2,1,0:T(8,128)(2,1)S(1)}, u32[]{:S(2)}, u32[]{:S(2)}) async-start(bf16[16,80,512]{2,1,0:T(8,128)(2,1)} %shard_map.192), calls=%async_computation.3 | async-start | bytes 2621440 | tf_op jit(solution)/shard_map/all_to_all | solution.py:45
  115.6 2.7 %collective-permute-start.12 = (bf16[1504,128]{1,0:T(8,128)(2,1)}, bf16[1504,128]{1,0:T(8,128)(2,1)}, u32[]{:S(2)}, u32[]{:S(2)}) collective-permute-start(bf16[1504,128]{1,0:T(8,128)(2,1)} %pad_maximum_fusion.3), channel_id=1, source_target_pairs={{0,96},{32,0},{64,32},{96,64},{1,97},{33,1},{65,33},{97,65},{2,98}... | collective-permute-start | bytes 1155080 | tf_op jit(solution)/shard_map/ppermute | solution.py:41
  122.3 3.8 %collective-permute-done.11.wa = bf16[1504,128]{1,0:T(8,128)(2,1)S(1)} collective-permute-done((bf16[1504,128]{1,0:T(8,128)(2,1)}, bf16[1504,128]{1,0:T(8,128)(2,1)S(1)}, u32[]{:S(2)}, u32[]{:S(2)}) %collective-permute-start.11) | collective-permute-done | bytes 385056 | tf_op jit(solution)/shard_map/ppermute | solution.py:41
  129.6 5.8 %shard_map.194 = (f32[2752,128]{1,0:T(8,128)}, f32[2752,128]{1,0:T(8,128)}, f32[2752,128]{1,0:T(8,128)}) custom-call(bf16[512,128]{1,0:T(8,128)(2,1)} %pad_maximum_fusion.7.left, bf16[2752,128]{1,0:T(8,128)(2,1)} %copy-done.2, bf16[3136,128]{1,0:T(8,128)(2,1)} %copy-done.4, bf16[3136,128]{1,0:T(8,128)(2,1)} %copy-done.5, bf16[1504,128]{1,0:T(8,128)(2,1)} %copy-done.12, ...), custom_call_target="tpu_custom_call" | custom-call | flops 1048576 | bytes 8388608 | tf_op jit(solution)/shard_map/pallas_call | solution.py:378
  136.9 10.3 %shard_map.195 = (f32[2752,128]{1,0:T(8,128)}, f32[2752,128]{1,0:T(8,128)}, f32[2752,128]{1,0:T(8,128)}) custom-call(s32[1]{0:T(128)} %bitcast.27.core, bf16[512,86]{1,0:T(8,128)(2,1)} %pad_maximum_fusion.4.left, bf16[128,4096]{1,0:T(8,128)(2,1)} %copy-done.1, bf16[64,4096]{1,0:T(8,128)(2,1)} %copy-done.6, bf16[64,4096]{1,0:T(8,128)(2,1)} %collective-permute-done.1.b, ...), custom_call_target="tpu_custom_call" | custom-call | flops 1048576 | bytes 8388608 | tf_op jit(solution)/shard_map/pallas_call | solution.py:445
  148.4 6.4 %shard_map.193 = bf16[64,4096]{1,0:T(8,128)(2,1)} custom-call(s32[1]{0:T(128)} %bitcast.col, bf16[2,8,80,512]{3,2,1,0:T(8,128)(2,1)} %bitcast.54, bf16[2,8,80,512]{3,2,1,0:T(8,128)(2,1)} %bitcast.55, s32[64,1]{1,0:T(8,128)} %constant_dynamic-slice_fusion.1.codes, bf16[156,4096]{1,0:T(8,128)(2,1)} %table.3, bf16[4,4096]{1,0:T(4,128)(2,1)} %constant_dynamic-slice_fusion.right), custom_call_target="tpu_custom_call" | custom-call | flops 1048576 | bytes 4194304 | tf_op jit(solution)/shard_map/pallas_call | solution.py:330
  (114 shorter events, 29.5 us)
Async XLA Ops:
  2.8 24.4 %all-to-all-start = ((bf16[8,344,128]{2,1,0:T(8,128)(2,1)}), bf16[8,344,128]{2,1,0:T(8,128)(2,1)}, u32[]{:S(2)}, u32[]{:S(2)}) async-start(bf16[8,344,128]{2,1,0:T(8,128)(2,1)} %shard_map.189), calls=%async_computation | async-start | bytes 1409024 | tf_op jit(solution)/shard_map/all_to_all | solution.py:45
  12.0 15.2 %collective-permute-start = (bf16[64,4096]{1,0:T(8,128)(2,1)S(1)}, bf16[64,4096]{1,0:T(8,128)(2,1)S(1)}, u32[]{:S(2)}, u32[]{:S(2)}) collective-permute-start(bf16[64,4096]{1,0:T(8,128)(2,1)S(1)} %constant_dynamic-slice_fusion.3), channel_id=1, source_target_pairs={{0,32},{32,64},{64,96},{96,0},{1,33},{33,65},{65,97},{97,1},{2,34}... | collective-permute-start | bytes 1572872 | tf_op jit(solution)/shard_map/ppermute | solution.py:41
  13.7 13.5 %collective-permute-start.1 = (bf16[64,4096]{1,0:T(8,128)(2,1)S(1)}, bf16[64,4096]{1,0:T(8,128)(2,1)}, u32[]{:S(2)}, u32[]{:S(2)}) collective-permute-start(bf16[64,4096]{1,0:T(8,128)(2,1)S(1)} %constant_dynamic-slice_fusion.3), channel_id=1, source_target_pairs={{0,96},{32,0},{64,32},{96,64},{1,97},{33,1},{65,33},{97,65},{2,98}... | collective-permute-start | bytes 1572872 | tf_op jit(solution)/shard_map/ppermute | solution.py:41
  27.2 75.2 %copy-start.6 = (bf16[64,4096]{1,0:T(8,128)(2,1)}, bf16[64,4096]{1,0:T(8,128)(2,1)S(1)}, u32[]{:S(2)}) copy-start(bf16[64,4096]{1,0:T(8,128)(2,1)S(1)} %collective-permute-done.a) | copy-start | bytes 1572868
  27.2 21.4 %all-to-all-start.1 = ((bf16[8,160,384]{2,1,0:T(8,128)(2,1)}), bf16[8,160,384]{2,1,0:T(8,128)(2,1)S(1)}, u32[]{:S(2)}, u32[]{:S(2)}) async-start(bf16[8,160,384]{2,1,0:T(8,128)(2,1)} %shard_map.190), calls=%async_computation.1 | async-start | bytes 1966080 | tf_op jit(solution)/shard_map/all_to_all | solution.py:45
  32.0 16.6 %collective-permute-start.2 = (bf16[2752,128]{1,0:T(8,128)(2,1)}, bf16[2752,128]{1,0:T(8,128)(2,1)S(1)}, u32[]{:S(2)}, u32[]{:S(2)}) collective-permute-start(bf16[2752,128]{1,0:T(8,128)(2,1)} %bitcast.4.w0), channel_id=1, source_target_pairs={{0,32},{32,64},{64,96},{96,0},{1,33},{33,65},{65,97},{97,1},{2,34}... | collective-permute-start | bytes 2113544 | tf_op jit(solution)/shard_map/ppermute | solution.py:41
  32.5 16.1 %collective-permute-start.3 = (bf16[2752,128]{1,0:T(8,128)(2,1)}, bf16[2752,128]{1,0:T(8,128)(2,1)}, u32[]{:S(2)}, u32[]{:S(2)}) collective-permute-start(bf16[2752,128]{1,0:T(8,128)(2,1)} %bitcast.4.w0), channel_id=1, source_target_pairs={{0,96},{32,0},{64,32},{96,64},{1,97},{33,1},{65,33},{97,65},{2,98}... | collective-permute-start | bytes 2113544 | tf_op jit(solution)/shard_map/ppermute | solution.py:41
  49.8 23.0 %all-to-all-start.2 = ((bf16[8,160,384]{2,1,0:T(8,128)(2,1)}), bf16[8,160,384]{2,1,0:T(8,128)(2,1)S(1)}, u32[]{:S(2)}, u32[]{:S(2)}) async-start(bf16[8,160,384]{2,1,0:T(8,128)(2,1)} %broadcast_in_dim.16), calls=%async_computation.2 | async-start | bytes 1966080 | tf_op jit(solution)/shard_map/all_to_all | solution.py:45
  55.6 12.7 %collective-permute-start.6 = (bf16[32,4096]{1,0:T(8,128)(2,1)}, bf16[32,4096]{1,0:T(8,128)(2,1)}, u32[]{:S(2)}, u32[]{:S(2)}) collective-permute-start(bf16[32,4096]{1,0:T(8,128)(2,1)} %slice.65), channel_id=1, source_target_pairs={{0,32},{32,64},{64,96},{96,0},{1,33},{33,65},{65,97},{97,1},{2,34}... | collective-permute-start | bytes 786440 | tf_op jit(solution)/shard_map/ppermute | solution.py:41
  57.4 10.9 %collective-permute-start.7 = (bf16[32,4096]{1,0:T(8,128)(2,1)}, bf16[32,4096]{1,0:T(8,128)(2,1)}, u32[]{:S(2)}, u32[]{:S(2)}) collective-permute-start(bf16[32,4096]{1,0:T(8,128)(2,1)} %slice.66), channel_id=1, source_target_pairs={{0,96},{32,0},{64,32},{96,64},{1,97},{33,1},{65,33},{97,65},{2,98}... | collective-permute-start | bytes 786440 | tf_op jit(solution)/shard_map/ppermute | solution.py:41
  59.9 11.6 %collective-permute-start.4 = (bf16[1376,128]{1,0:T(8,128)(2,1)S(1)}, bf16[1376,128]{1,0:T(8,128)(2,1)}, u32[]{:S(2)}, u32[]{:S(2)}) collective-permute-start(bf16[1376,128]{1,0:T(8,128)(2,1)S(1)} %slice.63), channel_id=1, source_target_pairs={{0,32},{32,64},{64,96},{96,0},{1,33},{33,65},{65,97},{97,1},{2,34}... | collective-permute-start | bytes 1056776 | tf_op jit(solution)/shard_map/ppermute | solution.py:41
  61.8 11.0 %collective-permute-start.5 = (bf16[1376,128]{1,0:T(8,128)(2,1)}, bf16[1376,128]{1,0:T(8,128)(2,1)}, u32[]{:S(2)}, u32[]{:S(2)}) collective-permute-start(bf16[1376,128]{1,0:T(8,128)(2,1)} %slice.64), channel_id=1, source_target_pairs={{0,96},{32,0},{64,32},{96,64},{1,97},{33,1},{65,33},{97,65},{2,98}... | collective-permute-start | bytes 1056776 | tf_op jit(solution)/shard_map/ppermute | solution.py:41
  68.2 27.5 %copy-start.8 = (bf16[4,256,128]{2,1,0:T(8,128)(2,1)}, bf16[4,256,128]{2,1,0:T(8,128)(2,1)S(1)}, u32[]{:S(2)}) copy-start(bf16[4,256,128]{2,1,0:T(8,128)(2,1)S(1)} %fusion.2) | copy-start | bytes 786436
  74.3 21.4 %collective-permute-start.8 = (bf16[3136,128]{1,0:T(8,128)(2,1)}, bf16[3136,128]{1,0:T(8,128)(2,1)S(1)}, u32[]{:S(2)}, u32[]{:S(2)}) collective-permute-start(bf16[3136,128]{1,0:T(8,128)(2,1)} %get-tuple-element.87), channel_id=1, source_target_pairs={{0,32},{32,64},{64,96},{96,0},{1,33},{33,65},{65,97},{97,1},{2,34}... | collective-permute-start | bytes 2408456 | tf_op jit(solution)/shard_map/ppermute | solution.py:41
  74.3 21.4 %collective-permute-start.9 = (bf16[3136,128]{1,0:T(8,128)(2,1)}, bf16[3136,128]{1,0:T(8,128)(2,1)S(1)}, u32[]{:S(2)}, u32[]{:S(2)}) collective-permute-start(bf16[3136,128]{1,0:T(8,128)(2,1)} %get-tuple-element.86), channel_id=1, source_target_pairs={{0,96},{32,0},{64,32},{96,64},{1,97},{33,1},{65,33},{97,65},{2,98}... | collective-permute-start | bytes 2408456 | tf_op jit(solution)/shard_map/ppermute | solution.py:41
  95.7 19.0 %copy-start.5 = (bf16[3136,128]{1,0:T(8,128)(2,1)}, bf16[3136,128]{1,0:T(8,128)(2,1)S(1)}, u32[]{:S(2)}) copy-start(bf16[3136,128]{1,0:T(8,128)(2,1)S(1)} %collective-permute-done.9.w2) | copy-start | bytes 2408452
  99.0 5.8 %collective-permute-start.10 = (bf16[2,528,512]{2,1,0:T(8,128)(2,1)S(1)}, bf16[2,528,512]{2,1,0:T(8,128)(2,1)}, u32[]{:S(2)}, u32[]{:S(2)}) collective-permute-start(bf16[2,528,512]{2,1,0:T(8,128)(2,1)S(1)} %get-tuple-element.78), channel_id=1, source_target_pairs={{0,8},{8,0},{1,9},{9,1},{2,10},{10,2},{3,11},{11,3},{4,12},{12,4},... | collective-permute-start | bytes 3244040 | tf_op jit(solution)/shard_map/ppermute | solution.py:41
  102.4 33.7 %collective-permute-start.13 = (bf16[64,4096]{1,0:T(8,128)(2,1)S(1)}, bf16[64,4096]{1,0:T(8,128)(2,1)}, u32[]{:S(2)}, u32[]{:S(2)}) collective-permute-start(bf16[64,4096]{1,0:T(8,128)(2,1)S(1)} %collective-permute-done.a), channel_id=1, source_target_pairs={{0,8},{8,0},{1,9},{9,1},{2,10},{10,2},{3,11},{11,3},{4,12},{12,4},... | collective-permute-start | bytes 1572872 | tf_op jit(solution)/shard_map/ppermute | solution.py:41
  102.4 33.7 %collective-permute-start.14 = (bf16[64,4096]{1,0:T(8,128)(2,1)}, bf16[64,4096]{1,0:T(8,128)(2,1)}, u32[]{:S(2)}, u32[]{:S(2)}) collective-permute-start(bf16[64,4096]{1,0:T(8,128)(2,1)} %collective-permute-done.1.b), channel_id=1, source_target_pairs={{0,8},{8,0},{1,9},{9,1},{2,10},{10,2},{3,11},{11,3},{4,12},{12,4},... | collective-permute-start | bytes 1572872 | tf_op jit(solution)/shard_map/ppermute | solution.py:41
  107.4 39.8 %all-to-all-start.3 = ((bf16[16,80,512]{2,1,0:T(8,128)(2,1)}), bf16[16,80,512]{2,1,0:T(8,128)(2,1)S(1)}, u32[]{:S(2)}, u32[]{:S(2)}) async-start(bf16[16,80,512]{2,1,0:T(8,128)(2,1)} %shard_map.192), calls=%async_computation.3 | async-start | bytes 2621440 | tf_op jit(solution)/shard_map/all_to_all | solution.py:45
  114.7 11.3 %collective-permute-start.11 = (bf16[1504,128]{1,0:T(8,128)(2,1)}, bf16[1504,128]{1,0:T(8,128)(2,1)S(1)}, u32[]{:S(2)}, u32[]{:S(2)}) collective-permute-start(bf16[1504,128]{1,0:T(8,128)(2,1)} %pad_maximum_fusion.2), channel_id=1, source_target_pairs={{0,32},{32,64},{64,96},{96,0},{1,33},{33,65},{65,97},{97,1},{2,34}... | collective-permute-start | bytes 1155080 | tf_op jit(solution)/shard_map/ppermute | solution.py:41
  115.6 12.6 %collective-permute-start.12 = (bf16[1504,128]{1,0:T(8,128)(2,1)}, bf16[1504,128]{1,0:T(8,128)(2,1)}, u32[]{:S(2)}, u32[]{:S(2)}) collective-permute-start(bf16[1504,128]{1,0:T(8,128)(2,1)} %pad_maximum_fusion.3), channel_id=1, source_target_pairs={{0,96},{32,0},{64,32},{96,64},{1,97},{33,1},{65,33},{97,65},{2,98}... | collective-permute-start | bytes 1155080 | tf_op jit(solution)/shard_map/ppermute | solution.py:41
  121.1 15.0 %collective-permute-start.15 = (bf16[32,4096]{1,0:T(8,128)(2,1)}, bf16[32,4096]{1,0:T(8,128)(2,1)S(1)}, u32[]{:S(2)}, u32[]{:S(2)}) collective-permute-start(bf16[32,4096]{1,0:T(8,128)(2,1)} %collective-permute-done.6.c), channel_id=1, source_target_pairs={{0,8},{8,0},{1,9},{9,1},{2,10},{10,2},{3,11},{11,3},{4,12},{12,4},... | collective-permute-start | bytes 786440 | tf_op jit(solution)/shard_map/ppermute | solution.py:41
  126.0 10.0 %collective-permute-start.16 = (bf16[32,4096]{1,0:T(8,128)(2,1)}, bf16[32,4096]{1,0:T(8,128)(2,1)S(1)}, u32[]{:S(2)}, u32[]{:S(2)}) collective-permute-start(bf16[32,4096]{1,0:T(8,128)(2,1)} %collective-permute-done.7.d), channel_id=1, source_target_pairs={{0,8},{8,0},{1,9},{9,1},{2,10},{10,2},{3,11},{11,3},{4,12},{12,4},... | collective-permute-start | bytes 786440 | tf_op jit(solution)/shard_map/ppermute | solution.py:41
  (21 other events, 152.8 us)

commit v3 on v2

v3 whole, which is shorter than its diff:
```python
import jax
import jax.numpy as jnp
from jax import lax
from jax.experimental import pallas as pl
from jax.experimental.pallas import tpu as pltpu
from jax.sharding import Mesh
from jax.sharding import PartitionSpec as P

noise_scale = 0.01
fitness_eps = 1e-05
beta_first = 0.9
beta_second = 0.999
adam_eps = 1e-08

BF = jnp.bfloat16
F32 = jnp.float32
VMEM_LIMIT = 60 * 1024 * 1024
CODES = 160
CHUNK = 512
TAIL = 16
SHARE_ROWS = 352
NT = (((1,), (1,)), ((), ()))
TN = (((0,), (0,)), ((), ()))
ROW = ("xh", "core")


def params():
    return pltpu.CompilerParams(vmem_limit_bytes=VMEM_LIMIT)


def cost(flops, moved):
    return pl.CostEstimate(flops=flops, bytes_accessed=moved, transcendentals=0)


def whole(value):
    rank = len(value.shape)
    return pl.BlockSpec(value.shape, lambda *_: (0,) * rank)


def shifted(value, axis, step):
    size = lax.axis_size(axis)
    return lax.ppermute(value, axis, [(i, (i + step) % size) for i in range(size)])


def exchange(value, axis, split=0):
    return lax.all_to_all(value, axis, split, 0, tiled=True)


def ring_first(value):
    return shifted(value, "pop", 1), shifted(value, "pop", 3)


def ring_second(below, above):
    return shifted(below, "pop", 1), shifted(above, "pop", 3)


def together(*values):
    return lax.optimization_barrier(values)


def silu(value):
    half = 0.5 * value
    return half + half * jnp.tanh(half)


def table_kernel(where, table, up_t, left, *rest):
    downs, sent, columns = rest[:-2], rest[-2], rest[-1]

    @pl.when(pl.program_id(0) == 0)
    def _():
        columns[...] = jnp.zeros_like(columns)
        columns[:, 0 : table.shape[0]] = table[...].astype(F32).T.astype(BF)

    parts, share, _ = up_t.shape
    slots = left.shape[0] // parts
    codes = columns[...]
    tiles = pl.cdiv(share + slots, 128)
    spare = jnp.zeros((tiles * 128 - share - slots, codes.shape[1]), F32)
    probe = jnp.dot(left[...], codes, preferred_element_type=F32)
    for part in range(parts):
        product = jnp.dot(up_t[part], codes, preferred_element_type=F32)
        own = probe[part * slots : (part + 1) * slots]
        both = jnp.concatenate([product, own, spare], axis=0).T.astype(BF)
        for tile in range(tiles):
            sent[part, pl.ds(tile * CODES, CODES), :] = both[
                0:CODES, tile * 128 : (tile + 1) * 128
            ]
        for index in range(2):
            down = downs[2 * part + index]
            start = tiles * CODES + index * SHARE_ROWS
            sent[part, pl.ds(start, down.shape[0]), :] = down[...]


def table_products(where, table, up_t, left, down):
    vocab = table.shape[0]
    parts, share, width = up_t.shape
    slots = left.shape[0] // parts
    height = pl.cdiv(share + slots, 128) * CODES + 2 * SHARE_ROWS
    pops = down.shape[1] // parts // 128
    some = 4

    def cut(part, far):
        def index(i, w):
            return (0, (i * some + part) * pops + lax.rem(w[1] + 2 * far, pops))

        return pl.BlockSpec((down.shape[0], 128), index)

    cuts = [cut(part, far) for part in range(some) for far in range(2)]
    return pl.pallas_call(
        table_kernel,
        grid_spec=pltpu.PrefetchScalarGridSpec(
            num_scalar_prefetch=1,
            grid=(parts // some,),
            in_specs=[
                pl.BlockSpec((vocab, width), lambda i, w: (0, w[0])),
                pl.BlockSpec((some, share, width), lambda i, w: (i, 0, 0)),
                pl.BlockSpec((some * slots, width), lambda i, w: (i, 0)),
            ]
            + cuts,
            out_specs=pl.BlockSpec((some, height, 128), lambda i, w: (i, 0, 0)),
            scratch_shapes=[pltpu.VMEM((width, 256), BF)],
        ),
        out_shape=jax.ShapeDtypeStruct((parts, height, 128), BF),
        compiler_params=params(),
        cost_estimate=cost(1 << 20, 1 << 20),
    )(where, table, up_t, left, *([down] * len(cuts)))


def hidden_kernel(
    where, codes, shares, right, own_share, own_right, own_left, w0, w1, w2, w3,
    mine_out, other_out, rhs, own, hid, weight, sems,
):
    parts, height, _ = shares.shape
    tiles = height // CODES
    ff = right.shape[1]
    share = own_right.shape[1]
    slots = right.shape[0]
    rows = codes.shape[2]
    depth = rhs.shape[0]
    per_slot = rows // slots
    width = w0.shape[1]
    step = pl.program_id(0)
    copies = [
        pltpu.make_async_copy(part, weight.at[:, pl.ds(i * width, width)], sems.at[i])
        for i, part in enumerate((w0, w1, w2, w3))
    ]

    @pl.when(step == 0)
    def _():
        for copy in copies:
            copy.start()
        rhs[...] = jnp.zeros_like(rhs)
        for part in range(parts):
            for tile in range(tiles):
                low = tile * 128
                high = min(low + 128, share)
                rhs[pl.ds(0, CODES), part * share + low : part * share + high] = shares[
                    part, pl.ds(tile * CODES, CODES), 0 : high - low
                ]
        own[...] = jnp.zeros_like(own)
        for tile in range(tiles):
            low = tile * 128
            high = min(low + 128, share)
            own[pl.ds(0, CODES), low:high] = own_share[pl.ds(tile * CODES, CODES), 0 : high - low]

    first = CODES
    second = CODES + slots
    for start in (first, second):
        rhs[pl.ds(start, slots), :] = right[...]
        own[pl.ds(start, slots), :] = own_right[...]

    line = lax.broadcasted_iota(jnp.int32, (depth, rows), 0)
    slot = lax.broadcasted_iota(jnp.int32, (depth, rows), 1) // per_slot
    hot = jnp.where(line == codes[0], 1.0, 0.0)
    hot_b = hot[0:CODES].astype(BF)
    pairs = 2
    per_part = slots // pairs
    start = share - (tiles - 1) * 128
    looked = []
    for pair in range(pairs):
        tile = shares[step * pairs + pair, pl.ds((tiles - 1) * CODES, CODES), :]
        term = lax.dot_general(tile, hot_b, TN, preferred_element_type=F32)
        looked.append(term[start : start + per_part])
    row_slot = lax.broadcasted_iota(jnp.int32, (slots, rows), 1) // per_slot
    own_row = lax.broadcasted_iota(jnp.int32, (slots, rows), 0) == row_slot
    probe = jnp.where(own_row, jnp.concatenate(looked, axis=0), 0.0)
    probe = noise_scale * jnp.sum(probe, axis=0, keepdims=True)
    high = probe.astype(BF).astype(F32)
    lhs = jnp.where(line - first == slot, high, hot)
    lhs = jnp.where(line - second == slot, probe - high, lhs)
    lhs = lhs.T.astype(BF)

    pre = jnp.dot(lhs, own[...], preferred_element_type=F32)
    mine = silu(pre).astype(BF)
    probes = lax.dot_general(own_left[...], mine, NT, preferred_element_type=F32)
    probe_row = jnp.sum(jnp.where(own_row, probes, 0.0), axis=0, keepdims=True)
    probe_high = probe_row.astype(BF).astype(F32)
    index = lax.broadcasted_iota(jnp.int32, (TAIL, rows), 0)
    tail = jnp.where(index == 0, probe_high, jnp.where(index == 1, probe_row - probe_high, 0.0))

    for start in range(0, ff, 256):
        size = min(256, ff - start)
        pre = jnp.dot(lhs, rhs[:, start : start + size], preferred_element_type=F32)
        hid[:, start : start + size] = silu(pre).astype(BF)

    @pl.when(step == 0)
    def _():
        for copy in copies:
            copy.wait()

    product = jnp.dot(hid[...], weight[...], preferred_element_type=F32).astype(BF)

    def store(out):
        out[0, pl.ds(rows, TAIL), :] = tail.astype(BF)
        for i, source in enumerate(slot_order(where[0])):
            at = pl.multiple_of(source * width, width)
            out[0, pl.ds(0, rows), pl.ds(at, width)] = product[:, i * width : (i + 1) * width]

    @pl.when(step % 2 == where[1])
    def _():
        store(mine_out)

    @pl.when(step % 2 != where[1])
    def _():
        store(other_out)


def hidden_product(where, codes, shares, right, own_share, own_right, own_left, weights):
    steps, _, rows = codes.shape
    ff = right.shape[1]
    share = own_right.shape[1]
    slots = right.shape[0] // steps
    width = 4 * weights[0].shape[1]
    assert width == rows
    out = jax.ShapeDtypeStruct((steps // 2, rows + TAIL, width), BF)
    spec = pl.BlockSpec((1, rows + TAIL, width), lambda i, p: (i // 2, 0, 0))
    return pl.pallas_call(
        hidden_kernel,
        grid_spec=pltpu.PrefetchScalarGridSpec(
            num_scalar_prefetch=1,
            grid=(steps,),
            in_specs=[
                pl.BlockSpec((1, 1, rows), lambda i, p: (i, 0, 0)),
                whole(shares),
                pl.BlockSpec((slots, ff), lambda i, p: (i, 0)),
                whole(own_share),
                pl.BlockSpec((slots, share), lambda i, p: (i, 0)),
                pl.BlockSpec((slots, share), lambda i, p: (i, 0)),
            ]
            + [pl.BlockSpec(memory_space=pl.ANY)] * 4,
            out_specs=[spec, spec],
            scratch_shapes=[
                pltpu.VMEM((256, ff), BF),
                pltpu.VMEM((256, share), BF),
                pltpu.VMEM((rows, ff), BF),
                pltpu.VMEM((ff, width), BF),
                pltpu.SemaphoreType.DMA((4,)),
            ],
        ),
        out_shape=[out, out],
        compiler_params=params(),
        cost_estimate=cost(2 * steps * rows * ff * (256 + width), 8 << 20),
    )(where, codes, shares, right, own_share, own_right, own_left, *weights)


def pieces_kernel(mine, theirs, out):
    parts, piece, _ = out.shape
    rows = piece - TAIL
    total = mine[0].astype(F32) + theirs[0].astype(F32)
    top = total.shape[0] - TAIL
    probe = total[top : top + 1, :] + total[top + 1 : top + 2, :]
    high = probe.astype(BF).astype(F32)
    index = lax.broadcasted_iota(jnp.int32, (TAIL, total.shape[1]), 0)
    tail = jnp.where(index == 0, high, jnp.where(index == 1, probe - high, 0.0)).astype(BF)
    for part in range(parts):
        out[part, pl.ds(0, rows), :] = total[part * rows : (part + 1) * rows, :].astype(BF)
        out[part, pl.ds(rows, TAIL), :] = tail


def pieces(mine, theirs, parts):
    count, height, width = mine.shape
    rows = (height - TAIL) // parts
    spec = pl.BlockSpec((1, height, width), lambda i: (i, 0, 0))
    return pl.pallas_call(
        pieces_kernel,
        grid=(count,),
        in_specs=[spec, spec],
        out_specs=pl.BlockSpec((parts, rows + TAIL, width), lambda i: (i, 0, 0)),
        out_shape=jax.ShapeDtypeStruct((count * parts, rows + TAIL, width), BF),
        compiler_params=params(),
        cost_estimate=cost(1 << 20, 4 << 20),
    )(mine, theirs)


def final_kernel(col, got, tails, codes, table, right, out, own):
    rows = out.shape[0]
    halves, parts, _, width = got.shape
    slots = right.shape[0]
    per_slot = rows // slots

    @pl.when(pl.program_id(0) == 0)
    def _():
        probe = jnp.sum(tails[...].astype(F32), axis=(0, 1))
        probe = jnp.sum(probe, axis=0, keepdims=True)
        lane = lax.broadcasted_iota(jnp.int32, (rows, width), 1)
        line = lax.broadcasted_iota(jnp.int32, (rows, width), 0)
        mine = jnp.where(lane == line + col[0] * rows, probe, 0.0)
        own[...] = noise_scale * jnp.sum(mine, axis=1, keepdims=True)

    hot = lax.broadcasted_iota(jnp.int32, (rows, table.shape[0]), 1) == codes[...]
    hot = jnp.where(hot, 1.0, 0.0).astype(BF)
    for part in range(parts):
        cols = slice(part * width, (part + 1) * width)
        product = got[0, part, 0:rows, :].astype(F32)
        for index in range(1, halves):
            product = product + got[index, part, 0:rows, :].astype(F32)
        spread = jnp.concatenate(
            [
                jnp.broadcast_to(right[i : i + 1, cols].astype(F32), (per_slot, width))
                for i in range(slots)
            ],
            axis=0,
        )
        residual = jnp.dot(hot, table[:, cols], preferred_element_type=F32)
        out[:, cols] = (residual + product + own[...] * spread).astype(BF)


def final_sum(col, got, codes, table, right):
    halves, parts, height, width = got.shape
    rows = height - TAIL
    some = 4
    return pl.pallas_call(
        final_kernel,
        grid_spec=pltpu.PrefetchScalarGridSpec(
            num_scalar_prefetch=1,
            grid=(parts // some,),
            in_specs=[
                pl.BlockSpec((halves, some, height, width), lambda i, c: (0, i, 0, 0)),
                pl.BlockSpec(
                    (halves, parts, TAIL, width), lambda i, c: (0, 0, rows // TAIL, 0)
                ),
                whole(codes),
                pl.BlockSpec((table.shape[0], some * width), lambda i, c: (0, i)),
                pl.BlockSpec((right.shape[0], some * width), lambda i, c: (0, i)),
            ],
            out_specs=pl.BlockSpec((rows, some * width), lambda i, c: (0, i)),
            scratch_shapes=[pltpu.VMEM((rows, 1), F32)],
        ),
        out_shape=jax.ShapeDtypeStruct((rows, parts * width), BF),
        compiler_params=params(),
        cost_estimate=cost(1 << 20, 4 << 20),
    )(col, got, got, codes, table, right)


def slot_order(pop):
    return [lax.rem(pop + step, 4) for step in (0, 3, 1, 2)]


def moments(grad, moment, second):
    first = beta_first * moment + (1.0 - beta_first) * grad
    sec = beta_second * second + (1.0 - beta_second) * grad * grad
    return first, sec, first / (jnp.sqrt(sec) + adam_eps)


def up_kernel(left, a, b, c, d, moment, second, first_new, second_new, step):
    weighted = jnp.concatenate([a[...], b[...], c[...], d[...]], axis=1)
    grad = jnp.dot(weighted, left[...], preferred_element_type=F32)
    first, sec, direction = moments(grad, moment[...], second[...])
    first_new[...] = first
    second_new[...] = sec
    step[...] = direction


def up_adam(left, weighted, moment, second, tile):
    rows, columns = moment.shape
    slots = left.shape[0] // 4
    state = pl.BlockSpec((tile, columns), lambda j: (j, 0))
    return pl.pallas_call(
        up_kernel,
        grid=(rows // tile,),
        in_specs=[whole(left)]
        + [pl.BlockSpec((tile, slots), lambda j: (j, 0))] * 4
        + [state] * 2,
        out_specs=[state] * 3,
        out_shape=[jax.ShapeDtypeStruct(moment.shape, F32)] * 3,
        compiler_params=params(),
        cost_estimate=cost(1 << 20, 8 << 20),
    )(left, *weighted, moment, second)


def down_kernel(
    core, left, own, a, b, c, d, e, f, g, h,
    moment, second, first_new, second_new, step, grad, factor, sems,
):
    slots, width = own.shape
    lines = width // 128
    half = slots // 2
    quarter = half // 2

    @pl.when(pl.program_id(0) == 0)
    def _():
        copies = [pltpu.make_async_copy(own, factor.at[pl.ds(0, slots)], sems.at[0])]
        for place, parts in ((core[0], (a, b, c, d)), (1 - core[0], (e, f, g, h))):
            at = pl.multiple_of(place * half, half)
            starts = (slots, 2 * slots, 3 * slots, 3 * slots + quarter)
            for start, part in zip(starts, parts):
                copies.append(
                    pltpu.make_async_copy(
                        part, factor.at[pl.ds(at + start, part.shape[0])], sems.at[len(copies)]
                    )
                )
        for copy in copies:
            copy.start()
        for copy in copies:
            copy.wait()
        total = lax.dot_general(left[...], factor[...], TN, preferred_element_type=F32)
        high = grad.shape[0] // lines
        for line in range(lines):
            grad[pl.ds(line, high, stride=lines), :] = total[
                0:high, line * 128 : (line + 1) * 128
            ]

    rows = moment.shape[0]
    start = pl.multiple_of(pl.program_id(0) * rows, rows)
    first, sec, direction = moments(grad[pl.ds(start, rows), :], moment[...], second[...])
    first_new[...] = first
    second_new[...] = sec
    step[...] = direction


def down_adam(core, left, own, parts, moment, second, rows):
    slots, width = own.shape
    lines = width // 128
    steps = pl.cdiv(moment.shape[0] // lines, rows)
    state = pl.BlockSpec((rows * lines, 128), lambda j, p: (j, 0))
    return pl.pallas_call(
        down_kernel,
        grid_spec=pltpu.PrefetchScalarGridSpec(
            num_scalar_prefetch=1,
            grid=(steps,),
            in_specs=[whole(left)] + [pl.BlockSpec(memory_space=pl.ANY)] * 9 + [state] * 2,
            out_specs=[state] * 3,
            scratch_shapes=[
                pltpu.VMEM((rows * lines * steps, 128), F32),
                pltpu.VMEM((4 * slots, width), BF),
                pltpu.SemaphoreType.DMA((9,)),
            ],
        ),
        out_shape=[jax.ShapeDtypeStruct(moment.shape, F32)] * 3,
        compiler_params=params(),
        cost_estimate=cost(1 << 20, 8 << 20),
    )(core, left, own, *parts, moment, second)


def per_device(
    obs_ids,
    member_ids,
    fitness,
    embed_table,
    up_weight,
    down_weight,
    up_left,
    up_right,
    down_left,
    down_right,
    up_moment,
    up_second,
    down_moment,
    down_second,
):
    member_count, per_member = obs_ids.shape
    row_count = member_count * per_member
    model = embed_table.shape[1]
    feat_width, ff_quarter = up_weight.shape
    ff_share = down_weight.shape[0]
    cols = lax.axis_size("col")
    pops = lax.axis_size("pop")
    col_index = lax.axis_index("col")
    col_ref = col_index.reshape(1)
    pop_ref = lax.axis_index("pop").reshape(1)
    codes = obs_ids.reshape(row_count, 1)

    up_rows = feat_width // pops
    down_rows = ff_share // pops
    lefts = jnp.concatenate(
        [
            up_left.reshape(member_count, pops, up_rows).transpose(1, 0, 2),
            jnp.pad(
                down_left.reshape(member_count, pops, down_rows).transpose(1, 0, 2),
                ((0, 0), (0, 0), (0, up_rows - down_rows)),
            ),
        ],
        axis=1,
    )
    core = lax.axis_index("core")
    pop_index = lax.axis_index("pop")

    def factor(step):
        return lax.dynamic_index_in_dim(lefts, (pop_index + step) % pops, 0, keepdims=False)

    sent = table_products(
        jnp.stack([col_index, pop_index]),
        embed_table,
        up_weight.T.reshape(cols, ff_share, feat_width),
        up_left,
        down_weight,
    )
    sent, fitness = together(sent, fitness)
    got = exchange(sent, "col")
    members_all = fitness.shape[0]
    fit_mean = jnp.mean(fitness)
    fit_var = jnp.mean((fitness - fit_mean) * (fitness - fit_mean))
    slot_fit = jnp.sum(
        jnp.where(member_ids[:, None] == jnp.arange(members_all)[None, :], fitness[None, :], 0.0),
        axis=1,
    )
    fit_scale = (
        (slot_fit - fit_mean) / jnp.sqrt(fit_var + fitness_eps) / (members_all * noise_scale)
    )
    up_weighted = (fit_scale[None, :] * up_right.T.astype(F32)).astype(BF)
    down_weighted = (fit_scale[:, None] * down_right.astype(F32)).astype(BF)
    small = [jnp.concatenate([up_weighted, factor(step)], axis=0) for step in range(pops)]
    small = [small[0]] + [shifted(small[step], "pop", step) for step in (1, 3, 2)]
    own_right = lax.dynamic_slice_in_dim(up_right, col_index * ff_share, ff_share, 1)
    share_rows = row_count // (4 * cols)
    share_slots = share_rows // per_member
    place_index = lax.axis_index(ROW + ("col",))
    mine_codes = lax.dynamic_slice_in_dim(
        obs_ids.reshape(row_count, 1), place_index * share_rows, share_rows, 0
    )
    mine_right = lax.dynamic_slice_in_dim(down_right, place_index * share_slots, share_slots, 0)
    half = member_count // 2
    down_own = lax.dynamic_slice_in_dim(down_weighted, core * half, half, 0)
    got, own_right, mine_codes, mine_right, down_own = together(
        got, own_right, mine_codes, mine_right, down_own
    )

    height = got.shape[1] - 2 * SHARE_ROWS
    share = jnp.sum(got[:, :height].astype(F32), axis=0).astype(BF)
    weight = got[:, height : height + ff_share].reshape(ff_quarter, -1)
    weight_far = got[:, height + SHARE_ROWS : height + SHARE_ROWS + ff_share]
    weight_near = ring_first(weight)
    shares = exchange(jnp.broadcast_to(share[None], (cols,) + share.shape), "col")
    weights = [weight, *weight_near, weight_far.reshape(ff_quarter, -1)]
    up_out = up_adam(
        jnp.concatenate([part[ff_quarter : ff_quarter + member_count] for part in small], axis=0),
        small,
        up_moment.reshape(up_rows, ff_quarter).T,
        up_second.reshape(up_rows, ff_quarter).T,
        1376,
    )
    shares, down_own, up_out, *weights = together(shares, down_own, up_out, *weights)

    down_near = ring_first(down_own)
    mine, other = hidden_product(
        jnp.stack([pop_index, core]),
        obs_ids.reshape(row_count // CHUNK, 1, CHUNK),
        shares,
        up_right,
        share,
        own_right,
        down_left,
        weights,
    )
    mine, other, *down_near = together(mine, other, *down_near)

    theirs = shifted(other, "core", 1)
    got = exchange(pieces(mine, theirs, cols), ("xh", "col"))
    got = got.reshape((2, cols) + got.shape[1:])
    block_out = final_sum(col_ref, got, mine_codes, embed_table, mine_right)

    down_parts = list(down_near) + list(
        ring_second(down_near[0][: half // 2], down_near[1][half // 2 :])
    )
    down_theirs = [shifted(part, "core", 1) for part in down_parts]
    down_out = down_adam(
        core.reshape(1),
        jnp.concatenate([part[ff_quarter + member_count :] for part in small], axis=0),
        down_weighted,
        (*down_parts, *down_theirs),
        down_moment.reshape(-1, 128),
        down_second.reshape(-1, 128),
        48,
    )
    up_out = [value.T.reshape(up_moment.shape) for value in up_out]
    down_out = [value.reshape(down_moment.shape) for value in down_out]
    return (block_out, *up_out, *down_out)


def solution(mesh):
    devices = mesh.devices
    pops, rows, cols = devices.shape
    fine = Mesh(devices.reshape(pops, rows // 2, 2, cols), ("pop", "xh", "core", "col"))
    split = ROW + ("col",)
    in_specs = (
        P("pop", None),
        P("pop"),
        P(),
        P(),
        P("col", ROW),
        P(split, None),
        P("pop", "col"),
        P("pop", ROW),
        P("pop", split),
        P("pop", None),
        P("col", "pop", None, ROW),
        P("col", "pop", None, ROW),
        P(split, "pop", None, None),
        P(split, "pop", None, None),
    )
    out_specs = (
        P(("pop",) + split, None),
        P("col", "pop", None, ROW),
        P("col", "pop", None, ROW),
        P("col", "pop", None, ROW),
        P(split, "pop", None, None),
        P(split, "pop", None, None),
        P(split, "pop", None, None),
    )
    return jax.shard_map(
        per_device, mesh=fine, in_specs=in_specs, out_specs=out_specs, check_vma=False
    )
```

time: 156 us -> 136 us (0.87)
  starting transfers between devices: 47.2 us -> 35 us
  Pallas kernels: 52.4 us -> 41.7 us
  other arithmetic: 6.2 us -> 8.06 us
    all_to_all x4 -> x3, starting transfers between devices: 22.4 us -> 16.3 us  [exchange(): return lax.all_to_all(value, axis, split, 0, tiled=True)]
    ppermute x17 -> x14, starting transfers between devices: 24.7 us -> 18.7 us  [shifted(): lax.ppermute(value, axis, [(i, (i + step) % size) for i in range(size)])]
    all_to_all x4 -> x3, waiting for transfers between devices: 0.01 us -> 5.52 us  [exchange(): return lax.all_to_all(value, axis, split, 0, tiled=True)]
    ppermute x17 -> x14, waiting for transfers between devices: 25.6 us -> 21.2 us  [shifted(): lax.ppermute(value, axis, [(i, (i + step) % size) for i in range(size)])]
    pallas_call x1, Pallas kernels: 6.43 us -> 2.88 us  [final_sum(): pl.pallas_call(final_kernel, grid_spec=pltpu.PrefetchScalarGridSpec(num_s...]
    squeeze x1 -> x0, local copies, waits for them, and re-layouts: 3.31 us -> none  [per_device(): other = lax.dynamic_index_in_dim(by_core, 1 - core, 1, keepdims=False)]
    unnamed x52, local copies, waits for them, and re-layouts: 4.17 us -> 6.85 us
    slice x12 -> x7, local copies, waits for them, and re-layouts: 6.99 us -> 4.39 us  [the longest x4 3.12 us: per_device(): part[ff_quarter + member_count:]]
  transfers between devices with their start and end apart: 21 -> 17, of which waited for: 6 -> 7; matrix products, arithmetic and copies ran while one was open for 12% -> 18% of each run, Pallas kernels for 28% -> 23%
where the time goes in v3:
time: 136 us; the launch traced here: 135 us
  Pallas kernels  41.7 us (31%)
  starting transfers between devices  35 us (26%)
  waiting for transfers between devices  26.7 us (20%)
  local copies, waits for them, and re-layouts  20.9 us (15%)
  other arithmetic  8.06 us (6%)
  between operations  2.37 us (2%)
    ppermute x14, waiting for transfers between devices, shifted(): lax.ppermute(value, axis, [(i, (i + step) % size) for i in range(size)])  21.2 us
    pallas_call x1, Pallas kernels, hidden_product(): pl.pallas_call(hidden_kernel, grid_spec=pltpu.PrefetchScalarGridSpec(num_...  18.7 us
    ppermute x14, starting transfers between devices, shifted(): lax.ppermute(value, axis, [(i, (i + step) % size) for i in range(size)])  18.7 us
    all_to_all x3, starting transfers between devices, exchange(): return lax.all_to_all(value, axis, split, 0, tiled=True)  16.3 us
    pallas_call x1, Pallas kernels, down_adam(): pl.pallas_call(down_kernel, grid_spec=pltpu.PrefetchScalarGridSpec(num_sc...  7.77 us
    unnamed x52, local copies, waits for them, and re-layouts  6.85 us
    all_to_all x3, waiting for transfers between devices, exchange(): return lax.all_to_all(value, axis, split, 0, tiled=True)  5.52 us
    pallas_call x1, Pallas kernels, table_products(): pl.pallas_call(table_kernel, grid_spec=pltpu.PrefetchScalarGridSpec(num_s...  5.16 us
  transfers between devices with their start and end apart: 17, of which 7 were waited for; matrix products, arithmetic and copies ran while one was open for 18% of the time, Pallas kernels for 23%

profile of v3, /device:TPU:1, one launch (start us, length us, event | category | flops | bytes accessed | tf_op | source)
XLA Modules:
  0.0 134.7 jit_solution(12237255760333964094)
XLA Ops:
  1.2 5.2 %shard_map.189 = bf16[8,1184,128]{2,1,0:T(8,128)(2,1)} custom-call(s32[2]{0:T(128)} %get-tuple-element.103.where, bf16[156,4096]{1,0:T(8,128)(2,1)} %table.3, bf16[8,344,512]{2,1,0:T(8,128)(2,1)} %bitcast.50, bf16[128,512]{1,0:T(8,128)(2,1)} %left.1, bf16[344,4096]{1,0:T(8,128)(2,1)} %rest_7_.1, bf16[344,4096]{1,0:T(8,128)(2,1)} %rest_7_.1, ...), custom_call_target="tpu_custom_call" | custom-call | flops 1048576 | bytes 1048576 | tf_op jit(solution)/shard_map/pallas_call | solution.py:109
  6.4 6.1 %all-to-all-start = ((bf16[8,1184,128]{2,1,0:T(8,128)(2,1)}), bf16[8,1184,128]{2,1,0:T(8,128)(2,1)S(1)}, u32[]{:S(2)}, u32[]{:S(2)}) async-start(bf16[8,1184,128]{2,1,0:T(8,128)(2,1)} %shard_map.189), calls=%async_computation | async-start | bytes 4849664 | tf_op jit(solution)/shard_map/all_to_all | solution.py:46
  17.6 2.1 %pad_maximum_fusion.3 = (bf16[3008,128]{1,0:T(8,128)(2,1)}, bf16[3008,128]{1,0:T(8,128)(2,1)}, bf16[3008,128]{1,0:T(8,128)(2,1)}, bf16[3008,128]{1,0:T(8,128)(2,1)}) fusion(bf16[256,128]{1,0:T(8,128)(2,1)S(1)} %get-tuple-element.98, bf16[2752,128]{1,0:T(8,128)(2,1)S(1)} %fusion, bf16[256,128]{1,0:T(8,128)(2,1)S(1)} %get-tuple-element.100, ...), kind=kLoop, calls=%fused_computation.6 | loop fusion | flops 5005312 | bytes 4046848 | tf_op jit(solution)/shard_map/concatenate | solution.py:522
  19.7 3.7 %collective-permute-start.2 = (bf16[3008,128]{1,0:T(8,128)(2,1)}, bf16[3008,128]{1,0:T(8,128)(2,1)}, u32[]{:S(2)}, u32[]{:S(2)}) collective-permute-start(bf16[3008,128]{1,0:T(8,128)(2,1)} %get-tuple-element.94), channel_id=1, source_target_pairs={{0,64},{32,96},{64,0},{96,32},{1,65},{33,97},{65,1},{97,33},{2,66}... | collective-permute-start | bytes 2310152 | tf_op jit(solution)/shard_map/ppermute | solution.py:42
  26.8 1.6 %reshape.107 = s32[2048,1]{1,0:T(8,128)} reshape(s32[128,16]{1,0:T(8,128)S(1)} %copy.42) | data formatting | bytes 16384 | tf_op jit(solution)/shard_map/reshape | solution.py:529
  30.5 1.5 %multiply_convert_fusion.own = bf16[128,4096]{1,0:T(8,128)(2,1)S(1)} fusion(bf16[128,4096]{1,0:T(8,128)(2,1)} %param.23, f32[128]{0:T(128)S(1)} %divide_multiply_fusion), kind=kLoop, calls=%fused_computation | loop fusion | flops 1572864 | bytes 2097664 | tf_op jit(solution)/shard_map/convert_element_type | solution.py:521
  33.8 1.6 %constant_dynamic-slice_fusion.3.own_right = bf16[128,344]{1,0:T(8,128)(2,1)} fusion(bf16[128,2752]{1,0:T(8,128)(2,1)} %copy.43.right, s32[]{:T(128)S(6)} %select_n.48), kind=kLoop, calls=%fused_computation.24 | loop fusion | bytes 176132 | tf_op jit(solution)/shard_map/dynamic_slice | solution.py:524
  36.8 5.5 %all-to-all-done = bf16[8,1184,128]{2,1,0:T(8,128)(2,1)S(1)} async-done(((bf16[8,1184,128]{2,1,0:T(8,128)(2,1)}), bf16[8,1184,128]{2,1,0:T(8,128)(2,1)S(1)}, u32[]{:S(2)}, u32[]{:S(2)}) %all-to-all-start) | async-done | bytes 2424864 | tf_op jit(solution)/shard_map/all_to_all | solution.py:46
  44.1 3.7 %all-to-all-start.1 = ((bf16[8,480,128]{2,1,0:T(8,128)(2,1)}), bf16[8,480,128]{2,1,0:T(8,128)(2,1)S(1)}, u32[]{:S(2)}, u32[]{:S(2)}) async-start(bf16[8,480,128]{2,1,0:T(8,128)(2,1)} %broadcast_in_dim.16), calls=%async_computation.1 | async-start | bytes 1966080 | tf_op jit(solution)/shard_map/all_to_all | solution.py:46
  49.1 1.5 %collective-permute-start.3 = (bf16[2752,128]{1,0:T(8,128)(2,1)}, bf16[2752,128]{1,0:T(8,128)(2,1)S(1)}, u32[]{:S(2)}, u32[]{:S(2)}) collective-permute-start(bf16[2752,128]{1,0:T(8,128)(2,1)} %bitcast.18.w0), channel_id=1, source_target_pairs={{0,32},{32,64},{64,96},{96,0},{1,33},{33,65},{65,97},{97,1},{2,34}... | collective-permute-start | bytes 2113544 | tf_op jit(solution)/shard_map/ppermute | solution.py:42
  50.6 2.2 %collective-permute-start.4 = (bf16[2752,128]{1,0:T(8,128)(2,1)}, bf16[2752,128]{1,0:T(8,128)(2,1)S(1)}, u32[]{:S(2)}, u32[]{:S(2)}) collective-permute-start(bf16[2752,128]{1,0:T(8,128)(2,1)} %bitcast.18.w0), channel_id=1, source_target_pairs={{0,96},{32,0},{64,32},{96,64},{1,97},{33,1},{65,33},{97,65},{2,98}... | collective-permute-start | bytes 2113544 | tf_op jit(solution)/shard_map/ppermute | solution.py:42
  53.6 3.9 %collective-permute-done.1.c = bf16[3008,128]{1,0:T(8,128)(2,1)} collective-permute-done((bf16[3008,128]{1,0:T(8,128)(2,1)}, bf16[3008,128]{1,0:T(8,128)(2,1)}, u32[]{:S(2)}, u32[]{:S(2)}) %collective-permute-start.1) | collective-permute-done | bytes 770080 | tf_op jit(solution)/shard_map/ppermute | solution.py:42
  59.7 4.6 %shard_map.190 = (f32[2752,128]{1,0:T(8,128)}, f32[2752,128]{1,0:T(8,128)}, f32[2752,128]{1,0:T(8,128)}) custom-call(bf16[512,128]{1,0:T(8,128)(2,1)} %pad_maximum_fusion.4.left, bf16[3008,128]{1,0:T(8,128)(2,1)} %get-tuple-element.92.a, bf16[3008,128]{1,0:T(8,128)(2,1)} %collective-permute-done.b, bf16[3008,128]{1,0:T(8,128)(2,1)} %collective-permute-done.1.c, ...), custom_call_target="tpu_custom_call" | custom-call | flops 1048576 | bytes 8388608 | tf_op jit(solution)/shard_map/pallas_call | solution.py:378
  64.4 8.5 %collective-permute-done.3.w1 = bf16[2752,128]{1,0:T(8,128)(2,1)S(1)} collective-permute-done((bf16[2752,128]{1,0:T(8,128)(2,1)}, bf16[2752,128]{1,0:T(8,128)(2,1)S(1)}, u32[]{:S(2)}, u32[]{:S(2)}) %collective-permute-start.3) | collective-permute-done | bytes 704544 | tf_op jit(solution)/shard_map/ppermute | solution.py:42
  74.7 2.1 %collective-permute-start.6 = (bf16[64,4096]{1,0:T(8,128)(2,1)S(1)}, bf16[64,4096]{1,0:T(8,128)(2,1)S(1)}, u32[]{:S(2)}, u32[]{:S(2)}) collective-permute-start(bf16[64,4096]{1,0:T(8,128)(2,1)S(1)} %copy-done.11), channel_id=1, source_target_pairs={{0,96},{32,0},{64,32},{96,64},{1,97},{33,1},{65,33},{97,65},{2,98}... | collective-permute-start | bytes 1572872 | tf_op jit(solution)/shard_map/ppermute | solution.py:42
  76.8 18.7 %shard_map.191 = (bf16[2,528,512]{2,1,0:T(8,128)(2,1)}, bf16[2,528,512]{2,1,0:T(8,128)(2,1)}) custom-call(s32[2]{0:T(128)} %get-tuple-element.102.where, s32[4,1,512]{2,1,0:T(1,128)} %reshape.106.codes, bf16[8,480,128]{2,1,0:T(8,128)(2,1)} %copy-done.7, bf16[128,2752]{1,0:T(8,128)(2,1)} %copy.43.right, bf16[480,128]{1,0:T(8,128)(2,1)} %copy-done.12, ...), custom_call_target="tpu_custom_call" | custom-call | flops 8657043456 | bytes 8388608 | tf_op jit(solution)/shard_map/pallas_call | solution.py:237
  95.5 1.5 %collective-permute-start.7 = (bf16[2,528,512]{2,1,0:T(8,128)(2,1)}, bf16[2,528,512]{2,1,0:T(8,128)(2,1)S(1)}, u32[]{:S(2)}, u32[]{:S(2)}) collective-permute-start(bf16[2,528,512]{2,1,0:T(8,128)(2,1)} %get-tuple-element.52), channel_id=1, source_target_pairs={{0,8},{8,0},{1,9},{9,1},{2,10},{10,2},{3,11},{11,3},{4,12},{12,4},... | collective-permute-start | bytes 3244040 | tf_op jit(solution)/shard_map/ppermute | solution.py:42
  97.1 2.5 %collective-permute-done.7.theirs = bf16[2,528,512]{2,1,0:T(8,128)(2,1)S(1)} collective-permute-done((bf16[2,528,512]{2,1,0:T(8,128)(2,1)}, bf16[2,528,512]{2,1,0:T(8,128)(2,1)S(1)}, u32[]{:S(2)}, u32[]{:S(2)}) %collective-permute-start.7) | collective-permute-done | bytes 1081376 | tf_op jit(solution)/shard_map/ppermute | solution.py:42
  100.6 2.5 %shard_map.192 = bf16[16,80,512]{2,1,0:T(8,128)(2,1)} custom-call(bf16[2,528,512]{2,1,0:T(8,128)(2,1)} %get-tuple-element.51.mine, bf16[2,528,512]{2,1,0:T(8,128)(2,1)} %copy-done.6), custom_call_target="tpu_custom_call" | custom-call | flops 1048576 | bytes 4194304 | tf_op jit(solution)/shard_map/pallas_call | solution.py:284
  103.1 6.5 %all-to-all-start.2 = ((bf16[16,80,512]{2,1,0:T(8,128)(2,1)}), bf16[16,80,512]{2,1,0:T(8,128)(2,1)S(1)}, u32[]{:S(2)}, u32[]{:S(2)}) async-start(bf16[16,80,512]{2,1,0:T(8,128)(2,1)} %shard_map.192), calls=%async_computation.2 | async-start | bytes 2621440 | tf_op jit(solution)/shard_map/all_to_all | solution.py:46
  110.8 3.0 %collective-permute-start.9 = (bf16[32,4096]{1,0:T(8,128)(2,1)S(1)}, bf16[32,4096]{1,0:T(8,128)(2,1)S(1)}, u32[]{:S(2)}, u32[]{:S(2)}) collective-permute-start(bf16[32,4096]{1,0:T(8,128)(2,1)S(1)} %slice.59), channel_id=1, source_target_pairs={{0,96},{32,0},{64,32},{96,64},{1,97},{33,1},{65,33},{97,65},{2,98}... | collective-permute-start | bytes 786440 | tf_op jit(solution)/shard_map/ppermute | solution.py:42
  113.7 5.5 %collective-permute-done.8.c = bf16[32,4096]{1,0:T(8,128)(2,1)S(1)} collective-permute-done((bf16[32,4096]{1,0:T(8,128)(2,1)S(1)}, bf16[32,4096]{1,0:T(8,128)(2,1)S(1)}, u32[]{:S(2)}, u32[]{:S(2)}) %collective-permute-start.8) | collective-permute-done | bytes 262176 | tf_op jit(solution)/shard_map/ppermute | solution.py:42
  122.9 7.8 %shard_map.194 = (f32[2752,128]{1,0:T(8,128)}, f32[2752,128]{1,0:T(8,128)}, f32[2752,128]{1,0:T(8,128)}) custom-call(s32[1]{0:T(128)} %bitcast.2.core, bf16[512,128]{1,0:T(8,128)(2,1)} %pad_maximum_fusion.5.left, bf16[128,4096]{1,0:T(8,128)(2,1)} %copy-done.1, bf16[64,4096]{1,0:T(8,128)(2,1)} %copy-done.4, bf16[64,4096]{1,0:T(8,128)(2,1)} %copy-done.5, ...), custom_call_target="tpu_custom_call" | custom-call | flops 1048576 | bytes 8388608 | tf_op jit(solution)/shard_map/pallas_call | solution.py:436
  131.8 2.9 %shard_map.193 = bf16[64,4096]{1,0:T(8,128)(2,1)} custom-call(s32[1]{0:T(128)} %bitcast.col, bf16[2,8,80,512]{3,2,1,0:T(8,128)(2,1)} %bitcast.48, bf16[2,8,80,512]{3,2,1,0:T(8,128)(2,1)} %bitcast.49, s32[64,1]{1,0:T(8,128)} %constant_dynamic-slice_fusion.2.codes, bf16[156,4096]{1,0:T(8,128)(2,1)} %table.3, bf16[4,4096]{1,0:T(4,128)(2,1)} %constant_dynamic-slice_fusion.1.right), custom_call_target="tpu_custom_call" | custom-call | flops 1048576 | bytes 4194304 | tf_op jit(solution)/shard_map/pallas_call | solution.py:332
  (98 shorter events, 27.7 us)
Async XLA Ops:
  6.4 6.3 %copy-start.19 = (f32[512]{0:T(512)S(1)}, f32[512]{0:T(512)}, u32[]{:S(2)}) copy-start(f32[512]{0:T(512)} %param.16) | copy-start | bytes 6148
  6.4 9.1 %copy-start.13 = (bf16[128,344]{0,1:T(8,128)(2,1)S(1)}, bf16[128,344]{0,1:T(8,128)(2,1)}, u32[]{:S(2)}) copy-start(bf16[128,344]{0,1:T(8,128)(2,1)} %param.22) | copy-start | bytes 264196
  6.4 35.9 %all-to-all-start = ((bf16[8,1184,128]{2,1,0:T(8,128)(2,1)}), bf16[8,1184,128]{2,1,0:T(8,128)(2,1)S(1)}, u32[]{:S(2)}, u32[]{:S(2)}) async-start(bf16[8,1184,128]{2,1,0:T(8,128)(2,1)} %shard_map.189), calls=%async_computation | async-start | bytes 4849664 | tf_op jit(solution)/shard_map/all_to_all | solution.py:46
  19.7 8.6 %copy-start.14 = (bf16[128,344]{0,1:T(8,128)(2,1)S(1)}, bf16[128,344]{0,1:T(8,128)(2,1)}, u32[]{:S(2)}) copy-start(bf16[128,344]{0,1:T(8,128)(2,1)} %param.22) | copy-start | bytes 264196
  19.7 33.2 %collective-permute-start.2 = (bf16[3008,128]{1,0:T(8,128)(2,1)}, bf16[3008,128]{1,0:T(8,128)(2,1)}, u32[]{:S(2)}, u32[]{:S(2)}) collective-permute-start(bf16[3008,128]{1,0:T(8,128)(2,1)} %get-tuple-element.94), channel_id=1, source_target_pairs={{0,64},{32,96},{64,0},{96,32},{1,65},{33,97},{65,1},{97,33},{2,66}... | collective-permute-start | bytes 2310152 | tf_op jit(solution)/shard_map/ppermute | solution.py:42
  23.4 34.1 %collective-permute-start.1 = (bf16[3008,128]{1,0:T(8,128)(2,1)}, bf16[3008,128]{1,0:T(8,128)(2,1)}, u32[]{:S(2)}, u32[]{:S(2)}) collective-permute-start(bf16[3008,128]{1,0:T(8,128)(2,1)} %get-tuple-element.93), channel_id=1, source_target_pairs={{0,96},{32,0},{64,32},{96,64},{1,97},{33,1},{65,33},{97,65},{2,98}... | collective-permute-start | bytes 2310152 | tf_op jit(solution)/shard_map/ppermute | solution.py:42
  23.8 34.5 %collective-permute-start = (bf16[3008,128]{1,0:T(8,128)(2,1)}, bf16[3008,128]{1,0:T(8,128)(2,1)}, u32[]{:S(2)}, u32[]{:S(2)}) collective-permute-start(bf16[3008,128]{1,0:T(8,128)(2,1)} %get-tuple-element.95), channel_id=1, source_target_pairs={{0,32},{32,64},{64,96},{96,0},{1,33},{33,65},{65,97},{97,1},{2,34}... | collective-permute-start | bytes 2310152 | tf_op jit(solution)/shard_map/ppermute | solution.py:42
  32.0 12.1 %copy-start.1 = (bf16[128,4096]{1,0:T(8,128)(2,1)}, bf16[128,4096]{1,0:T(8,128)(2,1)S(1)}, u32[]{:S(2)}) copy-start(bf16[128,4096]{1,0:T(8,128)(2,1)S(1)} %multiply_convert_fusion.own) | copy-start | bytes 3145732
  44.1 28.7 %all-to-all-start.1 = ((bf16[8,480,128]{2,1,0:T(8,128)(2,1)}), bf16[8,480,128]{2,1,0:T(8,128)(2,1)S(1)}, u32[]{:S(2)}, u32[]{:S(2)}) async-start(bf16[8,480,128]{2,1,0:T(8,128)(2,1)} %broadcast_in_dim.16), calls=%async_computation.1 | async-start | bytes 1966080 | tf_op jit(solution)/shard_map/all_to_all | solution.py:46
  49.1 23.7 %collective-permute-start.3 = (bf16[2752,128]{1,0:T(8,128)(2,1)}, bf16[2752,128]{1,0:T(8,128)(2,1)S(1)}, u32[]{:S(2)}, u32[]{:S(2)}) collective-permute-start(bf16[2752,128]{1,0:T(8,128)(2,1)} %bitcast.18.w0), channel_id=1, source_target_pairs={{0,32},{32,64},{64,96},{96,0},{1,33},{33,65},{65,97},{97,1},{2,34}... | collective-permute-start | bytes 2113544 | tf_op jit(solution)/shard_map/ppermute | solution.py:42
  50.6 22.2 %collective-permute-start.4 = (bf16[2752,128]{1,0:T(8,128)(2,1)}, bf16[2752,128]{1,0:T(8,128)(2,1)S(1)}, u32[]{:S(2)}, u32[]{:S(2)}) collective-permute-start(bf16[2752,128]{1,0:T(8,128)(2,1)} %bitcast.18.w0), channel_id=1, source_target_pairs={{0,96},{32,0},{64,32},{96,64},{1,97},{33,1},{65,33},{97,65},{2,98}... | collective-permute-start | bytes 2113544 | tf_op jit(solution)/shard_map/ppermute | solution.py:42
  59.7 14.0 %copy-start.11 = (bf16[64,4096]{1,0:T(8,128)(2,1)S(1)}, bf16[64,4096]{1,0:T(8,128)(2,1)}, u32[]{:S(2)}) copy-start(bf16[64,4096]{1,0:T(8,128)(2,1)} %constant_dynamic-slice_fusion) | copy-start | bytes 1572868
  73.7 21.8 %collective-permute-start.5 = (bf16[64,4096]{1,0:T(8,128)(2,1)S(1)}, bf16[64,4096]{1,0:T(8,128)(2,1)S(1)}, u32[]{:S(2)}, u32[]{:S(2)}) collective-permute-start(bf16[64,4096]{1,0:T(8,128)(2,1)S(1)} %copy-done.11), channel_id=1, source_target_pairs={{0,32},{32,64},{64,96},{96,0},{1,33},{33,65},{65,97},{97,1},{2,34}... | collective-permute-start | bytes 1572872 | tf_op jit(solution)/shard_map/ppermute | solution.py:42
  74.7 20.8 %collective-permute-start.6 = (bf16[64,4096]{1,0:T(8,128)(2,1)S(1)}, bf16[64,4096]{1,0:T(8,128)(2,1)S(1)}, u32[]{:S(2)}, u32[]{:S(2)}) collective-permute-start(bf16[64,4096]{1,0:T(8,128)(2,1)S(1)} %copy-done.11), channel_id=1, source_target_pairs={{0,96},{32,0},{64,32},{96,64},{1,97},{33,1},{65,33},{97,65},{2,98}... | collective-permute-start | bytes 1572872 | tf_op jit(solution)/shard_map/ppermute | solution.py:42
  95.5 14.1 %copy-start.4 = (bf16[64,4096]{1,0:T(8,128)(2,1)}, bf16[64,4096]{1,0:T(8,128)(2,1)S(1)}, u32[]{:S(2)}) copy-start(bf16[64,4096]{1,0:T(8,128)(2,1)S(1)} %collective-permute-done.5.a) | copy-start | bytes 1572868
  95.5 14.9 %copy-start.5 = (bf16[64,4096]{1,0:T(8,128)(2,1)}, bf16[64,4096]{1,0:T(8,128)(2,1)S(1)}, u32[]{:S(2)}) copy-start(bf16[64,4096]{1,0:T(8,128)(2,1)S(1)} %collective-permute-done.6.b) | copy-start | bytes 1572868
  95.5 4.0 %collective-permute-start.7 = (bf16[2,528,512]{2,1,0:T(8,128)(2,1)}, bf16[2,528,512]{2,1,0:T(8,128)(2,1)S(1)}, u32[]{:S(2)}, u32[]{:S(2)}) collective-permute-start(bf16[2,528,512]{2,1,0:T(8,128)(2,1)} %get-tuple-element.52), channel_id=1, source_target_pairs={{0,8},{8,0},{1,9},{9,1},{2,10},{10,2},{3,11},{11,3},{4,12},{12,4},... | collective-permute-start | bytes 3244040 | tf_op jit(solution)/shard_map/ppermute | solution.py:42
  103.1 27.6 %all-to-all-start.2 = ((bf16[16,80,512]{2,1,0:T(8,128)(2,1)}), bf16[16,80,512]{2,1,0:T(8,128)(2,1)S(1)}, u32[]{:S(2)}, u32[]{:S(2)}) async-start(bf16[16,80,512]{2,1,0:T(8,128)(2,1)} %shard_map.192), calls=%async_computation.2 | async-start | bytes 2621440 | tf_op jit(solution)/shard_map/all_to_all | solution.py:46
  109.7 11.4 %collective-permute-start.10 = (bf16[64,4096]{1,0:T(8,128)(2,1)S(1)}, bf16[64,4096]{1,0:T(8,128)(2,1)S(1)}, u32[]{:S(2)}, u32[]{:S(2)}) collective-permute-start(bf16[64,4096]{1,0:T(8,128)(2,1)S(1)} %collective-permute-done.5.a), channel_id=1, source_target_pairs={{0,8},{8,0},{1,9},{9,1},{2,10},{10,2},{3,11},{11,3},{4,12},{12,4},... | collective-permute-start | bytes 1572872 | tf_op jit(solution)/shard_map/ppermute | solution.py:42
  110.4 8.9 %collective-permute-start.8 = (bf16[32,4096]{1,0:T(8,128)(2,1)S(1)}, bf16[32,4096]{1,0:T(8,128)(2,1)S(1)}, u32[]{:S(2)}, u32[]{:S(2)}) collective-permute-start(bf16[32,4096]{1,0:T(8,128)(2,1)S(1)} %slice.58), channel_id=1, source_target_pairs={{0,32},{32,64},{64,96},{96,0},{1,33},{33,65},{65,97},{97,1},{2,34}... | collective-permute-start | bytes 786440 | tf_op jit(solution)/shard_map/ppermute | solution.py:42
  110.4 10.7 %collective-permute-start.11 = (bf16[64,4096]{1,0:T(8,128)(2,1)S(1)}, bf16[64,4096]{1,0:T(8,128)(2,1)S(1)}, u32[]{:S(2)}, u32[]{:S(2)}) collective-permute-start(bf16[64,4096]{1,0:T(8,128)(2,1)S(1)} %collective-permute-done.6.b), channel_id=1, source_target_pairs={{0,8},{8,0},{1,9},{9,1},{2,10},{10,2},{3,11},{11,3},{4,12},{12,4},... | collective-permute-start | bytes 1572872 | tf_op jit(solution)/shard_map/ppermute | solution.py:42
  110.8 9.5 %collective-permute-start.9 = (bf16[32,4096]{1,0:T(8,128)(2,1)S(1)}, bf16[32,4096]{1,0:T(8,128)(2,1)S(1)}, u32[]{:S(2)}, u32[]{:S(2)}) collective-permute-start(bf16[32,4096]{1,0:T(8,128)(2,1)S(1)} %slice.59), channel_id=1, source_target_pairs={{0,96},{32,0},{64,32},{96,64},{1,97},{33,1},{65,33},{97,65},{2,98}... | collective-permute-start | bytes 786440 | tf_op jit(solution)/shard_map/ppermute | solution.py:42
  119.2 2.2 %collective-permute-start.12 = (bf16[32,4096]{1,0:T(8,128)(2,1)S(1)}, bf16[32,4096]{1,0:T(8,128)(2,1)S(1)}, u32[]{:S(2)}, u32[]{:S(2)}) collective-permute-start(bf16[32,4096]{1,0:T(8,128)(2,1)S(1)} %collective-permute-done.8.c), channel_id=1, source_target_pairs={{0,8},{8,0},{1,9},{9,1},{2,10},{10,2},{3,11},{11,3},{4,12},{12,4},... | collective-permute-start | bytes 786440 | tf_op jit(solution)/shard_map/ppermute | solution.py:42
  120.3 1.5 %collective-permute-start.13 = (bf16[32,4096]{1,0:T(8,128)(2,1)S(1)}, bf16[32,4096]{1,0:T(8,128)(2,1)S(1)}, u32[]{:S(2)}, u32[]{:S(2)}) collective-permute-start(bf16[32,4096]{1,0:T(8,128)(2,1)S(1)} %collective-permute-done.9.d), channel_id=1, source_target_pairs={{0,8},{8,0},{1,9},{9,1},{2,10},{10,2},{3,11},{11,3},{4,12},{12,4},... | collective-permute-start | bytes 786440 | tf_op jit(solution)/shard_map/ppermute | solution.py:42
  (17 other events, 48.9 us)

commit v4 on v3

--- a/solution.py
+++ b/solution.py
@@ -59,7 +59,7 @@
 
 
 def silu(value):
-    half = 0.5 * value
+    half = (0.5 * value).astype(BF)
     return half + half * jnp.tanh(half)
 
 
@@ -292,7 +292,7 @@
     )(mine, theirs)
 
 
-def final_kernel(col, got, tails, codes, table, right, out, own):
+def final_kernel(col, got, tails, features, right, out, own):
     rows = out.shape[0]
     halves, parts, _, width = got.shape
     slots = right.shape[0]
@@ -307,8 +307,6 @@
         mine = jnp.where(lane == line + col[0] * rows, probe, 0.0)
         own[...] = noise_scale * jnp.sum(mine, axis=1, keepdims=True)
 
-    hot = lax.broadcasted_iota(jnp.int32, (rows, table.shape[0]), 1) == codes[...]
-    hot = jnp.where(hot, 1.0, 0.0).astype(BF)
     for part in range(parts):
         cols = slice(part * width, (part + 1) * width)
         product = got[0, part, 0:rows, :].astype(F32)
@@ -321,11 +319,11 @@
             ],
             axis=0,
         )
-        residual = jnp.dot(hot, table[:, cols], preferred_element_type=F32)
+        residual = features[:, cols].astype(F32)
         out[:, cols] = (residual + product + own[...] * spread).astype(BF)
 
 
-def final_sum(col, got, codes, table, right):
+def final_sum(col, got, features, right):
     halves, parts, height, width = got.shape
     rows = height - TAIL
     some = 4
@@ -339,8 +337,7 @@
                 pl.BlockSpec(
                     (halves, parts, TAIL, width), lambda i, c: (0, 0, rows // TAIL, 0)
                 ),
-                whole(codes),
-                pl.BlockSpec((table.shape[0], some * width), lambda i, c: (0, i)),
+                pl.BlockSpec((rows, some * width), lambda i, c: (0, i)),
                 pl.BlockSpec((right.shape[0], some * width), lambda i, c: (0, i)),
             ],
             out_specs=pl.BlockSpec((rows, some * width), lambda i, c: (0, i)),
@@ -349,7 +346,7 @@
         out_shape=jax.ShapeDtypeStruct((rows, parts * width), BF),
         compiler_params=params(),
         cost_estimate=cost(1 << 20, 4 << 20),
-    )(col, got, got, codes, table, right)
+    )(col, got, got, features, right)
 
 
 def slot_order(pop):
@@ -526,13 +523,15 @@
     share_slots = share_rows // per_member
     place_index = lax.axis_index(ROW + ("col",))
     mine_codes = lax.dynamic_slice_in_dim(
-        obs_ids.reshape(row_count, 1), place_index * share_rows, share_rows, 0
-    )
+        obs_ids, place_index * share_slots, share_slots, 0
+    ).reshape(share_rows, 1)
+    hot = (mine_codes == jnp.arange(embed_table.shape[0])[None, :]).astype(BF)
+    features = jnp.dot(hot, embed_table, preferred_element_type=F32).astype(BF)
     mine_right = lax.dynamic_slice_in_dim(down_right, place_index * share_slots, share_slots, 0)
     half = member_count // 2
     down_own = lax.dynamic_slice_in_dim(down_weighted, core * half, half, 0)
-    got, own_right, mine_codes, mine_right, down_own = together(
-        got, own_right, mine_codes, mine_right, down_own
+    got, own_right, features, mine_right, down_own = together(
+        got, own_right, features, mine_right, down_own
     )
 
     height = got.shape[1] - 2 * SHARE_ROWS
@@ -567,7 +566,7 @@
     theirs = shifted(other, "core", 1)
     got = exchange(pieces(mine, theirs, cols), ("xh", "col"))
     got = got.reshape((2, cols) + got.shape[1:])
-    block_out = final_sum(col_ref, got, mine_codes, embed_table, mine_right)
+    block_out = final_sum(col_ref, got, features, mine_right)
 
     down_parts = list(down_near) + list(
         ring_second(down_near[0][: half // 2], down_near[1][half // 2 :])

time: 136 us -> 134 us (0.985)
  local copies, waits for them, and re-layouts: 20.9 us -> 17.5 us
  waiting for transfers between devices: 26.7 us -> 29.3 us
  Pallas kernels: 41.7 us -> 39.8 us
    all_to_all x3, waiting for transfers between devices: 5.52 us -> 7.2 us  [exchange(): return lax.all_to_all(value, axis, split, 0, tiled=True)]
    reshape x1 -> x0, local copies, waits for them, and re-layouts: 1.55 us -> none  [per_device(): obs_ids.reshape(row_count, 1)]
    pallas_call x1, Pallas kernels: 18.7 us -> 17.3 us  [hidden_product(): pl.pallas_call(hidden_kernel, grid_spec=pltpu.PrefetchScalarGridSpec(num_...]
    unnamed x52 -> x56, local copies, waits for them, and re-layouts: 6.85 us -> 6.25 us
  transfers between devices with their start and end apart: 17 -> 17, of which waited for: 7 -> 7; matrix products, arithmetic and copies ran while one was open for 18% -> 17% of each run, Pallas kernels for 23% -> 22%
where the time goes in v4:
time: 134 us; the launch traced here: 133 us
  Pallas kernels  39.8 us (30%)
  starting transfers between devices  34.6 us (26%)
  waiting for transfers between devices  29.3 us (22%)
  local copies, waits for them, and re-layouts  17.5 us (13%)
  other arithmetic  8.11 us (6%)
  between operations  2.37 us (2%)
    ppermute x14, waiting for transfers between devices, shifted(): lax.ppermute(value, axis, [(i, (i + step) % size) for i in range(size)])  22.1 us
    ppermute x14, starting transfers between devices, shifted(): lax.ppermute(value, axis, [(i, (i + step) % size) for i in range(size)])  18.2 us
    pallas_call x1, Pallas kernels, hidden_product(): pl.pallas_call(hidden_kernel, grid_spec=pltpu.PrefetchScalarGridSpec(num_...  17.3 us
    all_to_all x3, starting transfers between devices, exchange(): return lax.all_to_all(value, axis, split, 0, tiled=True)  16.5 us
    pallas_call x1, Pallas kernels, down_adam(): pl.pallas_call(down_kernel, grid_spec=pltpu.PrefetchScalarGridSpec(num_sc...  7.78 us
    all_to_all x3, waiting for transfers between devices, exchange(): return lax.all_to_all(value, axis, split, 0, tiled=True)  7.2 us
    unnamed x56, local copies, waits for them, and re-layouts  6.25 us
    pallas_call x1, Pallas kernels, table_products(): pl.pallas_call(table_kernel, grid_spec=pltpu.PrefetchScalarGridSpec(num_s...  5.17 us
  transfers between devices with their start and end apart: 17, of which 7 were waited for; matrix products, arithmetic and copies ran while one was open for 17% of the time, Pallas kernels for 22%

profile of v4, /device:TPU:1, one launch (start us, length us, event | category | flops | bytes accessed | tf_op | source)
XLA Modules:
  0.0 132.9 jit_solution(14032621581116449518)
XLA Ops:
  1.2 5.2 %shard_map.189 = bf16[8,1184,128]{2,1,0:T(8,128)(2,1)} custom-call(s32[2]{0:T(128)} %get-tuple-element.103.where, bf16[156,4096]{1,0:T(8,128)(2,1)} %table.1, bf16[8,344,512]{2,1,0:T(8,128)(2,1)} %bitcast.51, bf16[128,512]{1,0:T(8,128)(2,1)} %left.1, bf16[344,4096]{1,0:T(8,128)(2,1)} %rest_7_.1, bf16[344,4096]{1,0:T(8,128)(2,1)} %rest_7_.1, ...), custom_call_target="tpu_custom_call" | custom-call | flops 1048576 | bytes 1048576 | tf_op jit(solution)/shard_map/pallas_call | solution.py:109
  6.4 6.1 %all-to-all-start = ((bf16[8,1184,128]{2,1,0:T(8,128)(2,1)}), bf16[8,1184,128]{2,1,0:T(8,128)(2,1)S(1)}, u32[]{:S(2)}, u32[]{:S(2)}) async-start(bf16[8,1184,128]{2,1,0:T(8,128)(2,1)} %shard_map.189), calls=%async_computation | async-start | bytes 4849664 | tf_op jit(solution)/shard_map/all_to_all | solution.py:46
  17.6 2.0 %pad_maximum_fusion.3 = (bf16[3008,128]{1,0:T(8,128)(2,1)}, bf16[3008,128]{1,0:T(8,128)(2,1)}, bf16[3008,128]{1,0:T(8,128)(2,1)}, bf16[3008,128]{1,0:T(8,128)(2,1)}) fusion(bf16[256,128]{1,0:T(8,128)(2,1)S(1)} %get-tuple-element.98, bf16[2752,128]{1,0:T(8,128)(2,1)S(1)} %fusion, bf16[256,128]{1,0:T(8,128)(2,1)S(1)} %get-tuple-element.100, ...), kind=kLoop, calls=%fused_computation.7 | loop fusion | flops 5005312 | bytes 4046848 | tf_op jit(solution)/shard_map/concatenate | solution.py:519
  19.6 3.6 %collective-permute-start.2 = (bf16[3008,128]{1,0:T(8,128)(2,1)}, bf16[3008,128]{1,0:T(8,128)(2,1)}, u32[]{:S(2)}, u32[]{:S(2)}) collective-permute-start(bf16[3008,128]{1,0:T(8,128)(2,1)} %get-tuple-element.94), channel_id=1, source_target_pairs={{0,64},{32,96},{64,0},{96,32},{1,65},{33,97},{65,1},{97,33},{2,66}... | collective-permute-start | bytes 2310152 | tf_op jit(solution)/shard_map/ppermute | solution.py:42
  27.6 1.6 %constant_dynamic-slice_fusion.3.own_right = bf16[128,344]{1,0:T(8,128)(2,1)} fusion(bf16[128,2752]{1,0:T(8,128)(2,1)} %copy.42.right, s32[]{:T(128)S(6)} %select_n.46), kind=kLoop, calls=%fused_computation.27 | loop fusion | bytes 176132 | tf_op jit(solution)/shard_map/dynamic_slice | solution.py:521
  29.3 1.5 %constant_dynamic-slice_fusion.1.right = bf16[4,4096]{1,0:T(4,128)(2,1)} fusion(bf16[128,4096]{1,0:T(8,128)(2,1)} %param.23, s32[]{:T(128)S(6)} %select_n.47), kind=kLoop, calls=%fused_computation.25 | loop fusion | bytes 65540 | tf_op jit(solution)/shard_map/dynamic_slice | solution.py:530
  30.7 1.6 %multiply_convert_fusion.own = bf16[128,4096]{1,0:T(8,128)(2,1)S(1)} fusion(bf16[128,4096]{1,0:T(8,128)(2,1)} %param.23, f32[128]{0:T(128)S(1)} %divide_multiply_fusion), kind=kLoop, calls=%fused_computation.1 | loop fusion | flops 1572864 | bytes 2097664 | tf_op jit(solution)/shard_map/convert_element_type | solution.py:518
  35.1 7.2 %all-to-all-done = bf16[8,1184,128]{2,1,0:T(8,128)(2,1)S(1)} async-done(((bf16[8,1184,128]{2,1,0:T(8,128)(2,1)}), bf16[8,1184,128]{2,1,0:T(8,128)(2,1)S(1)}, u32[]{:S(2)}, u32[]{:S(2)}) %all-to-all-start) | async-done | bytes 2424864 | tf_op jit(solution)/shard_map/all_to_all | solution.py:46
  43.5 3.7 %all-to-all-start.1 = ((bf16[8,480,128]{2,1,0:T(8,128)(2,1)}), bf16[8,480,128]{2,1,0:T(8,128)(2,1)S(1)}, u32[]{:S(2)}, u32[]{:S(2)}) async-start(bf16[8,480,128]{2,1,0:T(8,128)(2,1)} %broadcast_in_dim.16), calls=%async_computation.1 | async-start | bytes 1966080 | tf_op jit(solution)/shard_map/all_to_all | solution.py:46
  48.5 1.5 %collective-permute-start.3 = (bf16[2752,128]{1,0:T(8,128)(2,1)}, bf16[2752,128]{1,0:T(8,128)(2,1)S(1)}, u32[]{:S(2)}, u32[]{:S(2)}) collective-permute-start(bf16[2752,128]{1,0:T(8,128)(2,1)} %bitcast.18.w0), channel_id=1, source_target_pairs={{0,32},{32,64},{64,96},{96,0},{1,33},{33,65},{65,97},{97,1},{2,34}... | collective-permute-start | bytes 2113544 | tf_op jit(solution)/shard_map/ppermute | solution.py:42
  50.0 2.2 %collective-permute-start.4 = (bf16[2752,128]{1,0:T(8,128)(2,1)}, bf16[2752,128]{1,0:T(8,128)(2,1)S(1)}, u32[]{:S(2)}, u32[]{:S(2)}) collective-permute-start(bf16[2752,128]{1,0:T(8,128)(2,1)} %bitcast.18.w0), channel_id=1, source_target_pairs={{0,96},{32,0},{64,32},{96,64},{1,97},{33,1},{65,33},{97,65},{2,98}... | collective-permute-start | bytes 2113544 | tf_op jit(solution)/shard_map/ppermute | solution.py:42
  53.0 4.4 %collective-permute-done.1.c = bf16[3008,128]{1,0:T(8,128)(2,1)} collective-permute-done((bf16[3008,128]{1,0:T(8,128)(2,1)}, bf16[3008,128]{1,0:T(8,128)(2,1)}, u32[]{:S(2)}, u32[]{:S(2)}) %collective-permute-start.1) | collective-permute-done | bytes 770080 | tf_op jit(solution)/shard_map/ppermute | solution.py:42
  59.6 4.6 %shard_map.190 = (f32[2752,128]{1,0:T(8,128)}, f32[2752,128]{1,0:T(8,128)}, f32[2752,128]{1,0:T(8,128)}) custom-call(bf16[512,128]{1,0:T(8,128)(2,1)} %pad_maximum_fusion.4.left, bf16[3008,128]{1,0:T(8,128)(2,1)} %get-tuple-element.92.a, bf16[3008,128]{1,0:T(8,128)(2,1)} %collective-permute-done.b, bf16[3008,128]{1,0:T(8,128)(2,1)} %collective-permute-done.1.c, ...), custom_call_target="tpu_custom_call" | custom-call | flops 1048576 | bytes 8388608 | tf_op jit(solution)/shard_map/pallas_call | solution.py:375
  64.2 8.5 %collective-permute-done.3.w1 = bf16[2752,128]{1,0:T(8,128)(2,1)S(1)} collective-permute-done((bf16[2752,128]{1,0:T(8,128)(2,1)}, bf16[2752,128]{1,0:T(8,128)(2,1)S(1)}, u32[]{:S(2)}, u32[]{:S(2)}) %collective-permute-start.3) | collective-permute-done | bytes 704544 | tf_op jit(solution)/shard_map/ppermute | solution.py:42
  74.5 2.1 %collective-permute-start.6 = (bf16[64,4096]{1,0:T(8,128)(2,1)S(1)}, bf16[64,4096]{1,0:T(8,128)(2,1)S(1)}, u32[]{:S(2)}, u32[]{:S(2)}) collective-permute-start(bf16[64,4096]{1,0:T(8,128)(2,1)S(1)} %copy-done.11), channel_id=1, source_target_pairs={{0,96},{32,0},{64,32},{96,64},{1,97},{33,1},{65,33},{97,65},{2,98}... | collective-permute-start | bytes 1572872 | tf_op jit(solution)/shard_map/ppermute | solution.py:42
  76.6 17.3 %shard_map.191 = (bf16[2,528,512]{2,1,0:T(8,128)(2,1)}, bf16[2,528,512]{2,1,0:T(8,128)(2,1)}) custom-call(s32[2]{0:T(128)} %get-tuple-element.102.where, s32[4,1,512]{2,1,0:T(1,128)} %reshape.104.codes, bf16[8,480,128]{2,1,0:T(8,128)(2,1)} %copy-done.7, bf16[128,2752]{1,0:T(8,128)(2,1)} %copy.42.right, bf16[480,128]{1,0:T(8,128)(2,1)} %copy-done.12, ...), custom_call_target="tpu_custom_call" | custom-call | flops 8657043456 | bytes 8388608 | tf_op jit(solution)/shard_map/pallas_call | solution.py:237
  93.9 1.5 %collective-permute-start.7 = (bf16[2,528,512]{2,1,0:T(8,128)(2,1)}, bf16[2,528,512]{2,1,0:T(8,128)(2,1)S(1)}, u32[]{:S(2)}, u32[]{:S(2)}) collective-permute-start(bf16[2,528,512]{2,1,0:T(8,128)(2,1)} %get-tuple-element.52), channel_id=1, source_target_pairs={{0,8},{8,0},{1,9},{9,1},{2,10},{10,2},{3,11},{11,3},{4,12},{12,4},... | collective-permute-start | bytes 3244040 | tf_op jit(solution)/shard_map/ppermute | solution.py:42
  95.4 2.5 %collective-permute-done.7.theirs = bf16[2,528,512]{2,1,0:T(8,128)(2,1)S(1)} collective-permute-done((bf16[2,528,512]{2,1,0:T(8,128)(2,1)}, bf16[2,528,512]{2,1,0:T(8,128)(2,1)S(1)}, u32[]{:S(2)}, u32[]{:S(2)}) %collective-permute-start.7) | collective-permute-done | bytes 1081376 | tf_op jit(solution)/shard_map/ppermute | solution.py:42
  99.0 2.5 %shard_map.192 = bf16[16,80,512]{2,1,0:T(8,128)(2,1)} custom-call(bf16[2,528,512]{2,1,0:T(8,128)(2,1)} %get-tuple-element.51.mine, bf16[2,528,512]{2,1,0:T(8,128)(2,1)} %copy-done.6), custom_call_target="tpu_custom_call" | custom-call | flops 1048576 | bytes 4194304 | tf_op jit(solution)/shard_map/pallas_call | solution.py:284
  101.5 6.7 %all-to-all-start.2 = ((bf16[16,80,512]{2,1,0:T(8,128)(2,1)}), bf16[16,80,512]{2,1,0:T(8,128)(2,1)S(1)}, u32[]{:S(2)}, u32[]{:S(2)}) async-start(bf16[16,80,512]{2,1,0:T(8,128)(2,1)} %shard_map.192), calls=%async_computation.2 | async-start | bytes 2621440 | tf_op jit(solution)/shard_map/all_to_all | solution.py:46
  109.1 2.9 %collective-permute-start.9 = (bf16[32,4096]{1,0:T(8,128)(2,1)S(1)}, bf16[32,4096]{1,0:T(8,128)(2,1)S(1)}, u32[]{:S(2)}, u32[]{:S(2)}) collective-permute-start(bf16[32,4096]{1,0:T(8,128)(2,1)S(1)} %slice.59), channel_id=1, source_target_pairs={{0,96},{32,0},{64,32},{96,64},{1,97},{33,1},{65,33},{97,65},{2,98}... | collective-permute-start | bytes 786440 | tf_op jit(solution)/shard_map/ppermute | solution.py:42
  112.1 5.9 %collective-permute-done.8.c = bf16[32,4096]{1,0:T(8,128)(2,1)S(1)} collective-permute-done((bf16[32,4096]{1,0:T(8,128)(2,1)S(1)}, bf16[32,4096]{1,0:T(8,128)(2,1)S(1)}, u32[]{:S(2)}, u32[]{:S(2)}) %collective-permute-start.8) | collective-permute-done | bytes 262176 | tf_op jit(solution)/shard_map/ppermute | solution.py:42
  121.5 7.8 %shard_map.194 = (f32[2752,128]{1,0:T(8,128)}, f32[2752,128]{1,0:T(8,128)}, f32[2752,128]{1,0:T(8,128)}) custom-call(s32[1]{0:T(128)} %bitcast.2.core, bf16[512,128]{1,0:T(8,128)(2,1)} %pad_maximum_fusion.5.left, bf16[128,4096]{1,0:T(8,128)(2,1)} %copy-done.1, bf16[64,4096]{1,0:T(8,128)(2,1)} %copy-done.4, bf16[64,4096]{1,0:T(8,128)(2,1)} %copy-done.5, ...), custom_call_target="tpu_custom_call" | custom-call | flops 1048576 | bytes 8388608 | tf_op jit(solution)/shard_map/pallas_call | solution.py:433
  130.4 2.4 %shard_map.193 = bf16[64,4096]{1,0:T(8,128)(2,1)} custom-call(s32[1]{0:T(128)} %bitcast.col, bf16[2,8,80,512]{3,2,1,0:T(8,128)(2,1)} %bitcast.49, bf16[2,8,80,512]{3,2,1,0:T(8,128)(2,1)} %bitcast.50, bf16[64,4096]{1,0:T(8,128)(2,1)} %convolution_convert_fusion.features, bf16[4,4096]{1,0:T(4,128)(2,1)} %constant_dynamic-slice_fusion.1.right), custom_call_target="tpu_custom_call" | custom-call | flops 1048576 | bytes 4194304 | tf_op jit(solution)/shard_map/pallas_call | solution.py:330
  (104 shorter events, 25.2 us)
Async XLA Ops:
  6.4 9.1 %copy-start.13 = (bf16[128,344]{0,1:T(8,128)(2,1)S(1)}, bf16[128,344]{0,1:T(8,128)(2,1)}, u32[]{:S(2)}) copy-start(bf16[128,344]{0,1:T(8,128)(2,1)} %param.22) | copy-start | bytes 264196
  6.4 35.9 %all-to-all-start = ((bf16[8,1184,128]{2,1,0:T(8,128)(2,1)}), bf16[8,1184,128]{2,1,0:T(8,128)(2,1)S(1)}, u32[]{:S(2)}, u32[]{:S(2)}) async-start(bf16[8,1184,128]{2,1,0:T(8,128)(2,1)} %shard_map.189), calls=%async_computation | async-start | bytes 4849664 | tf_op jit(solution)/shard_map/all_to_all | solution.py:46
  19.6 7.0 %copy-start.21 = (s32[128,16]{0,1:T(8,128)S(1)}, s32[128,16]{0,1:T(8,128)}, u32[]{:S(2)}) copy-start(s32[128,16]{0,1:T(8,128)} %param.14) | copy-start | bytes 24580
  19.6 32.6 %collective-permute-start.2 = (bf16[3008,128]{1,0:T(8,128)(2,1)}, bf16[3008,128]{1,0:T(8,128)(2,1)}, u32[]{:S(2)}, u32[]{:S(2)}) collective-permute-start(bf16[3008,128]{1,0:T(8,128)(2,1)} %get-tuple-element.94), channel_id=1, source_target_pairs={{0,64},{32,96},{64,0},{96,32},{1,65},{33,97},{65,1},{97,33},{2,66}... | collective-permute-start | bytes 2310152 | tf_op jit(solution)/shard_map/ppermute | solution.py:42
  23.2 34.1 %collective-permute-start.1 = (bf16[3008,128]{1,0:T(8,128)(2,1)}, bf16[3008,128]{1,0:T(8,128)(2,1)}, u32[]{:S(2)}, u32[]{:S(2)}) collective-permute-start(bf16[3008,128]{1,0:T(8,128)(2,1)} %get-tuple-element.93), channel_id=1, source_target_pairs={{0,96},{32,0},{64,32},{96,64},{1,97},{33,1},{65,33},{97,65},{2,98}... | collective-permute-start | bytes 2310152 | tf_op jit(solution)/shard_map/ppermute | solution.py:42
  23.7 34.5 %collective-permute-start = (bf16[3008,128]{1,0:T(8,128)(2,1)}, bf16[3008,128]{1,0:T(8,128)(2,1)}, u32[]{:S(2)}, u32[]{:S(2)}) collective-permute-start(bf16[3008,128]{1,0:T(8,128)(2,1)} %get-tuple-element.95), channel_id=1, source_target_pairs={{0,32},{32,64},{64,96},{96,0},{1,33},{33,65},{65,97},{97,1},{2,34}... | collective-permute-start | bytes 2310152 | tf_op jit(solution)/shard_map/ppermute | solution.py:42
  43.5 29.2 %all-to-all-start.1 = ((bf16[8,480,128]{2,1,0:T(8,128)(2,1)}), bf16[8,480,128]{2,1,0:T(8,128)(2,1)S(1)}, u32[]{:S(2)}, u32[]{:S(2)}) async-start(bf16[8,480,128]{2,1,0:T(8,128)(2,1)} %broadcast_in_dim.16), calls=%async_computation.1 | async-start | bytes 1966080 | tf_op jit(solution)/shard_map/all_to_all | solution.py:46
  47.2 11.7 %copy-start.20 = (bf16[128,128]{1,0:T(8,128)(2,1)S(1)}, bf16[128,128]{1,0:T(8,128)(2,1)}, u32[]{:S(2)}) copy-start(bf16[128,128]{1,0:T(8,128)(2,1)} %get-tuple-element.97) | copy-start | bytes 98308
  48.5 24.2 %collective-permute-start.3 = (bf16[2752,128]{1,0:T(8,128)(2,1)}, bf16[2752,128]{1,0:T(8,128)(2,1)S(1)}, u32[]{:S(2)}, u32[]{:S(2)}) collective-permute-start(bf16[2752,128]{1,0:T(8,128)(2,1)} %bitcast.18.w0), channel_id=1, source_target_pairs={{0,32},{32,64},{64,96},{96,0},{1,33},{33,65},{65,97},{97,1},{2,34}... | collective-permute-start | bytes 2113544 | tf_op jit(solution)/shard_map/ppermute | solution.py:42
  50.0 22.7 %collective-permute-start.4 = (bf16[2752,128]{1,0:T(8,128)(2,1)}, bf16[2752,128]{1,0:T(8,128)(2,1)S(1)}, u32[]{:S(2)}, u32[]{:S(2)}) collective-permute-start(bf16[2752,128]{1,0:T(8,128)(2,1)} %bitcast.18.w0), channel_id=1, source_target_pairs={{0,96},{32,0},{64,32},{96,64},{1,97},{33,1},{65,33},{97,65},{2,98}... | collective-permute-start | bytes 2113544 | tf_op jit(solution)/shard_map/ppermute | solution.py:42
  59.6 14.0 %copy-start.11 = (bf16[64,4096]{1,0:T(8,128)(2,1)S(1)}, bf16[64,4096]{1,0:T(8,128)(2,1)}, u32[]{:S(2)}) copy-start(bf16[64,4096]{1,0:T(8,128)(2,1)} %constant_dynamic-slice_fusion) | copy-start | bytes 1572868
  73.6 20.3 %collective-permute-start.5 = (bf16[64,4096]{1,0:T(8,128)(2,1)S(1)}, bf16[64,4096]{1,0:T(8,128)(2,1)S(1)}, u32[]{:S(2)}, u32[]{:S(2)}) collective-permute-start(bf16[64,4096]{1,0:T(8,128)(2,1)S(1)} %copy-done.11), channel_id=1, source_target_pairs={{0,32},{32,64},{64,96},{96,0},{1,33},{33,65},{65,97},{97,1},{2,34}... | collective-permute-start | bytes 1572872 | tf_op jit(solution)/shard_map/ppermute | solution.py:42
  74.5 19.4 %collective-permute-start.6 = (bf16[64,4096]{1,0:T(8,128)(2,1)S(1)}, bf16[64,4096]{1,0:T(8,128)(2,1)S(1)}, u32[]{:S(2)}, u32[]{:S(2)}) collective-permute-start(bf16[64,4096]{1,0:T(8,128)(2,1)S(1)} %copy-done.11), channel_id=1, source_target_pairs={{0,96},{32,0},{64,32},{96,64},{1,97},{33,1},{65,33},{97,65},{2,98}... | collective-permute-start | bytes 1572872 | tf_op jit(solution)/shard_map/ppermute | solution.py:42
  93.9 14.3 %copy-start.4 = (bf16[64,4096]{1,0:T(8,128)(2,1)}, bf16[64,4096]{1,0:T(8,128)(2,1)S(1)}, u32[]{:S(2)}) copy-start(bf16[64,4096]{1,0:T(8,128)(2,1)S(1)} %collective-permute-done.5.a) | copy-start | bytes 1572868
  93.9 15.0 %copy-start.5 = (bf16[64,4096]{1,0:T(8,128)(2,1)}, bf16[64,4096]{1,0:T(8,128)(2,1)S(1)}, u32[]{:S(2)}) copy-start(bf16[64,4096]{1,0:T(8,128)(2,1)S(1)} %collective-permute-done.6.b) | copy-start | bytes 1572868
  93.9 4.0 %collective-permute-start.7 = (bf16[2,528,512]{2,1,0:T(8,128)(2,1)}, bf16[2,528,512]{2,1,0:T(8,128)(2,1)S(1)}, u32[]{:S(2)}, u32[]{:S(2)}) collective-permute-start(bf16[2,528,512]{2,1,0:T(8,128)(2,1)} %get-tuple-element.52), channel_id=1, source_target_pairs={{0,8},{8,0},{1,9},{9,1},{2,10},{10,2},{3,11},{11,3},{4,12},{12,4},... | collective-permute-start | bytes 3244040 | tf_op jit(solution)/shard_map/ppermute | solution.py:42
  101.5 17.5 %copy-start.19 = (bf16[128,128]{1,0:T(8,128)(2,1)S(1)}, bf16[128,128]{1,0:T(8,128)(2,1)}, u32[]{:S(2)}) copy-start(bf16[128,128]{1,0:T(8,128)(2,1)} %get-tuple-element.96) | copy-start | bytes 98308
  101.5 27.8 %all-to-all-start.2 = ((bf16[16,80,512]{2,1,0:T(8,128)(2,1)}), bf16[16,80,512]{2,1,0:T(8,128)(2,1)S(1)}, u32[]{:S(2)}, u32[]{:S(2)}) async-start(bf16[16,80,512]{2,1,0:T(8,128)(2,1)} %shard_map.192), calls=%async_computation.2 | async-start | bytes 2621440 | tf_op jit(solution)/shard_map/all_to_all | solution.py:46
  108.2 11.5 %collective-permute-start.10 = (bf16[64,4096]{1,0:T(8,128)(2,1)S(1)}, bf16[64,4096]{1,0:T(8,128)(2,1)S(1)}, u32[]{:S(2)}, u32[]{:S(2)}) collective-permute-start(bf16[64,4096]{1,0:T(8,128)(2,1)S(1)} %collective-permute-done.5.a), channel_id=1, source_target_pairs={{0,8},{8,0},{1,9},{9,1},{2,10},{10,2},{3,11},{11,3},{4,12},{12,4},... | collective-permute-start | bytes 1572872 | tf_op jit(solution)/shard_map/ppermute | solution.py:42
  108.9 9.1 %collective-permute-start.8 = (bf16[32,4096]{1,0:T(8,128)(2,1)S(1)}, bf16[32,4096]{1,0:T(8,128)(2,1)S(1)}, u32[]{:S(2)}, u32[]{:S(2)}) collective-permute-start(bf16[32,4096]{1,0:T(8,128)(2,1)S(1)} %slice.58), channel_id=1, source_target_pairs={{0,32},{32,64},{64,96},{96,0},{1,33},{33,65},{65,97},{97,1},{2,34}... | collective-permute-start | bytes 786440 | tf_op jit(solution)/shard_map/ppermute | solution.py:42
  109.0 10.7 %collective-permute-start.11 = (bf16[64,4096]{1,0:T(8,128)(2,1)S(1)}, bf16[64,4096]{1,0:T(8,128)(2,1)S(1)}, u32[]{:S(2)}, u32[]{:S(2)}) collective-permute-start(bf16[64,4096]{1,0:T(8,128)(2,1)S(1)} %collective-permute-done.6.b), channel_id=1, source_target_pairs={{0,8},{8,0},{1,9},{9,1},{2,10},{10,2},{3,11},{11,3},{4,12},{12,4},... | collective-permute-start | bytes 1572872 | tf_op jit(solution)/shard_map/ppermute | solution.py:42
  109.1 9.7 %collective-permute-start.9 = (bf16[32,4096]{1,0:T(8,128)(2,1)S(1)}, bf16[32,4096]{1,0:T(8,128)(2,1)S(1)}, u32[]{:S(2)}, u32[]{:S(2)}) collective-permute-start(bf16[32,4096]{1,0:T(8,128)(2,1)S(1)} %slice.59), channel_id=1, source_target_pairs={{0,96},{32,0},{64,32},{96,64},{1,97},{33,1},{65,33},{97,65},{2,98}... | collective-permute-start | bytes 786440 | tf_op jit(solution)/shard_map/ppermute | solution.py:42
  118.0 2.0 %collective-permute-start.12 = (bf16[32,4096]{1,0:T(8,128)(2,1)S(1)}, bf16[32,4096]{1,0:T(8,128)(2,1)S(1)}, u32[]{:S(2)}, u32[]{:S(2)}) collective-permute-start(bf16[32,4096]{1,0:T(8,128)(2,1)S(1)} %collective-permute-done.8.c), channel_id=1, source_target_pairs={{0,8},{8,0},{1,9},{9,1},{2,10},{10,2},{3,11},{11,3},{4,12},{12,4},... | collective-permute-start | bytes 786440 | tf_op jit(solution)/shard_map/ppermute | solution.py:42
  118.9 1.5 %collective-permute-start.13 = (bf16[32,4096]{1,0:T(8,128)(2,1)S(1)}, bf16[32,4096]{1,0:T(8,128)(2,1)S(1)}, u32[]{:S(2)}, u32[]{:S(2)}) collective-permute-start(bf16[32,4096]{1,0:T(8,128)(2,1)S(1)} %collective-permute-done.9.d), channel_id=1, source_target_pairs={{0,8},{8,0},{1,9},{9,1},{2,10},{10,2},{3,11},{11,3},{4,12},{12,4},... | collective-permute-start | bytes 786440 | tf_op jit(solution)/shard_map/ppermute | solution.py:42
  (19 other events, 57.8 us)

commit v5 on v4

--- a/solution.py
+++ b/solution.py
@@ -17,6 +17,7 @@
 VMEM_LIMIT = 60 * 1024 * 1024
 CODES = 160
 CHUNK = 512
+PAIRS = 4
 TAIL = 16
 SHARE_ROWS = 352
 NT = (((1,), (1,)), ((), ()))
@@ -163,17 +164,13 @@
             high = min(low + 128, share)
             own[pl.ds(0, CODES), low:high] = own_share[pl.ds(tile * CODES, CODES), 0 : high - low]
 
-    first = CODES
-    second = CODES + slots
-    for start in (first, second):
-        rhs[pl.ds(start, slots), :] = right[...]
-        own[pl.ds(start, slots), :] = own_right[...]
-
+    rhs[pl.ds(CODES, slots), :] = right[...]
+    own[pl.ds(CODES, slots), :] = own_right[...]
     line = lax.broadcasted_iota(jnp.int32, (depth, rows), 0)
     slot = lax.broadcasted_iota(jnp.int32, (depth, rows), 1) // per_slot
     hot = jnp.where(line == codes[0], 1.0, 0.0)
     hot_b = hot[0:CODES].astype(BF)
-    pairs = 2
+    pairs = PAIRS
     per_part = slots // pairs
     start = share - (tiles - 1) * 128
     looked = []
@@ -185,9 +182,7 @@
     own_row = lax.broadcasted_iota(jnp.int32, (slots, rows), 0) == row_slot
     probe = jnp.where(own_row, jnp.concatenate(looked, axis=0), 0.0)
     probe = noise_scale * jnp.sum(probe, axis=0, keepdims=True)
-    high = probe.astype(BF).astype(F32)
-    lhs = jnp.where(line - first == slot, high, hot)
-    lhs = jnp.where(line - second == slot, probe - high, lhs)
+    lhs = jnp.where(line - CODES == slot, probe, hot)
     lhs = lhs.T.astype(BF)
 
     pre = jnp.dot(lhs, own[...], preferred_element_type=F32)
@@ -210,19 +205,19 @@
 
     product = jnp.dot(hid[...], weight[...], preferred_element_type=F32).astype(BF)
 
-    def store(out):
-        out[0, pl.ds(rows, TAIL), :] = tail.astype(BF)
+    def store(out, chunk):
+        at = slice(chunk * CHUNK, (chunk + 1) * CHUNK)
+        out[0, pl.ds(CHUNK, TAIL), :] = tail[:, at].astype(BF)
         for i, source in enumerate(slot_order(where[0])):
-            at = pl.multiple_of(source * width, width)
-            out[0, pl.ds(0, rows), pl.ds(at, width)] = product[:, i * width : (i + 1) * width]
-
-    @pl.when(step % 2 == where[1])
-    def _():
-        store(mine_out)
-
-    @pl.when(step % 2 != where[1])
-    def _():
-        store(other_out)
+            lanes = pl.ds(pl.multiple_of(source * width, width), width)
+            out[0, pl.ds(0, CHUNK), lanes] = product[at, i * width : (i + 1) * width]
+
+    for core in range(2):
+
+        @pl.when(where[1] == core)
+        def _():
+            store(mine_out, core)
+            store(other_out, 1 - core)
 
 
 def hidden_product(where, codes, shares, right, own_share, own_right, own_left, weights):
@@ -231,9 +226,9 @@
     share = own_right.shape[1]
     slots = right.shape[0] // steps
     width = 4 * weights[0].shape[1]
-    assert width == rows
-    out = jax.ShapeDtypeStruct((steps // 2, rows + TAIL, width), BF)
-    spec = pl.BlockSpec((1, rows + TAIL, width), lambda i, p: (i // 2, 0, 0))
+    assert width == CHUNK and rows == 2 * CHUNK
+    out = jax.ShapeDtypeStruct((steps, CHUNK + TAIL, width), BF)
+    spec = pl.BlockSpec((1, CHUNK + TAIL, width), lambda i, p: (i, 0, 0))
     return pl.pallas_call(
         hidden_kernel,
         grid_spec=pltpu.PrefetchScalarGridSpec(
@@ -553,7 +548,7 @@
     down_near = ring_first(down_own)
     mine, other = hidden_product(
         jnp.stack([pop_index, core]),
-        obs_ids.reshape(row_count // CHUNK, 1, CHUNK),
+        obs_ids.reshape(row_count // (2 * CHUNK), 1, 2 * CHUNK),
         shares,
         up_right,
         share,

time: 134 us -> 133 us (level)
  no operation moved by 1% of the time
where the time goes in v5:
time: 133 us; the launch traced here: 132 us
  Pallas kernels  38.6 us (29%)
  starting transfers between devices  34.7 us (26%)
  waiting for transfers between devices  29.3 us (22%)
  local copies, waits for them, and re-layouts  17.5 us (13%)
  other arithmetic  8.11 us (6%)
  between operations  2.37 us (2%)
    ppermute x14, waiting for transfers between devices, shifted(): lax.ppermute(value, axis, [(i, (i + step) % size) for i in range(size)])  22.1 us
    ppermute x14, starting transfers between devices, shifted(): lax.ppermute(value, axis, [(i, (i + step) % size) for i in range(size)])  18.2 us
    all_to_all x3, starting transfers between devices, exchange(): return lax.all_to_all(value, axis, split, 0, tiled=True)  16.4 us
    pallas_call x1, Pallas kernels, hidden_product(): pl.pallas_call(hidden_kernel, grid_spec=pltpu.PrefetchScalarGridSpec(num_...  16.1 us
    pallas_call x1, Pallas kernels, down_adam(): pl.pallas_call(down_kernel, grid_spec=pltpu.PrefetchScalarGridSpec(num_sc...  7.77 us
    all_to_all x3, waiting for transfers between devices, exchange(): return lax.all_to_all(value, axis, split, 0, tiled=True)  7.2 us
    unnamed x56, local copies, waits for them, and re-layouts  6.25 us
    pallas_call x1, Pallas kernels, table_products(): pl.pallas_call(table_kernel, grid_spec=pltpu.PrefetchScalarGridSpec(num_s...  5.17 us
  transfers between devices with their start and end apart: 17, of which 7 were waited for; matrix products, arithmetic and copies ran while one was open for 17% of the time, Pallas kernels for 22%

profile of v5, /device:TPU:1, one launch (start us, length us, event | category | flops | bytes accessed | tf_op | source)
XLA Modules:
  0.0 131.8 jit_solution(2264578799509969746)
XLA Ops:
  1.2 5.2 %shard_map.189 = bf16[8,1184,128]{2,1,0:T(8,128)(2,1)} custom-call(s32[2]{0:T(128)} %get-tuple-element.103.where, bf16[156,4096]{1,0:T(8,128)(2,1)} %table.1, bf16[8,344,512]{2,1,0:T(8,128)(2,1)} %bitcast.51, bf16[128,512]{1,0:T(8,128)(2,1)} %left.1, bf16[344,4096]{1,0:T(8,128)(2,1)} %rest_7_.1, bf16[344,4096]{1,0:T(8,128)(2,1)} %rest_7_.1, ...), custom_call_target="tpu_custom_call" | custom-call | flops 1048576 | bytes 1048576 | tf_op jit(solution)/shard_map/pallas_call | solution.py:110
  6.4 6.1 %all-to-all-start = ((bf16[8,1184,128]{2,1,0:T(8,128)(2,1)}), bf16[8,1184,128]{2,1,0:T(8,128)(2,1)S(1)}, u32[]{:S(2)}, u32[]{:S(2)}) async-start(bf16[8,1184,128]{2,1,0:T(8,128)(2,1)} %shard_map.189), calls=%async_computation | async-start | bytes 4849664 | tf_op jit(solution)/shard_map/all_to_all | solution.py:47
  17.6 2.0 %pad_maximum_fusion.3 = (bf16[3008,128]{1,0:T(8,128)(2,1)}, bf16[3008,128]{1,0:T(8,128)(2,1)}, bf16[3008,128]{1,0:T(8,128)(2,1)}, bf16[3008,128]{1,0:T(8,128)(2,1)}) fusion(bf16[256,128]{1,0:T(8,128)(2,1)S(1)} %get-tuple-element.98, bf16[2752,128]{1,0:T(8,128)(2,1)S(1)} %fusion, bf16[256,128]{1,0:T(8,128)(2,1)S(1)} %get-tuple-element.100, ...), kind=kLoop, calls=%fused_computation.7 | loop fusion | flops 5005312 | bytes 4046848 | tf_op jit(solution)/shard_map/concatenate | solution.py:514
  19.6 3.6 %collective-permute-start.2 = (bf16[3008,128]{1,0:T(8,128)(2,1)}, bf16[3008,128]{1,0:T(8,128)(2,1)}, u32[]{:S(2)}, u32[]{:S(2)}) collective-permute-start(bf16[3008,128]{1,0:T(8,128)(2,1)} %get-tuple-element.94), channel_id=1, source_target_pairs={{0,64},{32,96},{64,0},{96,32},{1,65},{33,97},{65,1},{97,33},{2,66}... | collective-permute-start | bytes 2310152 | tf_op jit(solution)/shard_map/ppermute | solution.py:43
  27.6 1.6 %constant_dynamic-slice_fusion.3.own_right = bf16[128,344]{1,0:T(8,128)(2,1)} fusion(bf16[128,2752]{1,0:T(8,128)(2,1)} %copy.42.right, s32[]{:T(128)S(6)} %select_n.46), kind=kLoop, calls=%fused_computation.27 | loop fusion | bytes 176132 | tf_op jit(solution)/shard_map/dynamic_slice | solution.py:516
  29.3 1.5 %constant_dynamic-slice_fusion.1.right = bf16[4,4096]{1,0:T(4,128)(2,1)} fusion(bf16[128,4096]{1,0:T(8,128)(2,1)} %param.23, s32[]{:T(128)S(6)} %select_n.47), kind=kLoop, calls=%fused_computation.25 | loop fusion | bytes 65540 | tf_op jit(solution)/shard_map/dynamic_slice | solution.py:525
  30.7 1.6 %multiply_convert_fusion.own = bf16[128,4096]{1,0:T(8,128)(2,1)S(1)} fusion(bf16[128,4096]{1,0:T(8,128)(2,1)} %param.23, f32[128]{0:T(128)S(1)} %divide_multiply_fusion), kind=kLoop, calls=%fused_computation.1 | loop fusion | flops 1572864 | bytes 2097664 | tf_op jit(solution)/shard_map/convert_element_type | solution.py:513
  35.1 7.2 %all-to-all-done = bf16[8,1184,128]{2,1,0:T(8,128)(2,1)S(1)} async-done(((bf16[8,1184,128]{2,1,0:T(8,128)(2,1)}), bf16[8,1184,128]{2,1,0:T(8,128)(2,1)S(1)}, u32[]{:S(2)}, u32[]{:S(2)}) %all-to-all-start) | async-done | bytes 2424864 | tf_op jit(solution)/shard_map/all_to_all | solution.py:47
  43.5 3.7 %all-to-all-start.1 = ((bf16[8,480,128]{2,1,0:T(8,128)(2,1)}), bf16[8,480,128]{2,1,0:T(8,128)(2,1)S(1)}, u32[]{:S(2)}, u32[]{:S(2)}) async-start(bf16[8,480,128]{2,1,0:T(8,128)(2,1)} %broadcast_in_dim.16), calls=%async_computation.1 | async-start | bytes 1966080 | tf_op jit(solution)/shard_map/all_to_all | solution.py:47
  48.5 1.5 %collective-permute-start.3 = (bf16[2752,128]{1,0:T(8,128)(2,1)}, bf16[2752,128]{1,0:T(8,128)(2,1)S(1)}, u32[]{:S(2)}, u32[]{:S(2)}) collective-permute-start(bf16[2752,128]{1,0:T(8,128)(2,1)} %bitcast.18.w0), channel_id=1, source_target_pairs={{0,32},{32,64},{64,96},{96,0},{1,33},{33,65},{65,97},{97,1},{2,34}... | collective-permute-start | bytes 2113544 | tf_op jit(solution)/shard_map/ppermute | solution.py:43
  50.0 2.2 %collective-permute-start.4 = (bf16[2752,128]{1,0:T(8,128)(2,1)}, bf16[2752,128]{1,0:T(8,128)(2,1)S(1)}, u32[]{:S(2)}, u32[]{:S(2)}) collective-permute-start(bf16[2752,128]{1,0:T(8,128)(2,1)} %bitcast.18.w0), channel_id=1, source_target_pairs={{0,96},{32,0},{64,32},{96,64},{1,97},{33,1},{65,33},{97,65},{2,98}... | collective-permute-start | bytes 2113544 | tf_op jit(solution)/shard_map/ppermute | solution.py:43
  53.0 4.4 %collective-permute-done.1.c = bf16[3008,128]{1,0:T(8,128)(2,1)} collective-permute-done((bf16[3008,128]{1,0:T(8,128)(2,1)}, bf16[3008,128]{1,0:T(8,128)(2,1)}, u32[]{:S(2)}, u32[]{:S(2)}) %collective-permute-start.1) | collective-permute-done | bytes 770080 | tf_op jit(solution)/shard_map/ppermute | solution.py:43
  59.6 4.6 %shard_map.190 = (f32[2752,128]{1,0:T(8,128)}, f32[2752,128]{1,0:T(8,128)}, f32[2752,128]{1,0:T(8,128)}) custom-call(bf16[512,128]{1,0:T(8,128)(2,1)} %pad_maximum_fusion.4.left, bf16[3008,128]{1,0:T(8,128)(2,1)} %get-tuple-element.92.a, bf16[3008,128]{1,0:T(8,128)(2,1)} %collective-permute-done.b, bf16[3008,128]{1,0:T(8,128)(2,1)} %collective-permute-done.1.c, ...), custom_call_target="tpu_custom_call" | custom-call | flops 1048576 | bytes 8388608 | tf_op jit(solution)/shard_map/pallas_call | solution.py:370
  64.2 8.5 %collective-permute-done.3.w1 = bf16[2752,128]{1,0:T(8,128)(2,1)S(1)} collective-permute-done((bf16[2752,128]{1,0:T(8,128)(2,1)}, bf16[2752,128]{1,0:T(8,128)(2,1)S(1)}, u32[]{:S(2)}, u32[]{:S(2)}) %collective-permute-start.3) | collective-permute-done | bytes 704544 | tf_op jit(solution)/shard_map/ppermute | solution.py:43
  74.5 2.1 %collective-permute-start.6 = (bf16[64,4096]{1,0:T(8,128)(2,1)S(1)}, bf16[64,4096]{1,0:T(8,128)(2,1)S(1)}, u32[]{:S(2)}, u32[]{:S(2)}) collective-permute-start(bf16[64,4096]{1,0:T(8,128)(2,1)S(1)} %copy-done.11), channel_id=1, source_target_pairs={{0,96},{32,0},{64,32},{96,64},{1,97},{33,1},{65,33},{97,65},{2,98}... | collective-permute-start | bytes 1572872 | tf_op jit(solution)/shard_map/ppermute | solution.py:43
  76.6 16.1 %shard_map.191 = (bf16[2,528,512]{2,1,0:T(8,128)(2,1)}, bf16[2,528,512]{2,1,0:T(8,128)(2,1)}) custom-call(s32[2]{0:T(128)} %get-tuple-element.102.where, s32[2,1,1024]{2,1,0:T(1,128)} %reshape.104.codes, bf16[8,480,128]{2,1,0:T(8,128)(2,1)} %copy-done.7, bf16[128,2752]{1,0:T(8,128)(2,1)} %copy.42.right, bf16[480,128]{1,0:T(8,128)(2,1)} %copy-done.12, ...), custom_call_target="tpu_custom_call" | custom-call | flops 8657043456 | bytes 8388608 | tf_op jit(solution)/shard_map/pallas_call | solution.py:232
  92.8 1.5 %collective-permute-start.7 = (bf16[2,528,512]{2,1,0:T(8,128)(2,1)}, bf16[2,528,512]{2,1,0:T(8,128)(2,1)S(1)}, u32[]{:S(2)}, u32[]{:S(2)}) collective-permute-start(bf16[2,528,512]{2,1,0:T(8,128)(2,1)} %get-tuple-element.52), channel_id=1, source_target_pairs={{0,8},{8,0},{1,9},{9,1},{2,10},{10,2},{3,11},{11,3},{4,12},{12,4},... | collective-permute-start | bytes 3244040 | tf_op jit(solution)/shard_map/ppermute | solution.py:43
  94.4 2.5 %collective-permute-done.7.theirs = bf16[2,528,512]{2,1,0:T(8,128)(2,1)S(1)} collective-permute-done((bf16[2,528,512]{2,1,0:T(8,128)(2,1)}, bf16[2,528,512]{2,1,0:T(8,128)(2,1)S(1)}, u32[]{:S(2)}, u32[]{:S(2)}) %collective-permute-start.7) | collective-permute-done | bytes 1081376 | tf_op jit(solution)/shard_map/ppermute | solution.py:43
  97.9 2.5 %shard_map.192 = bf16[16,80,512]{2,1,0:T(8,128)(2,1)} custom-call(bf16[2,528,512]{2,1,0:T(8,128)(2,1)} %get-tuple-element.51.mine, bf16[2,528,512]{2,1,0:T(8,128)(2,1)} %copy-done.6), custom_call_target="tpu_custom_call" | custom-call | flops 1048576 | bytes 4194304 | tf_op jit(solution)/shard_map/pallas_call | solution.py:279
  100.4 6.6 %all-to-all-start.2 = ((bf16[16,80,512]{2,1,0:T(8,128)(2,1)}), bf16[16,80,512]{2,1,0:T(8,128)(2,1)S(1)}, u32[]{:S(2)}, u32[]{:S(2)}) async-start(bf16[16,80,512]{2,1,0:T(8,128)(2,1)} %shard_map.192), calls=%async_computation.2 | async-start | bytes 2621440 | tf_op jit(solution)/shard_map/all_to_all | solution.py:47
  108.0 2.9 %collective-permute-start.9 = (bf16[32,4096]{1,0:T(8,128)(2,1)S(1)}, bf16[32,4096]{1,0:T(8,128)(2,1)S(1)}, u32[]{:S(2)}, u32[]{:S(2)}) collective-permute-start(bf16[32,4096]{1,0:T(8,128)(2,1)S(1)} %slice.59), channel_id=1, source_target_pairs={{0,96},{32,0},{64,32},{96,64},{1,97},{33,1},{65,33},{97,65},{2,98}... | collective-permute-start | bytes 786440 | tf_op jit(solution)/shard_map/ppermute | solution.py:43
  111.0 5.9 %collective-permute-done.8.c = bf16[32,4096]{1,0:T(8,128)(2,1)S(1)} collective-permute-done((bf16[32,4096]{1,0:T(8,128)(2,1)S(1)}, bf16[32,4096]{1,0:T(8,128)(2,1)S(1)}, u32[]{:S(2)}, u32[]{:S(2)}) %collective-permute-start.8) | collective-permute-done | bytes 262176 | tf_op jit(solution)/shard_map/ppermute | solution.py:43
  120.4 7.8 %shard_map.194 = (f32[2752,128]{1,0:T(8,128)}, f32[2752,128]{1,0:T(8,128)}, f32[2752,128]{1,0:T(8,128)}) custom-call(s32[1]{0:T(128)} %bitcast.2.core, bf16[512,128]{1,0:T(8,128)(2,1)} %pad_maximum_fusion.5.left, bf16[128,4096]{1,0:T(8,128)(2,1)} %copy-done.1, bf16[64,4096]{1,0:T(8,128)(2,1)} %copy-done.4, bf16[64,4096]{1,0:T(8,128)(2,1)} %copy-done.5, ...), custom_call_target="tpu_custom_call" | custom-call | flops 1048576 | bytes 8388608 | tf_op jit(solution)/shard_map/pallas_call | solution.py:428
  129.3 2.4 %shard_map.193 = bf16[64,4096]{1,0:T(8,128)(2,1)} custom-call(s32[1]{0:T(128)} %bitcast.col, bf16[2,8,80,512]{3,2,1,0:T(8,128)(2,1)} %bitcast.49, bf16[2,8,80,512]{3,2,1,0:T(8,128)(2,1)} %bitcast.50, bf16[64,4096]{1,0:T(8,128)(2,1)} %convolution_convert_fusion.features, bf16[4,4096]{1,0:T(4,128)(2,1)} %constant_dynamic-slice_fusion.1.right), custom_call_target="tpu_custom_call" | custom-call | flops 1048576 | bytes 4194304 | tf_op jit(solution)/shard_map/pallas_call | solution.py:325
  (104 shorter events, 25.2 us)
Async XLA Ops:
  6.4 9.1 %copy-start.13 = (bf16[128,344]{0,1:T(8,128)(2,1)S(1)}, bf16[128,344]{0,1:T(8,128)(2,1)}, u32[]{:S(2)}) copy-start(bf16[128,344]{0,1:T(8,128)(2,1)} %param.22) | copy-start | bytes 264196
  6.4 35.9 %all-to-all-start = ((bf16[8,1184,128]{2,1,0:T(8,128)(2,1)}), bf16[8,1184,128]{2,1,0:T(8,128)(2,1)S(1)}, u32[]{:S(2)}, u32[]{:S(2)}) async-start(bf16[8,1184,128]{2,1,0:T(8,128)(2,1)} %shard_map.189), calls=%async_computation | async-start | bytes 4849664 | tf_op jit(solution)/shard_map/all_to_all | solution.py:47
  19.6 7.0 %copy-start.21 = (s32[128,16]{0,1:T(8,128)S(1)}, s32[128,16]{0,1:T(8,128)}, u32[]{:S(2)}) copy-start(s32[128,16]{0,1:T(8,128)} %param.14) | copy-start | bytes 24580
  19.6 32.6 %collective-permute-start.2 = (bf16[3008,128]{1,0:T(8,128)(2,1)}, bf16[3008,128]{1,0:T(8,128)(2,1)}, u32[]{:S(2)}, u32[]{:S(2)}) collective-permute-start(bf16[3008,128]{1,0:T(8,128)(2,1)} %get-tuple-element.94), channel_id=1, source_target_pairs={{0,64},{32,96},{64,0},{96,32},{1,65},{33,97},{65,1},{97,33},{2,66}... | collective-permute-start | bytes 2310152 | tf_op jit(solution)/shard_map/ppermute | solution.py:43
  23.2 34.1 %collective-permute-start.1 = (bf16[3008,128]{1,0:T(8,128)(2,1)}, bf16[3008,128]{1,0:T(8,128)(2,1)}, u32[]{:S(2)}, u32[]{:S(2)}) collective-permute-start(bf16[3008,128]{1,0:T(8,128)(2,1)} %get-tuple-element.93), channel_id=1, source_target_pairs={{0,96},{32,0},{64,32},{96,64},{1,97},{33,1},{65,33},{97,65},{2,98}... | collective-permute-start | bytes 2310152 | tf_op jit(solution)/shard_map/ppermute | solution.py:43
  23.7 34.5 %collective-permute-start = (bf16[3008,128]{1,0:T(8,128)(2,1)}, bf16[3008,128]{1,0:T(8,128)(2,1)}, u32[]{:S(2)}, u32[]{:S(2)}) collective-permute-start(bf16[3008,128]{1,0:T(8,128)(2,1)} %get-tuple-element.95), channel_id=1, source_target_pairs={{0,32},{32,64},{64,96},{96,0},{1,33},{33,65},{65,97},{97,1},{2,34}... | collective-permute-start | bytes 2310152 | tf_op jit(solution)/shard_map/ppermute | solution.py:43
  43.5 29.2 %all-to-all-start.1 = ((bf16[8,480,128]{2,1,0:T(8,128)(2,1)}), bf16[8,480,128]{2,1,0:T(8,128)(2,1)S(1)}, u32[]{:S(2)}, u32[]{:S(2)}) async-start(bf16[8,480,128]{2,1,0:T(8,128)(2,1)} %broadcast_in_dim.16), calls=%async_computation.1 | async-start | bytes 1966080 | tf_op jit(solution)/shard_map/all_to_all | solution.py:47
  47.2 11.7 %copy-start.20 = (bf16[128,128]{1,0:T(8,128)(2,1)S(1)}, bf16[128,128]{1,0:T(8,128)(2,1)}, u32[]{:S(2)}) copy-start(bf16[128,128]{1,0:T(8,128)(2,1)} %get-tuple-element.97) | copy-start | bytes 98308
  48.5 24.2 %collective-permute-start.3 = (bf16[2752,128]{1,0:T(8,128)(2,1)}, bf16[2752,128]{1,0:T(8,128)(2,1)S(1)}, u32[]{:S(2)}, u32[]{:S(2)}) collective-permute-start(bf16[2752,128]{1,0:T(8,128)(2,1)} %bitcast.18.w0), channel_id=1, source_target_pairs={{0,32},{32,64},{64,96},{96,0},{1,33},{33,65},{65,97},{97,1},{2,34}... | collective-permute-start | bytes 2113544 | tf_op jit(solution)/shard_map/ppermute | solution.py:43
  50.0 22.7 %collective-permute-start.4 = (bf16[2752,128]{1,0:T(8,128)(2,1)}, bf16[2752,128]{1,0:T(8,128)(2,1)S(1)}, u32[]{:S(2)}, u32[]{:S(2)}) collective-permute-start(bf16[2752,128]{1,0:T(8,128)(2,1)} %bitcast.18.w0), channel_id=1, source_target_pairs={{0,96},{32,0},{64,32},{96,64},{1,97},{33,1},{65,33},{97,65},{2,98}... | collective-permute-start | bytes 2113544 | tf_op jit(solution)/shard_map/ppermute | solution.py:43
  59.6 14.0 %copy-start.11 = (bf16[64,4096]{1,0:T(8,128)(2,1)S(1)}, bf16[64,4096]{1,0:T(8,128)(2,1)}, u32[]{:S(2)}) copy-start(bf16[64,4096]{1,0:T(8,128)(2,1)} %constant_dynamic-slice_fusion) | copy-start | bytes 1572868
  73.6 19.2 %collective-permute-start.5 = (bf16[64,4096]{1,0:T(8,128)(2,1)S(1)}, bf16[64,4096]{1,0:T(8,128)(2,1)S(1)}, u32[]{:S(2)}, u32[]{:S(2)}) collective-permute-start(bf16[64,4096]{1,0:T(8,128)(2,1)S(1)} %copy-done.11), channel_id=1, source_target_pairs={{0,32},{32,64},{64,96},{96,0},{1,33},{33,65},{65,97},{97,1},{2,34}... | collective-permute-start | bytes 1572872 | tf_op jit(solution)/shard_map/ppermute | solution.py:43
  74.5 18.2 %collective-permute-start.6 = (bf16[64,4096]{1,0:T(8,128)(2,1)S(1)}, bf16[64,4096]{1,0:T(8,128)(2,1)S(1)}, u32[]{:S(2)}, u32[]{:S(2)}) collective-permute-start(bf16[64,4096]{1,0:T(8,128)(2,1)S(1)} %copy-done.11), channel_id=1, source_target_pairs={{0,96},{32,0},{64,32},{96,64},{1,97},{33,1},{65,33},{97,65},{2,98}... | collective-permute-start | bytes 1572872 | tf_op jit(solution)/shard_map/ppermute | solution.py:43
  92.8 14.3 %copy-start.4 = (bf16[64,4096]{1,0:T(8,128)(2,1)}, bf16[64,4096]{1,0:T(8,128)(2,1)S(1)}, u32[]{:S(2)}) copy-start(bf16[64,4096]{1,0:T(8,128)(2,1)S(1)} %collective-permute-done.5.a) | copy-start | bytes 1572868
  92.8 15.1 %copy-start.5 = (bf16[64,4096]{1,0:T(8,128)(2,1)}, bf16[64,4096]{1,0:T(8,128)(2,1)S(1)}, u32[]{:S(2)}) copy-start(bf16[64,4096]{1,0:T(8,128)(2,1)S(1)} %collective-permute-done.6.b) | copy-start | bytes 1572868
  92.8 4.1 %collective-permute-start.7 = (bf16[2,528,512]{2,1,0:T(8,128)(2,1)}, bf16[2,528,512]{2,1,0:T(8,128)(2,1)S(1)}, u32[]{:S(2)}, u32[]{:S(2)}) collective-permute-start(bf16[2,528,512]{2,1,0:T(8,128)(2,1)} %get-tuple-element.52), channel_id=1, source_target_pairs={{0,8},{8,0},{1,9},{9,1},{2,10},{10,2},{3,11},{11,3},{4,12},{12,4},... | collective-permute-start | bytes 3244040 | tf_op jit(solution)/shard_map/ppermute | solution.py:43
  100.4 17.5 %copy-start.19 = (bf16[128,128]{1,0:T(8,128)(2,1)S(1)}, bf16[128,128]{1,0:T(8,128)(2,1)}, u32[]{:S(2)}) copy-start(bf16[128,128]{1,0:T(8,128)(2,1)} %get-tuple-element.96) | copy-start | bytes 98308
  100.4 27.8 %all-to-all-start.2 = ((bf16[16,80,512]{2,1,0:T(8,128)(2,1)}), bf16[16,80,512]{2,1,0:T(8,128)(2,1)S(1)}, u32[]{:S(2)}, u32[]{:S(2)}) async-start(bf16[16,80,512]{2,1,0:T(8,128)(2,1)} %shard_map.192), calls=%async_computation.2 | async-start | bytes 2621440 | tf_op jit(solution)/shard_map/all_to_all | solution.py:47
  107.1 11.5 %collective-permute-start.10 = (bf16[64,4096]{1,0:T(8,128)(2,1)S(1)}, bf16[64,4096]{1,0:T(8,128)(2,1)S(1)}, u32[]{:S(2)}, u32[]{:S(2)}) collective-permute-start(bf16[64,4096]{1,0:T(8,128)(2,1)S(1)} %collective-permute-done.5.a), channel_id=1, source_target_pairs={{0,8},{8,0},{1,9},{9,1},{2,10},{10,2},{3,11},{11,3},{4,12},{12,4},... | collective-permute-start | bytes 1572872 | tf_op jit(solution)/shard_map/ppermute | solution.py:43
  107.8 9.1 %collective-permute-start.8 = (bf16[32,4096]{1,0:T(8,128)(2,1)S(1)}, bf16[32,4096]{1,0:T(8,128)(2,1)S(1)}, u32[]{:S(2)}, u32[]{:S(2)}) collective-permute-start(bf16[32,4096]{1,0:T(8,128)(2,1)S(1)} %slice.58), channel_id=1, source_target_pairs={{0,32},{32,64},{64,96},{96,0},{1,33},{33,65},{65,97},{97,1},{2,34}... | collective-permute-start | bytes 786440 | tf_op jit(solution)/shard_map/ppermute | solution.py:43
  107.9 10.7 %collective-permute-start.11 = (bf16[64,4096]{1,0:T(8,128)(2,1)S(1)}, bf16[64,4096]{1,0:T(8,128)(2,1)S(1)}, u32[]{:S(2)}, u32[]{:S(2)}) collective-permute-start(bf16[64,4096]{1,0:T(8,128)(2,1)S(1)} %collective-permute-done.6.b), channel_id=1, source_target_pairs={{0,8},{8,0},{1,9},{9,1},{2,10},{10,2},{3,11},{11,3},{4,12},{12,4},... | collective-permute-start | bytes 1572872 | tf_op jit(solution)/shard_map/ppermute | solution.py:43
  108.0 9.7 %collective-permute-start.9 = (bf16[32,4096]{1,0:T(8,128)(2,1)S(1)}, bf16[32,4096]{1,0:T(8,128)(2,1)S(1)}, u32[]{:S(2)}, u32[]{:S(2)}) collective-permute-start(bf16[32,4096]{1,0:T(8,128)(2,1)S(1)} %slice.59), channel_id=1, source_target_pairs={{0,96},{32,0},{64,32},{96,64},{1,97},{33,1},{65,33},{97,65},{2,98}... | collective-permute-start | bytes 786440 | tf_op jit(solution)/shard_map/ppermute | solution.py:43
  116.9 2.0 %collective-permute-start.12 = (bf16[32,4096]{1,0:T(8,128)(2,1)S(1)}, bf16[32,4096]{1,0:T(8,128)(2,1)S(1)}, u32[]{:S(2)}, u32[]{:S(2)}) collective-permute-start(bf16[32,4096]{1,0:T(8,128)(2,1)S(1)} %collective-permute-done.8.c), channel_id=1, source_target_pairs={{0,8},{8,0},{1,9},{9,1},{2,10},{10,2},{3,11},{11,3},{4,12},{12,4},... | collective-permute-start | bytes 786440 | tf_op jit(solution)/shard_map/ppermute | solution.py:43
  117.8 1.5 %collective-permute-start.13 = (bf16[32,4096]{1,0:T(8,128)(2,1)S(1)}, bf16[32,4096]{1,0:T(8,128)(2,1)S(1)}, u32[]{:S(2)}, u32[]{:S(2)}) collective-permute-start(bf16[32,4096]{1,0:T(8,128)(2,1)S(1)} %collective-permute-done.9.d), channel_id=1, source_target_pairs={{0,8},{8,0},{1,9},{9,1},{2,10},{10,2},{3,11},{11,3},{4,12},{12,4},... | collective-permute-start | bytes 786440 | tf_op jit(solution)/shard_map/ppermute | solution.py:43
  (19 other events, 57.8 us)

commit v6 on v5

--- a/solution.py
+++ b/solution.py
@@ -19,6 +19,7 @@
 CHUNK = 512
 PAIRS = 4
 TAIL = 16
+PIECE_TAIL = 8
 SHARE_ROWS = 352
 NT = (((1,), (1,)), ((), ()))
 TN = (((0,), (0,)), ((), ()))
@@ -260,16 +261,16 @@
 
 def pieces_kernel(mine, theirs, out):
     parts, piece, _ = out.shape
-    rows = piece - TAIL
+    rows = piece - PIECE_TAIL
     total = mine[0].astype(F32) + theirs[0].astype(F32)
     top = total.shape[0] - TAIL
     probe = total[top : top + 1, :] + total[top + 1 : top + 2, :]
     high = probe.astype(BF).astype(F32)
-    index = lax.broadcasted_iota(jnp.int32, (TAIL, total.shape[1]), 0)
+    index = lax.broadcasted_iota(jnp.int32, (PIECE_TAIL, total.shape[1]), 0)
     tail = jnp.where(index == 0, high, jnp.where(index == 1, probe - high, 0.0)).astype(BF)
     for part in range(parts):
         out[part, pl.ds(0, rows), :] = total[part * rows : (part + 1) * rows, :].astype(BF)
-        out[part, pl.ds(rows, TAIL), :] = tail
+        out[part, pl.ds(rows, PIECE_TAIL), :] = tail
 
 
 def pieces(mine, theirs, parts):
@@ -280,28 +281,27 @@
         pieces_kernel,
         grid=(count,),
         in_specs=[spec, spec],
-        out_specs=pl.BlockSpec((parts, rows + TAIL, width), lambda i: (i, 0, 0)),
-        out_shape=jax.ShapeDtypeStruct((count * parts, rows + TAIL, width), BF),
+        out_specs=pl.BlockSpec((parts, rows + PIECE_TAIL, width), lambda i: (i, 0, 0)),
+        out_shape=jax.ShapeDtypeStruct((count * parts, rows + PIECE_TAIL, width), BF),
         compiler_params=params(),
         cost_estimate=cost(1 << 20, 4 << 20),
     )(mine, theirs)
 
 
-def final_kernel(col, got, tails, features, right, out, own):
+def final_kernel(col, got, features, right, out):
     rows = out.shape[0]
-    halves, parts, _, width = got.shape
+    halves, parts, height, width = got.shape
     slots = right.shape[0]
     per_slot = rows // slots
-
-    @pl.when(pl.program_id(0) == 0)
-    def _():
-        probe = jnp.sum(tails[...].astype(F32), axis=(0, 1))
-        probe = jnp.sum(probe, axis=0, keepdims=True)
-        lane = lax.broadcasted_iota(jnp.int32, (rows, width), 1)
-        line = lax.broadcasted_iota(jnp.int32, (rows, width), 0)
-        mine = jnp.where(lane == line + col[0] * rows, probe, 0.0)
-        own[...] = noise_scale * jnp.sum(mine, axis=1, keepdims=True)
-
+    probe = jnp.zeros((1, width), F32)
+    for index in range(halves):
+        for part in range(parts):
+            tail = got[index, part, rows:height, :].astype(F32)
+            probe = probe + jnp.sum(tail, axis=0, keepdims=True)
+    lane = lax.broadcasted_iota(jnp.int32, (rows, width), 1)
+    line = lax.broadcasted_iota(jnp.int32, (rows, width), 0)
+    mine = jnp.where(lane == line + col[0] * rows, probe, 0.0)
+    own = noise_scale * jnp.sum(mine, axis=1, keepdims=True)
     for part in range(parts):
         cols = slice(part * width, (part + 1) * width)
         product = got[0, part, 0:rows, :].astype(F32)
@@ -315,33 +315,22 @@
             axis=0,
         )
         residual = features[:, cols].astype(F32)
-        out[:, cols] = (residual + product + own[...] * spread).astype(BF)
+        out[:, cols] = (residual + product + own * spread).astype(BF)
 
 
 def final_sum(col, got, features, right):
-    halves, parts, height, width = got.shape
-    rows = height - TAIL
-    some = 4
     return pl.pallas_call(
         final_kernel,
         grid_spec=pltpu.PrefetchScalarGridSpec(
             num_scalar_prefetch=1,
-            grid=(parts // some,),
-            in_specs=[
-                pl.BlockSpec((halves, some, height, width), lambda i, c: (0, i, 0, 0)),
-                pl.BlockSpec(
-                    (halves, parts, TAIL, width), lambda i, c: (0, 0, rows // TAIL, 0)
-                ),
-                pl.BlockSpec((rows, some * width), lambda i, c: (0, i)),
-                pl.BlockSpec((right.shape[0], some * width), lambda i, c: (0, i)),
-            ],
-            out_specs=pl.BlockSpec((rows, some * width), lambda i, c: (0, i)),
-            scratch_shapes=[pltpu.VMEM((rows, 1), F32)],
+            grid=(1,),
+            in_specs=[whole(got), whole(features), whole(right)],
+            out_specs=whole(features),
         ),
-        out_shape=jax.ShapeDtypeStruct((rows, parts * width), BF),
+        out_shape=jax.ShapeDtypeStruct(features.shape, BF),
         compiler_params=params(),
         cost_estimate=cost(1 << 20, 4 << 20),
-    )(col, got, got, features, right)
+    )(col, got, features, right)
 
 
 def slot_order(pop):

time: 133 us -> 132 us (level)
    unnamed x56 -> x54, local copies, waits for them, and re-layouts: 6.25 us -> 6.12 us
where the time goes in v6:
time: 132 us; the launch traced here: 131 us
  Pallas kernels  38.9 us (29%)
  starting transfers between devices  34 us (26%)
  waiting for transfers between devices  29.3 us (22%)
  local copies, waits for them, and re-layouts  17.4 us (13%)
  other arithmetic  8.2 us (6%)
  between operations  2.37 us (2%)
    ppermute x14, waiting for transfers between devices, shifted(): lax.ppermute(value, axis, [(i, (i + step) % size) for i in range(size)])  22.1 us
    ppermute x14, starting transfers between devices, shifted(): lax.ppermute(value, axis, [(i, (i + step) % size) for i in range(size)])  17.6 us
    all_to_all x3, starting transfers between devices, exchange(): return lax.all_to_all(value, axis, split, 0, tiled=True)  16.4 us
    pallas_call x1, Pallas kernels, hidden_product(): pl.pallas_call(hidden_kernel, grid_spec=pltpu.PrefetchScalarGridSpec(num_...  16.1 us
    pallas_call x1, Pallas kernels, down_adam(): pl.pallas_call(down_kernel, grid_spec=pltpu.PrefetchScalarGridSpec(num_sc...  7.78 us
    all_to_all x3, waiting for transfers between devices, exchange(): return lax.all_to_all(value, axis, split, 0, tiled=True)  7.22 us
    unnamed x54, local copies, waits for them, and re-layouts  6.12 us
    pallas_call x1, Pallas kernels, table_products(): pl.pallas_call(table_kernel, grid_spec=pltpu.PrefetchScalarGridSpec(num_s...  5.17 us
  transfers between devices with their start and end apart: 17, of which 7 were waited for; matrix products, arithmetic and copies ran while one was open for 17% of the time, Pallas kernels for 22%

profile of v6, /device:TPU:1, one launch (start us, length us, event | category | flops | bytes accessed | tf_op | source)
XLA Modules:
  0.0 131.3 jit_solution(9507447618619763142)
XLA Ops:
  1.3 5.2 %shard_map.189 = bf16[8,1184,128]{2,1,0:T(8,128)(2,1)} custom-call(s32[2]{0:T(128)} %get-tuple-element.103.where, bf16[156,4096]{1,0:T(8,128)(2,1)} %table.1, bf16[8,344,512]{2,1,0:T(8,128)(2,1)} %bitcast.50, bf16[128,512]{1,0:T(8,128)(2,1)} %left.1, bf16[344,4096]{1,0:T(8,128)(2,1)} %rest_7_.1, bf16[344,4096]{1,0:T(8,128)(2,1)} %rest_7_.1, ...), custom_call_target="tpu_custom_call" | custom-call | flops 1048576 | bytes 1048576 | tf_op jit(solution)/shard_map/pallas_call | solution.py:111
  6.5 6.1 %all-to-all-start = ((bf16[8,1184,128]{2,1,0:T(8,128)(2,1)}), bf16[8,1184,128]{2,1,0:T(8,128)(2,1)S(1)}, u32[]{:S(2)}, u32[]{:S(2)}) async-start(bf16[8,1184,128]{2,1,0:T(8,128)(2,1)} %shard_map.189), calls=%async_computation | async-start | bytes 4849664 | tf_op jit(solution)/shard_map/all_to_all | solution.py:48
  17.7 2.0 %pad_maximum_fusion.3 = (bf16[3008,128]{1,0:T(8,128)(2,1)}, bf16[3008,128]{1,0:T(8,128)(2,1)}, bf16[3008,128]{1,0:T(8,128)(2,1)}, bf16[3008,128]{1,0:T(8,128)(2,1)}) fusion(bf16[256,128]{1,0:T(8,128)(2,1)S(1)} %get-tuple-element.98, bf16[2752,128]{1,0:T(8,128)(2,1)S(1)} %fusion, bf16[256,128]{1,0:T(8,128)(2,1)S(1)} %get-tuple-element.100, ...), kind=kLoop, calls=%fused_computation.7 | loop fusion | flops 5005312 | bytes 4046848 | tf_op jit(solution)/shard_map/concatenate | solution.py:503
  19.7 3.6 %collective-permute-start.2 = (bf16[3008,128]{1,0:T(8,128)(2,1)}, bf16[3008,128]{1,0:T(8,128)(2,1)}, u32[]{:S(2)}, u32[]{:S(2)}) collective-permute-start(bf16[3008,128]{1,0:T(8,128)(2,1)} %get-tuple-element.94), channel_id=1, source_target_pairs={{0,64},{32,96},{64,0},{96,32},{1,65},{33,97},{65,1},{97,33},{2,66}... | collective-permute-start | bytes 2310152 | tf_op jit(solution)/shard_map/ppermute | solution.py:44
  27.7 1.6 %constant_dynamic-slice_fusion.3.own_right = bf16[128,344]{1,0:T(8,128)(2,1)} fusion(bf16[128,2752]{1,0:T(8,128)(2,1)} %copy.42.right, s32[]{:T(128)S(6)} %select_n.46), kind=kLoop, calls=%fused_computation.27 | loop fusion | bytes 176132 | tf_op jit(solution)/shard_map/dynamic_slice | solution.py:505
  29.4 1.5 %constant_dynamic-slice_fusion.1.right = bf16[4,4096]{1,0:T(4,128)(2,1)} fusion(bf16[128,4096]{1,0:T(8,128)(2,1)} %param.23, s32[]{:T(128)S(6)} %select_n.47), kind=kLoop, calls=%fused_computation.25 | loop fusion | bytes 65540 | tf_op jit(solution)/shard_map/dynamic_slice | solution.py:514
  30.8 1.6 %multiply_convert_fusion.own = bf16[128,4096]{1,0:T(8,128)(2,1)S(1)} fusion(bf16[128,4096]{1,0:T(8,128)(2,1)} %param.23, f32[128]{0:T(128)S(1)} %divide_multiply_fusion), kind=kLoop, calls=%fused_computation.1 | loop fusion | flops 1572864 | bytes 2097664 | tf_op jit(solution)/shard_map/convert_element_type | solution.py:502
  35.2 7.2 %all-to-all-done = bf16[8,1184,128]{2,1,0:T(8,128)(2,1)S(1)} async-done(((bf16[8,1184,128]{2,1,0:T(8,128)(2,1)}), bf16[8,1184,128]{2,1,0:T(8,128)(2,1)S(1)}, u32[]{:S(2)}, u32[]{:S(2)}) %all-to-all-start) | async-done | bytes 2424864 | tf_op jit(solution)/shard_map/all_to_all | solution.py:48
  43.6 3.7 %all-to-all-start.1 = ((bf16[8,480,128]{2,1,0:T(8,128)(2,1)}), bf16[8,480,128]{2,1,0:T(8,128)(2,1)S(1)}, u32[]{:S(2)}, u32[]{:S(2)}) async-start(bf16[8,480,128]{2,1,0:T(8,128)(2,1)} %broadcast_in_dim.16), calls=%async_computation.1 | async-start | bytes 1966080 | tf_op jit(solution)/shard_map/all_to_all | solution.py:48
  48.5 1.5 %collective-permute-start.3 = (bf16[2752,128]{1,0:T(8,128)(2,1)}, bf16[2752,128]{1,0:T(8,128)(2,1)S(1)}, u32[]{:S(2)}, u32[]{:S(2)}) collective-permute-start(bf16[2752,128]{1,0:T(8,128)(2,1)} %bitcast.18.w0), channel_id=1, source_target_pairs={{0,32},{32,64},{64,96},{96,0},{1,33},{33,65},{65,97},{97,1},{2,34}... | collective-permute-start | bytes 2113544 | tf_op jit(solution)/shard_map/ppermute | solution.py:44
  50.1 2.2 %collective-permute-start.4 = (bf16[2752,128]{1,0:T(8,128)(2,1)}, bf16[2752,128]{1,0:T(8,128)(2,1)}, u32[]{:S(2)}, u32[]{:S(2)}) collective-permute-start(bf16[2752,128]{1,0:T(8,128)(2,1)} %bitcast.18.w0), channel_id=1, source_target_pairs={{0,96},{32,0},{64,32},{96,64},{1,97},{33,1},{65,33},{97,65},{2,98}... | collective-permute-start | bytes 2113544 | tf_op jit(solution)/shard_map/ppermute | solution.py:44
  53.1 4.4 %collective-permute-done.1.c = bf16[3008,128]{1,0:T(8,128)(2,1)} collective-permute-done((bf16[3008,128]{1,0:T(8,128)(2,1)}, bf16[3008,128]{1,0:T(8,128)(2,1)}, u32[]{:S(2)}, u32[]{:S(2)}) %collective-permute-start.1) | collective-permute-done | bytes 770080 | tf_op jit(solution)/shard_map/ppermute | solution.py:44
  59.7 4.6 %shard_map.190 = (f32[2752,128]{1,0:T(8,128)}, f32[2752,128]{1,0:T(8,128)}, f32[2752,128]{1,0:T(8,128)}) custom-call(bf16[512,128]{1,0:T(8,128)(2,1)} %pad_maximum_fusion.4.left, bf16[3008,128]{1,0:T(8,128)(2,1)} %get-tuple-element.92.a, bf16[3008,128]{1,0:T(8,128)(2,1)} %collective-permute-done.b, bf16[3008,128]{1,0:T(8,128)(2,1)} %collective-permute-done.1.c, ...), custom_call_target="tpu_custom_call" | custom-call | flops 1048576 | bytes 8388608 | tf_op jit(solution)/shard_map/pallas_call | solution.py:359
  64.3 8.5 %collective-permute-done.3.w1 = bf16[2752,128]{1,0:T(8,128)(2,1)S(1)} collective-permute-done((bf16[2752,128]{1,0:T(8,128)(2,1)}, bf16[2752,128]{1,0:T(8,128)(2,1)S(1)}, u32[]{:S(2)}, u32[]{:S(2)}) %collective-permute-start.3) | collective-permute-done | bytes 704544 | tf_op jit(solution)/shard_map/ppermute | solution.py:44
  74.2 2.1 %collective-permute-start.6 = (bf16[64,4096]{1,0:T(8,128)(2,1)S(1)}, bf16[64,4096]{1,0:T(8,128)(2,1)S(1)}, u32[]{:S(2)}, u32[]{:S(2)}) collective-permute-start(bf16[64,4096]{1,0:T(8,128)(2,1)S(1)} %copy-done.11), channel_id=1, source_target_pairs={{0,96},{32,0},{64,32},{96,64},{1,97},{33,1},{65,33},{97,65},{2,98}... | collective-permute-start | bytes 1572872 | tf_op jit(solution)/shard_map/ppermute | solution.py:44
  76.3 16.1 %shard_map.191 = (bf16[2,528,512]{2,1,0:T(8,128)(2,1)}, bf16[2,528,512]{2,1,0:T(8,128)(2,1)}) custom-call(s32[2]{0:T(128)} %get-tuple-element.102.where, s32[2,1,1024]{2,1,0:T(1,128)} %reshape.104.codes, bf16[8,480,128]{2,1,0:T(8,128)(2,1)} %copy-done.7, bf16[128,2752]{1,0:T(8,128)(2,1)} %copy.42.right, bf16[480,128]{1,0:T(8,128)(2,1)} %copy-done.12, ...), custom_call_target="tpu_custom_call" | custom-call | flops 8657043456 | bytes 8388608 | tf_op jit(solution)/shard_map/pallas_call | solution.py:233
  92.5 1.3 collective-permute-start.7
  93.8 2.5 %collective-permute-done.7.theirs = bf16[2,528,512]{2,1,0:T(8,128)(2,1)S(1)} collective-permute-done((bf16[2,528,512]{2,1,0:T(8,128)(2,1)}, bf16[2,528,512]{2,1,0:T(8,128)(2,1)S(1)}, u32[]{:S(2)}, u32[]{:S(2)}) %collective-permute-start.7) | collective-permute-done | bytes 1081376 | tf_op jit(solution)/shard_map/ppermute | solution.py:44
  97.3 2.5 %shard_map.192 = bf16[16,72,512]{2,1,0:T(8,128)(2,1)} custom-call(bf16[2,528,512]{2,1,0:T(8,128)(2,1)} %get-tuple-element.51.mine, bf16[2,528,512]{2,1,0:T(8,128)(2,1)} %copy-done.6), custom_call_target="tpu_custom_call" | custom-call | flops 1048576 | bytes 4194304 | tf_op jit(solution)/shard_map/pallas_call | solution.py:280
  99.8 6.6 %all-to-all-start.2 = ((bf16[16,72,512]{2,1,0:T(8,128)(2,1)}), bf16[16,72,512]{2,1,0:T(8,128)(2,1)S(1)}, u32[]{:S(2)}, u32[]{:S(2)}) async-start(bf16[16,72,512]{2,1,0:T(8,128)(2,1)} %shard_map.192), calls=%async_computation.2 | async-start | bytes 2359296 | tf_op jit(solution)/shard_map/all_to_all | solution.py:48
  107.9 2.5 %collective-permute-start.9 = (bf16[32,4096]{1,0:T(8,128)(2,1)S(1)}, bf16[32,4096]{1,0:T(8,128)(2,1)S(1)}, u32[]{:S(2)}, u32[]{:S(2)}) collective-permute-start(bf16[32,4096]{1,0:T(8,128)(2,1)S(1)} %slice.59), channel_id=1, source_target_pairs={{0,96},{32,0},{64,32},{96,64},{1,97},{33,1},{65,33},{97,65},{2,98}... | collective-permute-start | bytes 786440 | tf_op jit(solution)/shard_map/ppermute | solution.py:44
  110.4 5.9 %collective-permute-done.8.c = bf16[32,4096]{1,0:T(8,128)(2,1)S(1)} collective-permute-done((bf16[32,4096]{1,0:T(8,128)(2,1)S(1)}, bf16[32,4096]{1,0:T(8,128)(2,1)S(1)}, u32[]{:S(2)}, u32[]{:S(2)}) %collective-permute-start.8) | collective-permute-done | bytes 262176 | tf_op jit(solution)/shard_map/ppermute | solution.py:44
  119.8 7.8 %shard_map.194 = (f32[2752,128]{1,0:T(8,128)}, f32[2752,128]{1,0:T(8,128)}, f32[2752,128]{1,0:T(8,128)}) custom-call(s32[1]{0:T(128)} %bitcast.2.core, bf16[512,128]{1,0:T(8,128)(2,1)} %pad_maximum_fusion.5.left, bf16[128,4096]{1,0:T(8,128)(2,1)} %copy-done, bf16[64,4096]{1,0:T(8,128)(2,1)} %copy-done.4, bf16[64,4096]{1,0:T(8,128)(2,1)} %copy-done.5, ...), custom_call_target="tpu_custom_call" | custom-call | flops 1048576 | bytes 8388608 | tf_op jit(solution)/shard_map/pallas_call | solution.py:417
  128.6 2.7 %shard_map.193 = bf16[64,4096]{1,0:T(8,128)(2,1)} custom-call(s32[1]{0:T(128)} %bitcast.col, bf16[2,8,72,512]{3,2,1,0:T(8,128)(2,1)} %bitcast.49, bf16[64,4096]{1,0:T(8,128)(2,1)} %convolution_convert_fusion.features, bf16[4,4096]{1,0:T(4,128)(2,1)} %constant_dynamic-slice_fusion.1.right), custom_call_target="tpu_custom_call" | custom-call | flops 1048576 | bytes 4194304 | tf_op jit(solution)/shard_map/pallas_call | solution.py:322
  (102 shorter events, 25.1 us)
Async XLA Ops:
  6.5 9.1 %copy-start.13 = (bf16[128,344]{0,1:T(8,128)(2,1)S(1)}, bf16[128,344]{0,1:T(8,128)(2,1)}, u32[]{:S(2)}) copy-start(bf16[128,344]{0,1:T(8,128)(2,1)} %param.22) | copy-start | bytes 264196
  6.5 35.9 %all-to-all-start = ((bf16[8,1184,128]{2,1,0:T(8,128)(2,1)}), bf16[8,1184,128]{2,1,0:T(8,128)(2,1)S(1)}, u32[]{:S(2)}, u32[]{:S(2)}) async-start(bf16[8,1184,128]{2,1,0:T(8,128)(2,1)} %shard_map.189), calls=%async_computation | async-start | bytes 4849664 | tf_op jit(solution)/shard_map/all_to_all | solution.py:48
  19.7 7.0 %copy-start.21 = (s32[128,16]{0,1:T(8,128)S(1)}, s32[128,16]{0,1:T(8,128)}, u32[]{:S(2)}) copy-start(s32[128,16]{0,1:T(8,128)} %param.14) | copy-start | bytes 24580
  19.7 32.6 %collective-permute-start.2 = (bf16[3008,128]{1,0:T(8,128)(2,1)}, bf16[3008,128]{1,0:T(8,128)(2,1)}, u32[]{:S(2)}, u32[]{:S(2)}) collective-permute-start(bf16[3008,128]{1,0:T(8,128)(2,1)} %get-tuple-element.94), channel_id=1, source_target_pairs={{0,64},{32,96},{64,0},{96,32},{1,65},{33,97},{65,1},{97,33},{2,66}... | collective-permute-start | bytes 2310152 | tf_op jit(solution)/shard_map/ppermute | solution.py:44
  23.3 34.1 %collective-permute-start.1 = (bf16[3008,128]{1,0:T(8,128)(2,1)}, bf16[3008,128]{1,0:T(8,128)(2,1)}, u32[]{:S(2)}, u32[]{:S(2)}) collective-permute-start(bf16[3008,128]{1,0:T(8,128)(2,1)} %get-tuple-element.93), channel_id=1, source_target_pairs={{0,96},{32,0},{64,32},{96,64},{1,97},{33,1},{65,33},{97,65},{2,98}... | collective-permute-start | bytes 2310152 | tf_op jit(solution)/shard_map/ppermute | solution.py:44
  23.7 34.5 %collective-permute-start = (bf16[3008,128]{1,0:T(8,128)(2,1)}, bf16[3008,128]{1,0:T(8,128)(2,1)}, u32[]{:S(2)}, u32[]{:S(2)}) collective-permute-start(bf16[3008,128]{1,0:T(8,128)(2,1)} %get-tuple-element.95), channel_id=1, source_target_pairs={{0,32},{32,64},{64,96},{96,0},{1,33},{33,65},{65,97},{97,1},{2,34}... | collective-permute-start | bytes 2310152 | tf_op jit(solution)/shard_map/ppermute | solution.py:44
  43.6 29.2 %all-to-all-start.1 = ((bf16[8,480,128]{2,1,0:T(8,128)(2,1)}), bf16[8,480,128]{2,1,0:T(8,128)(2,1)S(1)}, u32[]{:S(2)}, u32[]{:S(2)}) async-start(bf16[8,480,128]{2,1,0:T(8,128)(2,1)} %broadcast_in_dim.16), calls=%async_computation.1 | async-start | bytes 1966080 | tf_op jit(solution)/shard_map/all_to_all | solution.py:48
  47.3 11.7 %copy-start.20 = (bf16[128,128]{1,0:T(8,128)(2,1)S(1)}, bf16[128,128]{1,0:T(8,128)(2,1)}, u32[]{:S(2)}) copy-start(bf16[128,128]{1,0:T(8,128)(2,1)} %get-tuple-element.97) | copy-start | bytes 98308
  48.5 24.2 %collective-permute-start.3 = (bf16[2752,128]{1,0:T(8,128)(2,1)}, bf16[2752,128]{1,0:T(8,128)(2,1)S(1)}, u32[]{:S(2)}, u32[]{:S(2)}) collective-permute-start(bf16[2752,128]{1,0:T(8,128)(2,1)} %bitcast.18.w0), channel_id=1, source_target_pairs={{0,32},{32,64},{64,96},{96,0},{1,33},{33,65},{65,97},{97,1},{2,34}... | collective-permute-start | bytes 2113544 | tf_op jit(solution)/shard_map/ppermute | solution.py:44
  50.1 22.7 %collective-permute-start.4 = (bf16[2752,128]{1,0:T(8,128)(2,1)}, bf16[2752,128]{1,0:T(8,128)(2,1)}, u32[]{:S(2)}, u32[]{:S(2)}) collective-permute-start(bf16[2752,128]{1,0:T(8,128)(2,1)} %bitcast.18.w0), channel_id=1, source_target_pairs={{0,96},{32,0},{64,32},{96,64},{1,97},{33,1},{65,33},{97,65},{2,98}... | collective-permute-start | bytes 2113544 | tf_op jit(solution)/shard_map/ppermute | solution.py:44
  59.7 13.9 %copy-start.11 = (bf16[64,4096]{1,0:T(8,128)(2,1)S(1)}, bf16[64,4096]{1,0:T(8,128)(2,1)}, u32[]{:S(2)}) copy-start(bf16[64,4096]{1,0:T(8,128)(2,1)} %constant_dynamic-slice_fusion) | copy-start | bytes 1572868
  73.6 18.8 %collective-permute-start.5 = (bf16[64,4096]{1,0:T(8,128)(2,1)S(1)}, bf16[64,4096]{1,0:T(8,128)(2,1)S(1)}, u32[]{:S(2)}, u32[]{:S(2)}) collective-permute-start(bf16[64,4096]{1,0:T(8,128)(2,1)S(1)} %copy-done.11), channel_id=1, source_target_pairs={{0,32},{32,64},{64,96},{96,0},{1,33},{33,65},{65,97},{97,1},{2,34}... | collective-permute-start | bytes 1572872 | tf_op jit(solution)/shard_map/ppermute | solution.py:44
  74.2 18.3 %collective-permute-start.6 = (bf16[64,4096]{1,0:T(8,128)(2,1)S(1)}, bf16[64,4096]{1,0:T(8,128)(2,1)S(1)}, u32[]{:S(2)}, u32[]{:S(2)}) collective-permute-start(bf16[64,4096]{1,0:T(8,128)(2,1)S(1)} %copy-done.11), channel_id=1, source_target_pairs={{0,96},{32,0},{64,32},{96,64},{1,97},{33,1},{65,33},{97,65},{2,98}... | collective-permute-start | bytes 1572872 | tf_op jit(solution)/shard_map/ppermute | solution.py:44
  92.5 14.0 %copy-start.4 = (bf16[64,4096]{1,0:T(8,128)(2,1)}, bf16[64,4096]{1,0:T(8,128)(2,1)S(1)}, u32[]{:S(2)}) copy-start(bf16[64,4096]{1,0:T(8,128)(2,1)S(1)} %collective-permute-done.5.a) | copy-start | bytes 1572868
  92.5 15.0 %copy-start.5 = (bf16[64,4096]{1,0:T(8,128)(2,1)}, bf16[64,4096]{1,0:T(8,128)(2,1)S(1)}, u32[]{:S(2)}) copy-start(bf16[64,4096]{1,0:T(8,128)(2,1)S(1)} %collective-permute-done.6.b) | copy-start | bytes 1572868
  92.5 3.8 %collective-permute-start.7 = (bf16[2,528,512]{2,1,0:T(8,128)(2,1)}, bf16[2,528,512]{2,1,0:T(8,128)(2,1)S(1)}, u32[]{:S(2)}, u32[]{:S(2)}) collective-permute-start(bf16[2,528,512]{2,1,0:T(8,128)(2,1)} %get-tuple-element.52), channel_id=1, source_target_pairs={{0,8},{8,0},{1,9},{9,1},{2,10},{10,2},{3,11},{11,3},{4,12},{12,4},... | collective-permute-start | bytes 3244040 | tf_op jit(solution)/shard_map/ppermute | solution.py:44
  99.8 17.5 %copy-start.19 = (bf16[128,128]{1,0:T(8,128)(2,1)S(1)}, bf16[128,128]{1,0:T(8,128)(2,1)}, u32[]{:S(2)}) copy-start(bf16[128,128]{1,0:T(8,128)(2,1)} %get-tuple-element.96) | copy-start | bytes 98308
  99.8 27.8 %all-to-all-start.2 = ((bf16[16,72,512]{2,1,0:T(8,128)(2,1)}), bf16[16,72,512]{2,1,0:T(8,128)(2,1)S(1)}, u32[]{:S(2)}, u32[]{:S(2)}) async-start(bf16[16,72,512]{2,1,0:T(8,128)(2,1)} %shard_map.192), calls=%async_computation.2 | async-start | bytes 2359296 | tf_op jit(solution)/shard_map/all_to_all | solution.py:48
  106.5 11.5 %collective-permute-start.10 = (bf16[64,4096]{1,0:T(8,128)(2,1)S(1)}, bf16[64,4096]{1,0:T(8,128)(2,1)S(1)}, u32[]{:S(2)}, u32[]{:S(2)}) collective-permute-start(bf16[64,4096]{1,0:T(8,128)(2,1)S(1)} %collective-permute-done.5.a), channel_id=1, source_target_pairs={{0,8},{8,0},{1,9},{9,1},{2,10},{10,2},{3,11},{11,3},{4,12},{12,4},... | collective-permute-start | bytes 1572872 | tf_op jit(solution)/shard_map/ppermute | solution.py:44
  107.2 9.1 %collective-permute-start.8 = (bf16[32,4096]{1,0:T(8,128)(2,1)S(1)}, bf16[32,4096]{1,0:T(8,128)(2,1)S(1)}, u32[]{:S(2)}, u32[]{:S(2)}) collective-permute-start(bf16[32,4096]{1,0:T(8,128)(2,1)S(1)} %slice.58), channel_id=1, source_target_pairs={{0,32},{32,64},{64,96},{96,0},{1,33},{33,65},{65,97},{97,1},{2,34}... | collective-permute-start | bytes 786440 | tf_op jit(solution)/shard_map/ppermute | solution.py:44
  107.4 10.5 %collective-permute-start.11 = (bf16[64,4096]{1,0:T(8,128)(2,1)S(1)}, bf16[64,4096]{1,0:T(8,128)(2,1)S(1)}, u32[]{:S(2)}, u32[]{:S(2)}) collective-permute-start(bf16[64,4096]{1,0:T(8,128)(2,1)S(1)} %collective-permute-done.6.b), channel_id=1, source_target_pairs={{0,8},{8,0},{1,9},{9,1},{2,10},{10,2},{3,11},{11,3},{4,12},{12,4},... | collective-permute-start | bytes 1572872 | tf_op jit(solution)/shard_map/ppermute | solution.py:44
  107.9 9.3 %collective-permute-start.9 = (bf16[32,4096]{1,0:T(8,128)(2,1)S(1)}, bf16[32,4096]{1,0:T(8,128)(2,1)S(1)}, u32[]{:S(2)}, u32[]{:S(2)}) collective-permute-start(bf16[32,4096]{1,0:T(8,128)(2,1)S(1)} %slice.59), channel_id=1, source_target_pairs={{0,96},{32,0},{64,32},{96,64},{1,97},{33,1},{65,33},{97,65},{2,98}... | collective-permute-start | bytes 786440 | tf_op jit(solution)/shard_map/ppermute | solution.py:44
  116.3 2.0 %collective-permute-start.12 = (bf16[32,4096]{1,0:T(8,128)(2,1)S(1)}, bf16[32,4096]{1,0:T(8,128)(2,1)S(1)}, u32[]{:S(2)}, u32[]{:S(2)}) collective-permute-start(bf16[32,4096]{1,0:T(8,128)(2,1)S(1)} %collective-permute-done.8.c), channel_id=1, source_target_pairs={{0,8},{8,0},{1,9},{9,1},{2,10},{10,2},{3,11},{11,3},{4,12},{12,4},... | collective-permute-start | bytes 786440 | tf_op jit(solution)/shard_map/ppermute | solution.py:44
  117.2 1.5 %collective-permute-start.13 = (bf16[32,4096]{1,0:T(8,128)(2,1)S(1)}, bf16[32,4096]{1,0:T(8,128)(2,1)S(1)}, u32[]{:S(2)}, u32[]{:S(2)}) collective-permute-start(bf16[32,4096]{1,0:T(8,128)(2,1)S(1)} %collective-permute-done.9.d), channel_id=1, source_target_pairs={{0,8},{8,0},{1,9},{9,1},{2,10},{10,2},{3,11},{11,3},{4,12},{12,4},... | collective-permute-start | bytes 786440 | tf_op jit(solution)/shard_map/ppermute | solution.py:44
  (18 other events, 53.2 us)
